TPU v7x, 32 devices: a whole 2x2x4 slice. The times are simulated.
32 devices in a mesh: fsdp: 2 (over x), blk: 4 (over y, core), uly: 4 (over z).
Axes of the slice: x: 2, y: 2, z: 4, core: 2. Of those that a mesh axis runs over, the one named last changes fastest.
Arguments:
- tokens: bfloat16 [4096, 768], P(('fsdp', 'blk', 'uly')), may hold values from -6 to 6
- query_weight: bfloat16 [768, 768], P(('fsdp', 'blk'), 'uly'), may hold values from -0.4375 to 0.4375
- key_weight: bfloat16 [768, 768], P(('fsdp', 'blk'), 'uly'), may hold values from -0.21875 to 0.21875
- value_weight: bfloat16 [768, 768], P(('fsdp', 'blk'), 'uly'), may hold values from -0.21875 to 0.21875
- output_weight: bfloat16 [768, 768], P('uly', ('fsdp', 'blk')), may hold values from -0.875 to 0.875
- up_weight: bfloat16 [768, 3072], P(('fsdp', 'blk'), 'uly'), may hold values from -0.21875 to 0.21875
- down_weight: bfloat16 [3072, 768], P('uly', ('fsdp', 'blk')), may hold values from -0.15625 to 0.15625
- query_bias: bfloat16 [768], P(('fsdp', 'blk')), may hold values from -3 to 3
- value_bias: bfloat16 [768], P(('fsdp', 'blk')), may hold values from -3 to 3
- output_bias: bfloat16 [768], P(('fsdp', 'blk')), may hold values from -3 to 3
- up_bias: bfloat16 [3072], P(('fsdp', 'blk')), may hold values from -3 to 3
- down_bias: bfloat16 [768], P(('fsdp', 'blk')), may hold values from -3 to 3
- first_gain: bfloat16 [768], P(('fsdp', 'blk')), may hold values from 0.25 to 1.75
- first_shift: bfloat16 [768], P(('fsdp', 'blk')), may hold values from -3 to 3
- second_gain: bfloat16 [768], P(('fsdp', 'blk')), may hold values from 0.25 to 1.75
- second_shift: bfloat16 [768], P(('fsdp', 'blk')), may hold values from -3 to 3
- cotangent: bfloat16 [4096, 768], P(('fsdp', 'blk', 'uly')), may hold values from -6 to 6
Outputs:
- result: bfloat16 [4096, 768], P(('fsdp', 'blk', 'uly'))
- input_grad: bfloat16 [4096, 768], P(('fsdp', 'blk', 'uly'))
- query_weight_grad: float32 [768, 768], P(('fsdp', 'blk'), 'uly')
- key_weight_grad: float32 [768, 768], P(('fsdp', 'blk'), 'uly')
- value_weight_grad: float32 [768, 768], P(('fsdp', 'blk'), 'uly')
- output_weight_grad: float32 [768, 768], P('uly', ('fsdp', 'blk'))
- up_weight_grad: float32 [768, 3072], P(('fsdp', 'blk'), 'uly')
- down_weight_grad: float32 [3072, 768], P('uly', ('fsdp', 'blk'))
- query_bias_grad: float32 [768], P(('fsdp', 'blk', 'uly'))
- value_bias_grad: float32 [768], P(('fsdp', 'blk', 'uly'))
- output_bias_grad: float32 [768], P(('fsdp', 'blk', 'uly'))
- up_bias_grad: float32 [3072], P(('fsdp', 'blk', 'uly'))
- down_bias_grad: float32 [768], P(('fsdp', 'blk', 'uly'))
- first_gain_grad: float32 [768], P(('fsdp', 'blk', 'uly'))
- first_shift_grad: float32 [768], P(('fsdp', 'blk', 'uly'))
- second_gain_grad: float32 [768], P(('fsdp', 'blk', 'uly'))
- second_shift_grad: float32 [768], P(('fsdp', 'blk', 'uly'))
All inputs are finite; a program needn't handle non-finite values.
Results may differ from a plain program's by a relative error of at most 0.023.
Values may be sent and summed in bfloat16 or wider, within the bound.
No kernel may reach another device: no remote copies, remote signals or barrier semaphores. Data moves between devices by JAX's collectives and lax.ppermute only.
A program may use at most 128 MiB of HBM per device.

v0:
```python
import jax
import jax.numpy as jnp
from jax import lax
from jax.experimental import pallas as pl
from jax.experimental.pallas import tpu as pltpu
from jax.sharding import PartitionSpec as P

HEAD_DIM = 64
CUBE = ("fsdp", "blk")
VEC_ROWS = 16
VMEM_LIMIT = 56 * 1024 * 1024
KERNEL_COST = 30_000_000_000
BRIEF_COST = 1
NEAR_COST = 3_000_000_000

KEY_GROUP, KEY_HALF = (0, 0, 1), (0, 1, 0)
VALUE_GROUP, VALUE_HALF = (2, 2, 1), (0, 1, 1)


def dot_plain(left, right):
    return jnp.dot(left, right, preferred_element_type=jnp.float32)


def dot_rows(left, right):
    return lax.dot_general(
        left, right, (((0,), (0,)), ((), ())), preferred_element_type=jnp.float32
    )


def dot_cols(left, right):
    return lax.dot_general(
        left, right, (((1,), (1,)), ((), ())), preferred_element_type=jnp.float32
    )


def passed_along(array, by):
    peers = lax.axis_size("uly")
    return lax.ppermute(array, "uly", [(i, (i + by) % peers) for i in range(peers)])


def slots_of(array):
    return [array] + [passed_along(array, by) for by in range(1, lax.axis_size("uly"))]


def blk_swapped(array, flip):
    peers = lax.axis_size("blk")
    return lax.ppermute(array, "blk", [(i, i ^ flip) for i in range(peers)])


def cube_swapped(array, even, odd):
    peers = lax.axis_size(CUBE)
    pairs = [(i, i ^ (odd if i & 1 else even)) for i in range(peers)]
    return lax.ppermute(array, CUBE, pairs)


def cube_index():
    return lax.axis_index("fsdp") * lax.axis_size("blk") + lax.axis_index("blk")


def place_kernel(cuts, index_ref, own, first, second, other, *outs):
    me = index_ref[0]
    odd = me & 1
    near, far = jnp.where(odd == 1, 2, 4), jnp.where(odd == 1, 4, 2)
    pieces = [
        (own, 0),
        (first, near),
        (second.at[0], far),
        (second.at[1], 6),
        (other.at[0], 1),
        (other.at[1], far ^ 1),
        (other.at[2], near ^ 1),
        (other.at[3], 7),
    ]
    for piece, flip in pieces:
        for out, (row, rows, column, columns) in zip(outs, cuts):
            out[me ^ flip] = piece[row : row + rows, column : column + columns]


def paired():
    return lax.axis_size("fsdp") == 2 and lax.axis_size("blk") == 4


def after(array, *others):
    return lax.optimization_barrier((array,) + others)[0]


def cube_placed(cuts, pieces):
    index = cube_index().astype(jnp.int32).reshape(1)
    outs = [((8, rows, columns), pieces[0].dtype) for _, rows, _, columns in cuts]
    return on_core(lambda *refs: place_kernel(cuts, *refs), index, pieces, outs)


def cube_flips(me):
    odd = me & 1
    return jnp.where(odd == 1, 2, 4), jnp.where(odd == 1, 4, 2)


def grads_kernel(pairs, spread, index, *refs):
    ins, (sent, kept), (whole, extra) = refs[:-4], refs[-4:-2], refs[-2:]
    at = 0
    lefts = []
    for count, last, pad, column, columns in pairs:
        left, right = stacked_slots(ins[at : at + count], last), ins[at + count][...]
        at += count + 1
        if pad:
            right = jnp.concatenate([jnp.zeros((pad, right.shape[1]), right.dtype), right], axis=0).T
        term = dot_plain(left.T, right)
        if pad:
            whole[:, column : column + columns] += term
        else:
            whole[:, column : column + columns] = term
        lefts.append((left, right))
    rows = kept.shape[1]
    depth = whole.shape[0] // 8
    if spread:
        hidden_sum, seed_sum = ins[at][...], ins[at + 1][...]
        qkv_sum = jnp.sum(lefts[0][1].astype(jnp.float32), axis=0, keepdims=True)
        branch_sum = jnp.sum(lefts[1][0].astype(jnp.float32), axis=0, keepdims=True)
        wide = whole.shape[1]
        stacked = jnp.concatenate(
            [qkv_sum, hidden_sum, branch_sum, seed_sum, jnp.zeros((4, wide), jnp.float32)], axis=0
        )
        line = lax.broadcasted_iota(jnp.int32, stacked.shape, 0)
        for block in range(8):
            turned = stacked if block == 0 else pltpu.roll(stacked, wide - depth * block, 1)
            extra[block, 0:8] = jnp.where(line < 2, stacked, turned)
            extra[block, 8:16] = jnp.zeros((8, wide), jnp.float32)
    me = index[0]
    near, far = cube_flips(me)
    for slot, flip in enumerate((0, near, far, 6)):
        block = me ^ flip ^ 1
        sent[slot, 0:depth] = whole[pl.ds(pl.multiple_of(block * depth, 8), depth)].astype(sent.dtype)
        if spread:
            sent[slot, depth:rows] = extra[block].astype(sent.dtype)
    for slot, flip in enumerate((0, far, near, 6)):
        block = me ^ flip
        kept[slot, 0:depth] = whole[pl.ds(pl.multiple_of(block * depth, 8), depth)]
        if spread:
            kept[slot, depth:rows] = extra[block]


def grads_sent(pairs, columns, depth, sums):
    plan = [
        (len(left), last, pad, column, right.shape[0] + pad if pad else right.shape[1])
        for left, last, right, pad, column in pairs
    ]
    operands = [item for left, _, right, _, _ in pairs for item in [*left, right]]
    rows = depth + (VEC_ROWS if sums else 0)
    index = cube_index().astype(jnp.int32).reshape(1)
    return on_core(
        lambda *refs: grads_kernel(plan, bool(sums), *refs),
        index,
        operands + list(sums),
        [((4, rows, columns), jnp.bfloat16), ((4, rows, columns), jnp.float32)],
        [((8 * depth, columns), jnp.float32), ((8, VEC_ROWS, columns), jnp.float32)],
    )


def grads_scattered(pairs, columns, owners, sums):
    model = pairs[0][0][0].shape[1]
    depth = model // owners
    whole = jnp.zeros((model, columns), jnp.float32)

    pairs = [(stacked_slots(left, last), *rest) for left, last, *rest in pairs]
    for left, right, pad, column in pairs:
        if pad:
            column += pad
            right = right.T
        term = dot_rows(left, right)
        whole = whole.at[:, column : column + term.shape[1]].add(term)
    blocks = whole.reshape(owners, depth, columns)
    if sums:
        hidden_sum, seed_sum = sums
        branch_sum = jnp.sum(pairs[1][0].astype(jnp.float32), axis=0)
        extra = jnp.zeros((owners, VEC_ROWS, columns), jnp.float32)
        extra = extra.at[:, 0].set(jnp.sum(pairs[0][1].astype(jnp.float32), axis=0)[None])
        extra = extra.at[:, 1].set(hidden_sum)
        extra = extra.at[:, 2, :depth].set(branch_sum.reshape(owners, depth))
        extra = extra.at[:, 3, :depth].set(seed_sum.reshape(owners, depth))
        blocks = jnp.concatenate([blocks, extra], axis=1)
    return lax.psum_scatter(blocks, CUBE, scatter_dimension=0, tiled=False)


def half_padded(part, half):
    zero = jnp.zeros_like(part)
    return jnp.concatenate([part, zero] if half == 0 else [zero, part], axis=0)


def heads_across(array, halves):
    turned = array.T
    return [
        half_padded(turned[h * HEAD_DIM : (h + 1) * HEAD_DIM], halves[h])
        for h in range(len(halves))
    ]


def group_of(ref, group):
    return ref[:, group * 128 : (group + 1) * 128]


def slot_places(index, uly, slot_rows):
    return ((uly - index // slot_rows) & 3) * slot_rows + index % slot_rows


def causal(rows, uly):
    keys = lax.broadcasted_iota(jnp.int32, (rows, rows), 0)
    queries = lax.broadcasted_iota(jnp.int32, (rows, rows), 1)
    slot_rows = rows // 4
    return slot_places(keys, uly, slot_rows) <= slot_places(queries, uly, slot_rows)


def forward_block(query_t, kv_ref, top, total, mixed, allowed):
    turned = kv_ref[...].T
    for h in range(3):
        scores = dot_plain(group_of(kv_ref, KEY_GROUP[h]), query_t[h])
        if allowed is not None:
            scores = jnp.where(allowed, scores, -1e30)
        block_top = jnp.max(scores, axis=0, keepdims=True)
        low = VALUE_GROUP[h] * 128 + VALUE_HALF[h] * HEAD_DIM
        value_t = turned[low : low + HEAD_DIM]
        own = pl.ds(h * HEAD_DIM, HEAD_DIM)
        if allowed is not None:
            weights = jnp.exp(scores - block_top)
            top[h : h + 1] = block_top
            total[h : h + 1] = jnp.sum(weights, axis=0, keepdims=True)
            mixed[own] = dot_plain(value_t, weights.astype(jnp.bfloat16))
        else:
            old_top = top[h : h + 1]
            new_top = jnp.maximum(old_top, block_top)
            fade = jnp.exp(old_top - new_top)
            weights = jnp.exp(scores - new_top)
            top[h : h + 1] = new_top
            total[h : h + 1] = total[h : h + 1] * fade + jnp.sum(weights, axis=0, keepdims=True)
            mixed[own] = mixed[own] * fade + dot_plain(value_t, weights.astype(jnp.bfloat16))


def forward_near_kernel(place, query, kv_own, kv_core, top, total, mixed):
    blk, uly = place[0], place[1]
    query_t = heads_across(query[...], KEY_HALF)
    top[...] = jnp.zeros_like(top)
    total[...] = jnp.ones_like(total)
    forward_block(query_t, kv_own, top, total, mixed, causal(query.shape[0], uly))

    @pl.when((blk & 1) == 1)
    def _():
        forward_block(query_t, kv_core, top, total, mixed, None)


def forward_far_kernel(
    place, query, kv_y, kv_both, top_in, total_in, mixed_in, out, mixed, lse, top, total
):
    blk = place[0]
    top[...] = top_in[...]
    total[...] = total_in[...]
    mixed[...] = mixed_in[...]

    @pl.when((blk & 2) == 2)
    def _():
        query_t = heads_across(query[...], KEY_HALF)
        forward_block(query_t, kv_y, top, total, mixed, None)
        forward_block(query_t, kv_both, top, total, mixed, None)

    for h in range(3):
        own = pl.ds(h * HEAD_DIM, HEAD_DIM)
        mixed[own] = mixed[own] / total[h : h + 1]
    lse[...] = top[...] + jnp.log(total[...])
    out[...] = mixed[...].astype(jnp.bfloat16)


def backward_block(sides, kv_ref, dkv_ref, query_grad_t, allowed):
    query_t, grad_t, query_m, grad_m, delta, lse = sides
    turned = kv_ref[...].T
    columns = [None, None, None]

    def add(group, term):
        columns[group] = term if columns[group] is None else columns[group] + term

    for h in range(3):
        scores = dot_plain(group_of(kv_ref, KEY_GROUP[h]), query_t[h])
        probs = jnp.exp(scores - lse[h : h + 1])
        if allowed is not None:
            probs = jnp.where(allowed, probs, 0.0)
        prob_grad = dot_plain(group_of(kv_ref, VALUE_GROUP[h]), grad_t[h])
        score_grad = (probs * (prob_grad - delta[h])).astype(jnp.bfloat16)
        add(VALUE_GROUP[h], dot_plain(probs.astype(jnp.bfloat16), grad_m[h]))
        add(KEY_GROUP[h], dot_plain(score_grad, query_m[h]))
        low = KEY_GROUP[h] * 128 + KEY_HALF[h] * HEAD_DIM
        own = pl.ds(h * HEAD_DIM, HEAD_DIM)
        query_grad_t[own] += dot_plain(turned[low : low + HEAD_DIM], score_grad)
    for group in range(3):
        dkv_ref[:, group * 128 : (group + 1) * 128] = columns[group].astype(dkv_ref.dtype)


def backward_sides(query, grads, mixed, lse):
    query_t = heads_across(query[...], KEY_HALF)
    grad_all = jnp.concatenate([ref[...] for ref in grads], axis=1)
    grad_t = [
        half_padded(grad_all[h * HEAD_DIM : (h + 1) * HEAD_DIM], VALUE_HALF[h]) for h in range(3)
    ]
    product = grad_all.astype(jnp.float32) * mixed[...]
    delta = [
        jnp.sum(product[h * HEAD_DIM : (h + 1) * HEAD_DIM], axis=0, keepdims=True)
        for h in range(3)
    ]
    query_m = [item.T for item in query_t]
    grad_m = [item.T for item in grad_t]
    return query_t, grad_t, query_m, grad_m, delta, lse[...]


def backward_both_kernel(place, query, g0, g1, g2, g3, mixed, lse, kv_both, dkv_both, query_grad_t):
    query_grad_t[...] = jnp.zeros_like(query_grad_t)

    @pl.when((place[0] & 2) == 2)
    def _():
        sides = backward_sides(query, (g0, g1, g2, g3), mixed, lse)
        backward_block(sides, kv_both, dkv_both, query_grad_t, None)

    @pl.when((place[0] & 2) == 0)
    def _():
        dkv_both[...] = jnp.zeros_like(dkv_both)


def backward_y_kernel(
    place, query, g0, g1, g2, g3, mixed, lse, kv_y, dkv_core, grad_t_in, dkv_y, total, part
):
    total[...] = grad_t_in[...]

    @pl.when((place[0] & 2) == 2)
    def _():
        sides = backward_sides(query, (g0, g1, g2, g3), mixed, lse)
        backward_block(sides, kv_y, part, total, None)
        dkv_y[...] = (part[...] + dkv_core[...].astype(jnp.float32)).astype(dkv_y.dtype)

    @pl.when((place[0] & 2) == 0)
    def _():
        dkv_y[...] = jnp.zeros_like(dkv_y)


def backward_near_kernel(
    place,
    query,
    g0,
    g1,
    g2,
    g3,
    mixed,
    lse,
    kv_own,
    kv_core,
    grad_t_in,
    dkv_own,
    dkv_core,
    query_grad,
    total,
):
    blk, uly = place[0], place[1]
    total[...] = grad_t_in[...]
    sides = backward_sides(query, (g0, g1, g2, g3), mixed, lse)

    @pl.when((blk & 1) == 1)
    def _():
        backward_block(sides, kv_core, dkv_core, total, None)

    @pl.when((blk & 1) == 0)
    def _():
        dkv_core[...] = jnp.zeros_like(dkv_core)

    backward_block(sides, kv_own, dkv_own, total, causal(query.shape[0], uly))
    query_grad[...] = (total[...] * HEAD_DIM**-0.5).T.astype(jnp.bfloat16)


def on_core(kernel, place, operands, outs, scratch=(), cost=KERNEL_COST):
    vmem = pl.BlockSpec(memory_space=pltpu.VMEM)
    return pl.pallas_call(
        kernel,
        out_shape=[jax.ShapeDtypeStruct(shape, dtype) for shape, dtype in outs],
        in_specs=[pl.BlockSpec(memory_space=pltpu.SMEM)] + [vmem] * len(operands),
        out_specs=[vmem] * len(outs),
        scratch_shapes=[pltpu.VMEM(shape, dtype) for shape, dtype in scratch],
        compiler_params=pltpu.CompilerParams(vmem_limit_bytes=VMEM_LIMIT),
        cost_estimate=pl.CostEstimate(flops=cost, transcendentals=0, bytes_accessed=0),
    )(place, *operands)


def normalized(rows):
    centre = rows - jnp.mean(rows, axis=-1, keepdims=True)
    rstd = lax.rsqrt(jnp.mean(centre * centre, axis=-1, keepdims=True) + 1e-05)
    return centre * rstd, rstd


def norm_back(grad, xhat, rstd):
    return rstd * (
        grad
        - jnp.mean(grad, axis=-1, keepdims=True)
        - xhat * jnp.mean(grad * xhat, axis=-1, keepdims=True)
    )


def stacked_slots(refs, last=False):
    rows = refs[0].shape[0]
    return jnp.concatenate(
        [ref[ref.shape[0] - rows :] if last else ref[:rows] for ref in refs], axis=0
    )


def project_kernel(place, t0, t1, t2, t3, weight, named, bias, query, kv, xhat_low):
    rows = stacked_slots((t0, t1, t2, t3)).astype(jnp.float32)
    xhat, _ = normalized(rows)
    xhat_low[...] = xhat.astype(jnp.bfloat16)
    normed = (xhat * named[0:1] + named[1:2]).astype(jnp.bfloat16)
    qkv = dot_plain(normed, weight[...]) + bias[...]
    wide = kv.shape[1]
    kv[...] = qkv[:, :wide].astype(jnp.bfloat16)
    query[...] = qkv[:, wide:].astype(jnp.bfloat16) * jnp.asarray(HEAD_DIM**-0.5, jnp.bfloat16)


GELU_A, GELU_B = 0.7978845608028654, 0.044715


def middle_kernel(
    place,
    m0,
    m1,
    m2,
    m3,
    t0,
    t1,
    t2,
    t3,
    c0,
    c1,
    c2,
    c3,
    output_t,
    up,
    down_t,
    named,
    up_bias,
    middle_own,
    xhat_low,
    active_low,
    hidden_back_low,
    part_own,
    *parts,
):
    slot = t0.shape[0]
    mixed_t = jnp.concatenate(
        [m0[...]]
        + [
            jnp.concatenate([ref[:, (4 - by) * slot :], ref[:, : (4 - by) * slot]], axis=1)
            for by, ref in ((1, m1), (2, m2), (3, m3))
        ],
        axis=0,
    )
    branch = dot_plain(output_t[...], mixed_t).T
    middle = stacked_slots((t0, t1, t2, t3)).astype(jnp.float32) + (branch + named[0:1])
    middle_own[...] = middle[:slot]
    xhat, _ = normalized(middle)
    xhat_low[...] = xhat.astype(jnp.bfloat16)
    second = (xhat * named[1:2] + named[2:3]).astype(jnp.bfloat16)
    hidden = dot_plain(second, up[...]) + up_bias[...]
    active_grad = dot_plain(stacked_slots((c0, c1, c2, c3)), down_t[...])
    square = hidden * hidden
    bent = jnp.tanh(GELU_A * hidden * (1.0 + GELU_B * square))
    active_low[...] = (0.5 * hidden * (1.0 + bent)).astype(jnp.bfloat16)
    slope = 0.5 * (1.0 + bent) + (0.5 * GELU_A) * hidden * (1.0 - bent * bent) * (
        1.0 + (3.0 * GELU_B) * square
    )
    hidden_back = (active_grad * slope).astype(jnp.bfloat16)
    hidden_back_low[...] = hidden_back
    second_back = dot_cols(hidden_back, up[...])
    part_own[...] = second_back[:slot]
    for by in range(1, 4):
        parts[by - 1][...] = second_back[by * slot : (by + 1) * slot].astype(jnp.bfloat16)


def outside_kernel(
    place, active, down_t, hidden_back, c0, c1, c2, c3, hidden_sum, seed_sum, part_own, *parts
):
    slot = part_own.shape[0]
    outside = dot_cols(active[...], down_t[...])
    part_own[...] = outside[:slot]
    for by in range(1, 4):
        parts[by - 1][...] = outside[by * slot : (by + 1) * slot].astype(jnp.bfloat16)
    hidden_sum[...] = jnp.sum(hidden_back[...].astype(jnp.float32), axis=0, keepdims=True)
    seed = stacked_slots((c0, c1, c2, c3)).astype(jnp.float32)
    seed_sum[...] = jnp.sum(seed, axis=0, keepdims=True)


def branch_kernel(
    place,
    part_own,
    r1,
    r2,
    r3,
    middle,
    seed,
    gain,
    output_t,
    o1,
    o2,
    o3,
    middle_back,
    branch_back,
    s1,
    s2,
    s3,
    *mixed_back_t,
):
    second_back = part_own[...]
    for ref in (r1, r2, r3):
        second_back = second_back + ref[...].astype(jnp.float32)
    xhat, rstd = normalized(middle[...])
    grad = seed[...].astype(jnp.float32) + norm_back(second_back * gain[...], xhat, rstd)
    middle_back[...] = grad
    low = grad.astype(jnp.bfloat16)
    branch_back[...] = low
    slot = low.shape[0]
    for ref, outside in ((s1, o1), (s2, o2), (s3, o3)):
        ref[:slot] = outside[...]
        ref[slot:] = low
    turned = dot_plain(low, output_t[...]).T.astype(jnp.bfloat16)
    width = mixed_back_t[0].shape[0]
    for by in range(4):
        mixed_back_t[by][...] = turned[by * width : (by + 1) * width]


def gather_back_kernel(place, own, core, far, query, weight, dqkv, part_own, *parts):
    wide = own.shape[1]
    width = query.shape[1]
    total = own[...].astype(jnp.float32) + core[...].astype(jnp.float32)
    kv_grad = (total + far[...].astype(jnp.float32)).astype(jnp.bfloat16)
    dqkv[:, :wide] = kv_grad
    dqkv[:, wide : wide + width] = query[...]
    dqkv[:, wide + width :] = jnp.zeros((query.shape[0], width), jnp.bfloat16)
    normed_back = dot_cols(dqkv[:, : wide + width], weight[...])
    slot = part_own.shape[0]
    part_own[...] = normed_back[:slot]
    for by in range(1, 4):
        parts[by - 1][...] = normed_back[by * slot : (by + 1) * slot].astype(jnp.bfloat16)


def slots_returned(parts):
    return [passed_along(parts[by - 1], -by) for by in range(1, 4)]


def shards(
    tokens,
    query_weight,
    key_weight,
    value_weight,
    output_weight,
    up_weight,
    down_weight,
    query_bias,
    value_bias,
    output_bias,
    up_bias,
    down_bias,
    first_gain,
    first_shift,
    second_gain,
    second_shift,
    cotangent,
):
    bf16, f32 = jnp.bfloat16, jnp.float32
    uly, blk = lax.axis_index("uly"), lax.axis_index("blk")
    groups = lax.axis_size("uly")
    owners = lax.axis_size(CUBE)
    part = tokens.shape[0]
    rows = groups * part
    depth, width = query_weight.shape
    units = up_weight.shape[1]
    model = depth * owners
    place = jnp.stack([blk, uly]).astype(jnp.int32)

    qkv_own = jnp.concatenate(
        [key_weight, value_weight[:, 128:], value_weight[:, :128], query_weight], axis=1
    )
    vectors = [
        query_bias,
        value_bias,
        output_bias,
        down_bias,
        first_gain,
        first_shift,
        second_gain,
        second_shift,
    ]
    up_rows = up_bias.shape[0] // depth
    named = len(vectors) + up_rows
    wide = 3 * width
    vector_rows = jnp.concatenate(
        [vector.reshape(1, depth) for vector in vectors] + [up_bias.reshape(up_rows, depth)]
    )
    vector_rows = jnp.pad(vector_rows, ((0, VEC_ROWS - named), (0, wide - depth)))
    chunk = depth // groups
    output_own = output_weight.T
    output_rows = jnp.concatenate(
        [output_own[at * chunk : (at + 1) * chunk] for at in range(groups)], axis=1
    )
    spare = -(part + chunk) % 16
    token_sent = jnp.concatenate([tokens, jnp.pad(output_rows, ((0, spare), (0, 0)))], axis=0)
    token_slots = [tokens, passed_along(token_sent, 1), None, None]
    qkv_sent = jnp.concatenate([qkv_own, vector_rows], axis=0)
    qkv_cuts = [(0, depth, 0, wide), (depth, VEC_ROWS, 0, wide)]
    if paired():
        qkv_sent = after(qkv_sent, token_slots[1])
        token_later = after(token_sent, token_slots[1])
        token_slots[3] = passed_along(token_later, 3)
        token_slots[2] = passed_along(token_later, 2)
        qkv_first = after(cube_swapped(qkv_sent, 4, 2), token_slots[3])
        qkv_second = cube_swapped(jnp.stack([qkv_sent, qkv_first]), 2, 4)
        qkv_second = after(qkv_second, token_slots[2])
        qkv_other = cube_swapped(
            jnp.concatenate([qkv_sent[None], qkv_first[None], qkv_second]), 1, 1
        )
        qkv_whole, vector_whole = cube_placed(
            qkv_cuts, (qkv_sent, qkv_first, qkv_second, qkv_other)
        )
    else:
        token_slots = [tokens] + slots_of(token_sent)[1:]
        whole = lax.all_gather(qkv_sent, CUBE, axis=0, tiled=False)
        qkv_whole, vector_whole = whole[:, :depth], whole[:, depth:]
    qkv_whole = qkv_whole.reshape(model, wide)
    vector_whole = vector_whole[:, :named, :depth].astype(f32)
    up_bias_whole = vector_whole[:, len(vectors) :].reshape(-1)
    named = vector_whole.transpose(1, 0, 2).reshape(named, model)
    query_bias_own = lax.dynamic_slice_in_dim(named[0], uly * width, width)
    value_bias_own = lax.dynamic_slice_in_dim(named[1], uly * width, width)
    up_bias_own = lax.dynamic_slice_in_dim(up_bias_whole, uly * units, units)
    output_bias_all, down_bias_all = named[2], named[3]
    gain1, gain2, shift2 = named[4], named[6], named[7]

    qkv_bias = jnp.concatenate(
        [jnp.zeros((width,), f32), value_bias_own[128:], value_bias_own[:128], query_bias_own]
    )

    units_grad = 2 * units
    inner = groups * width
    rest_cuts = [
        (0, depth, 0, inner),
        (0, depth, inner, units),
        (0, depth, inner + units, units),
    ]
    cotangent_later = after(cotangent, *token_slots[1:])
    cotangent_slots = [cotangent] + [passed_along(cotangent_later, by) for by in range(1, groups)]
    output_slots = [output_own] + [
        jnp.concatenate(
            [item[part : part + chunk, at * width : (at + 1) * width] for at in range(groups)], axis=0
        )
        for item in token_slots[1:]
    ]
    rest_own = jnp.concatenate(output_slots + [up_weight, down_weight.T], axis=1)
    if paired():
        rest_own = after(rest_own, qkv_second)
        rest_first = cube_swapped(rest_own, 4, 2)

    query, kv_own, xhat1_low = on_core(
        project_kernel,
        place,
        token_slots + [after(qkv_whole, cotangent_slots[1]), named[4:6], qkv_bias[None]],
        [((rows, width), bf16), ((rows, 2 * width), bf16), ((rows, model), bf16)],
    )
    kv_y = blk_swapped(kv_own, 2)
    kv_core = blk_swapped(kv_own, 1)
    stats = ((8, rows), f32)
    turned = ((width, rows), f32)
    top, total, mixed_t = on_core(
        forward_near_kernel, place, (query, kv_own, kv_core), (stats, stats, turned)
    )
    kv_both = after(blk_swapped(after(kv_y, top), 1), *cotangent_slots[2:])
    if paired():
        rest_second = cube_swapped(after(jnp.stack([rest_own, rest_first]), kv_own), 2, 4)
        rest_second = after(rest_second, kv_both)
        rest_held = jnp.concatenate([rest_own[None], rest_first[None], rest_second])
        rest_other = cube_swapped(rest_held, 1, 1)
        kv_both = after(kv_both, rest_held)
    mixed_low, mixed_t, lse = on_core(
        forward_far_kernel,
        place,
        (query, kv_y, kv_both, top, total, mixed_t),
        (((width, rows), bf16), turned, stats),
        (stats, stats),
    )
    mixed_slots = slots_of(mixed_low)
    if paired():
        rest_other = after(rest_other, mixed_low)
        output_t, up_whole, down_t = cube_placed(
            rest_cuts, (rest_own, rest_first, rest_second, rest_other)
        )
    else:
        whole = lax.all_gather(rest_own, CUBE, axis=0, tiled=False)
        output_t, up_whole, down_t = [whole[:, :, c : c + n] for _, _, c, n in rest_cuts]
    output_t = output_t.reshape(model, inner)
    up_whole = up_whole.reshape(model, units)
    down_t = down_t.reshape(model, units)

    slab = ((part, model), f32)
    slabs = [((part, model), bf16)] * (groups - 1)
    wide_low = ((rows, model), bf16)
    units_low = ((rows, units), bf16)
    middle, xhat2_low, active, hidden_back, second_own, *second_parts = on_core(
        middle_kernel,
        place,
        mixed_slots
        + token_slots
        + cotangent_slots
        + [output_t, up_whole, down_t, jnp.stack([output_bias_all, gain2, shift2]), up_bias_own[None]],
        [slab, wide_low, units_low, units_low, slab] + slabs,
    )
    second_returned = slots_returned(second_parts)
    wide_pairs = [
        ([xhat2_low], False, hidden_back, 0, 0),
        (cotangent_slots, False, active, 0, units),
    ]
    if paired():
        wide_sent, wide_kept = grads_sent(wide_pairs, units_grad, depth, ())
        second_own = after(second_own, wide_sent)
    hidden_sum, seed_sum, outside_own, *outside_parts = on_core(
        outside_kernel,
        place,
        [active, down_t, hidden_back] + cotangent_slots,
        [((1, units), f32), ((1, model), f32), slab] + slabs,
    )
    second_own = after(second_own, outside_own)

    middle_back, branch_back, s1, s2, s3, *mixed_back_t = on_core(
        branch_kernel,
        place,
        [second_own] + second_returned + [middle, cotangent, gain2[None], output_t] + outside_parts,
        [slab, ((part, model), bf16)]
        + [((2 * part, model), bf16)] * 3
        + [((width, part), bf16)] * groups,
    )
    grad_slots = [mixed_back_t[0]] + [
        passed_along(mixed_back_t[by], -by) for by in range(groups - 1, 0, -1)
    ]
    if paired():
        wide_got = cube_swapped(after(wide_sent, mixed_back_t[0]), 1, 1)
    sides = [query] + grad_slots + [mixed_t, lse]
    pair = ((rows, 2 * width), bf16)
    dkv_both, query_grad_t = on_core(
        backward_both_kernel, place, sides + [kv_both], (pair, turned), cost=BRIEF_COST
    )
    shared = slots_returned([after(item, *grad_slots[1:]) for item in (s1, s2, s3)])
    branch_slots = [branch_back] + shared[::-1]
    if paired():
        wide_held = wide_kept + after(wide_got, dkv_both).astype(f32)
        wide_sent = wide_held[2:].astype(bf16)
        wide_got = cube_swapped(wide_sent, 4, 2)
    dkv_y, query_grad_t = on_core(
        backward_y_kernel,
        place,
        sides + [kv_y, blk_swapped(dkv_both, 1), query_grad_t],
        (pair, turned),
        [((rows, 2 * width), f32)],
        cost=BRIEF_COST,
    )
    dkv_from_y = blk_swapped(dkv_y, 2)
    if paired():
        wide_got = after(wide_got, dkv_y).astype(f32)
        wide_held = wide_held[:2] + wide_got
        wide_sent = wide_held[1].astype(bf16)
    dkv_own, dkv_core, query_grad = on_core(
        backward_near_kernel,
        place,
        sides + [kv_own, kv_core, query_grad_t],
        (pair, pair, ((rows, width), bf16)),
        (turned,),
        cost=NEAR_COST,
    )
    dkv_core = blk_swapped(dkv_core, 1)
    dqkv, normed_own, *normed_parts = on_core(
        gather_back_kernel,
        place,
        [dkv_own, dkv_core, dkv_from_y, query_grad, qkv_whole],
        [((rows, wide + width), bf16), slab] + slabs,
        cost=BRIEF_COST,
    )
    normed_returned = slots_returned(normed_parts)

    columns = wide + width
    near_pairs = [
        ([xhat1_low], False, dqkv, 0, 0),
        (branch_slots, True, mixed_low, wide - 512, 512),
    ]
    sums = (hidden_sum, seed_sum)
    if paired():
        near_sent, near_kept = grads_sent(near_pairs, columns, depth, sums)
        near_got = cube_swapped(near_sent, 1, 1).astype(f32)
        near_held = near_kept + near_got
        near_next = near_held[2:].astype(bf16)
        near_got = cube_swapped(near_next, 4, 2).astype(f32)
        near_held = near_held[:2] + near_got
        near_last = near_held[1].astype(bf16)
        near_got = cube_swapped(near_last, 2, 4).astype(f32)
        near_total = near_held[0] + near_got
        wide_got = cube_swapped(after(wide_sent, near_sent), 2, 4).astype(f32)
        wide_total = wide_held[0] + wide_got
    else:
        near_total = grads_scattered(near_pairs, columns, owners, sums)
        wide_total = grads_scattered(wide_pairs, units_grad, owners, ())
        near_last = near_total

    normed_back = normed_own
    for item in normed_returned:
        normed_back = normed_back + after(item, near_last).astype(f32)
    outside = outside_own
    for item in shared:
        outside = outside + after(item, near_last)[:part].astype(f32)
    xhat1, rstd1 = normalized(tokens.astype(f32))
    input_grad = (middle_back + norm_back(normed_back * gain1, xhat1, rstd1)).astype(bf16)
    result = (middle + (outside + down_bias_all)).astype(bf16)

    qkv_total = near_total[:depth, :wide]
    output_total = near_total[:depth, wide:].T
    qkv_sums, hidden_sums = near_total[depth, :wide], near_total[depth + 1, :units]
    branch_sums, seed_sums = near_total[depth + 2, :depth], near_total[depth + 3, :depth]
    up_total, down_total = wide_total[:, :units], wide_total[:, units:].T
    own_gain1, own_shift1 = first_gain.astype(f32), first_shift.astype(f32)
    own_gain2, own_shift2 = second_gain.astype(f32), second_shift.astype(f32)
    qkv_weight_grad = own_gain1[:, None] * qkv_total + own_shift1[:, None] * qkv_sums[None]
    up_weight_grad = own_gain2[:, None] * up_total + own_shift2[:, None] * hidden_sums[None]
    qkv_wide, up_wide = qkv_own.astype(f32), up_weight.astype(f32)
    terms = jnp.concatenate(
        [
            jnp.sum(qkv_wide * qkv_total, axis=1),
            jnp.sum(qkv_wide * qkv_sums[None], axis=1),
            jnp.sum(up_wide * up_total, axis=1),
            jnp.sum(up_wide * hidden_sums[None], axis=1),
            qkv_sums[2 * width :],
            qkv_sums[width + 64 : 2 * width],
            qkv_sums[width : width + 64],
            hidden_sums,
        ]
    )
    all_terms = jnp.stack(slots_of(terms))
    share = depth // groups
    added = jnp.sum(all_terms[:, : 4 * depth], axis=0).reshape(4, depth)
    added = lax.dynamic_slice_in_dim(added, uly * share, share, axis=1)
    rank = cube_index() * groups + uly

    def owned(start, length, count):
        at = rank * count
        source = (uly - at // length) % groups
        return lax.dynamic_slice(all_terms, (source, start + at % length), (1, count))[0]

    query_bias_grad = owned(4 * depth, width, share)
    value_bias_grad = owned(4 * depth + width, width, share)
    up_bias_grad = owned(4 * depth + 2 * width, units, up_bias.shape[0] // groups)
    output_bias_grad = lax.dynamic_slice_in_dim(branch_sums, uly * share, share)
    down_bias_grad = lax.dynamic_slice_in_dim(seed_sums, uly * share, share)
    value_weight_grad = jnp.concatenate(
        [qkv_weight_grad[:, width + 64 : 2 * width], qkv_weight_grad[:, width : width + 64]], axis=1
    )
    return (
        result,
        input_grad,
        qkv_weight_grad[:, 2 * width :],
        qkv_weight_grad[:, :width],
        value_weight_grad,
        output_total,
        up_weight_grad,
        down_total,
        query_bias_grad,
        value_bias_grad,
        output_bias_grad,
        up_bias_grad,
        down_bias_grad,
        added[0],
        added[1],
        added[2],
        added[3],
    )


def solution(mesh):
    rows = P(("fsdp", "blk", "uly"), None)
    tall, flat = P(("fsdp", "blk"), "uly"), P("uly", ("fsdp", "blk"))
    vector, vector_out = P(("fsdp", "blk")), P(("fsdp", "blk", "uly"))
    return jax.shard_map(
        shards,
        mesh=mesh,
        in_specs=(rows, tall, tall, tall, flat, tall, flat) + (vector,) * 9 + (rows,),
        out_specs=(rows, rows, tall, tall, tall, flat, tall, flat) + (vector_out,) * 9,
        check_vma=False,
    )
```

profile of v0, /device:TPU:0, one launch (start us, length us, event | category | flops | bytes accessed | tf_op | source)
XLA Modules:
  0.0 233.2 jit_solution(14290832811906071249)
XLA Ops:
  2.6 3.1 %collective-permute-start = (bf16[160,768]{1,0:T(8,128)(2,1)S(1)}, bf16[160,768]{1,0:T(8,128)(2,1)S(1)}, u32[]{:S(2)}, u32[]{:S(2)}) collective-permute-start(bf16[160,768]{1,0:T(8,128)(2,1)S(1)} %pad_maximum_fusion.4), channel_id=1, source_target_pairs={{0,1},{1,2},{2,3},{3,0},{4,5},{5,6},{6,7},{7,4},{8,9},{9,10},{10,1... | collective-permute-start | bytes 737288 | tf_op jit(solution)/shard_map/ppermute | solution.py:38
  8.0 5.7 %collective-permute-done.t1 = bf16[160,768]{1,0:T(8,128)(2,1)S(1)} collective-permute-done((bf16[160,768]{1,0:T(8,128)(2,1)S(1)}, bf16[160,768]{1,0:T(8,128)(2,1)S(1)}, u32[]{:S(2)}, u32[]{:S(2)}) %collective-permute-start) | collective-permute-done | bytes 245792 | tf_op jit(solution)/shard_map/ppermute | solution.py:38
  13.7 1.7 collective-permute-start.2
  17.2 1.6 collective-permute-start.3
  18.8 3.6 %collective-permute-done.3.refs_2_ = bf16[112,576]{1,0:T(8,128)(2,1)S(1)} collective-permute-done((bf16[112,576]{1,0:T(8,128)(2,1)S(1)}, bf16[112,576]{1,0:T(8,128)(2,1)S(1)}, u32[]{:S(2)}, u32[]{:S(2)}) %collective-permute-start.3) | collective-permute-done | bytes 129056 | tf_op jit(solution)/shard_map/ppermute | solution.py:53
  22.4 1.6 collective-permute-start.4
  24.7 6.5 %collective-permute-done.1.t2 = bf16[160,768]{1,0:T(8,128)(2,1)S(1)} collective-permute-done((bf16[160,768]{1,0:T(8,128)(2,1)S(1)}, bf16[160,768]{1,0:T(8,128)(2,1)S(1)}, u32[]{:S(2)}, u32[]{:S(2)}) %collective-permute-start.1) | collective-permute-done | bytes 245792 | tf_op jit(solution)/shard_map/ppermute | solution.py:38
  32.4 1.6 collective-permute-start.12
  34.1 2.4 %shard_map.296 = (bf16[8,96,576]{2,1,0:T(8,128)(2,1)}, bf16[8,16,576]{2,1,0:T(8,128)(2,1)}) custom-call(s32[1]{0:T(128)} %bitcast.3.refs_0_, bf16[112,576]{1,0:T(8,128)(2,1)} %copy-done.4, bf16[112,576]{1,0:T(8,128)(2,1)} %copy-done.8, bf16[2,112,576]{2,1,0:T(8,128)(2,1)} %copy-done.17, bf16[4,112,576]{2,1,0:T(8,128)(2,1)} %collective-permute-done.5.refs_4_), custom_call_target="tpu_custom_call" | custom-call | flops 30000001024 | tf_op jit(solution)/shard_map/pallas_call | solution.py:374
  38.0 1.6 collective-permute-done.6.c1.refs_4_
  41.2 3.9 %shard_map.297 = (bf16[512,192]{1,0:T(8,128)(2,1)}, bf16[512,384]{1,0:T(8,128)(2,1)}, bf16[512,768]{1,0:T(8,128)(2,1)}) custom-call(s32[2]{0:T(128)} %pad_add_fusion.place, bf16[128,768]{1,0:T(8,128)(2,1)} %t0.3, bf16[160,768]{1,0:T(8,128)(2,1)} %copy-done.37, bf16[160,768]{1,0:T(8,128)(2,1)} %copy-done.39, bf16[160,768]{1,0:T(8,128)(2,1)} %copy-done.38, ...), custom_call_target="tpu_custom_call" | custom-call | flops 30000001024 | tf_op jit(solution)/shard_map/pallas_call | solution.py:374
  46.1 1.5 collective-permute-start.7
  48.9 3.7 %shard_map.298 = (f32[8,512]{1,0:T(8,128)}, f32[8,512]{1,0:T(8,128)}, f32[192,512]{1,0:T(8,128)}) custom-call(s32[2]{0:T(128)} %pad_add_fusion.place, bf16[512,192]{1,0:T(8,128)(2,1)} %get-tuple-element.106.query, bf16[512,384]{1,0:T(8,128)(2,1)} %get-tuple-element.107.kv_own, bf16[512,384]{1,0:T(8,128)(2,1)} %copy-done.47), custom_call_target="tpu_custom_call" | custom-call | flops 30000001024 | tf_op jit(solution)/shard_map/pallas_call | solution.py:374
  52.6 4.2 %collective-permute-done.7.kv_y = bf16[512,384]{1,0:T(8,128)(2,1)S(1)} collective-permute-done((bf16[512,384]{1,0:T(8,128)(2,1)S(1)}, bf16[512,384]{1,0:T(8,128)(2,1)S(1)}, u32[]{:S(2)}, u32[]{:S(2)}) %collective-permute-start.7) | collective-permute-done | bytes 393248 | tf_op jit(solution)/shard_map/ppermute | solution.py:47
  56.9 2.2 collective-permute-start.10
  60.7 8.1 %collective-permute-done.10.c2.refs_5_ = bf16[128,768]{1,0:T(8,128)(2,1)} collective-permute-done((bf16[128,768]{1,0:T(8,128)(2,1)S(1)}, bf16[128,768]{1,0:T(8,128)(2,1)}, u32[]{:S(2)}, u32[]{:S(2)}) %collective-permute-start.10) | collective-permute-done | bytes 196640 | tf_op jit(solution)/shard_map/ppermute | solution.py:38
  71.2 2.2 shard_map.299
  73.4 3.3 %collective-permute-start.14 = (bf16[192,512]{1,0:T(8,128)(2,1)}, bf16[192,512]{1,0:T(8,128)(2,1)S(1)}, u32[]{:S(2)}, u32[]{:S(2)}) collective-permute-start(bf16[192,512]{1,0:T(8,128)(2,1)} %get-tuple-element.117.m0.refs_7_), channel_id=1, source_target_pairs={{0,1},{1,2},{2,3},{3,0},{4,5},{5,6},{6,7},{7,4},{8,9},{9,10},{10,1... | collective-permute-start | bytes 589832 | tf_op jit(solution)/shard_map/ppermute | solution.py:38
  76.7 2.5 %collective-permute-start.15 = (bf16[192,512]{1,0:T(8,128)(2,1)}, bf16[192,512]{1,0:T(8,128)(2,1)S(1)}, u32[]{:S(2)}, u32[]{:S(2)}) collective-permute-start(bf16[192,512]{1,0:T(8,128)(2,1)} %get-tuple-element.117.m0.refs_7_), channel_id=1, source_target_pairs={{0,2},{1,3},{2,0},{3,1},{4,6},{5,7},{6,4},{7,5},{8,10},{9,11},{10,... | collective-permute-start | bytes 589832 | tf_op jit(solution)/shard_map/ppermute | solution.py:38
  80.6 4.1 %shard_map.300 = (bf16[8,96,768]{2,1,0:T(8,128)(2,1)}, bf16[8,96,768]{2,1,0:T(8,128)(2,1)}, bf16[8,96,768]{2,1,0:T(8,128)(2,1)}) custom-call(s32[1]{0:T(128)} %bitcast.3.refs_0_, bf16[96,2304]{1,0:T(8,128)(2,1)} %copy-done.1, bf16[96,2304]{1,0:T(8,128)(2,1)} %copy-done.3, bf16[2,96,2304]{2,1,0:T(8,128)(2,1)} %copy-done.5, bf16[4,96,2304]{2,1,0:T(8,128)(2,1)} %copy-done.44), custom_call_target="tpu_custom_call" | custom-call | flops 30000001024 | tf_op jit(solution)/shard_map/pallas_call | solution.py:374
  84.8 8.2 %collective-permute-done.15.m2 = bf16[192,512]{1,0:T(8,128)(2,1)S(1)} collective-permute-done((bf16[192,512]{1,0:T(8,128)(2,1)}, bf16[192,512]{1,0:T(8,128)(2,1)S(1)}, u32[]{:S(2)}, u32[]{:S(2)}) %collective-permute-start.15) | collective-permute-done | bytes 196640 | tf_op jit(solution)/shard_map/ppermute | solution.py:38
  93.8 7.5 %shard_map.301 = (f32[128,768]{1,0:T(8,128)}, bf16[512,768]{1,0:T(8,128)(2,1)}, bf16[512,768]{1,0:T(8,128)(2,1)}, bf16[512,768]{1,0:T(8,128)(2,1)}, f32[128,768]...) custom-call(s32[2]{0:T(128)} %pad_add_fusion.place, ...), custom_call_target="tpu_custom_call" | custom-call | flops 30000001024 | tf_op jit(solution)/shard_map/pallas_call | solution.py:374
  101.3 4.5 %collective-permute-start.18 = (bf16[128,768]{1,0:T(8,128)(2,1)}, bf16[128,768]{1,0:T(8,128)(2,1)S(1)}, u32[]{:S(2)}, u32[]{:S(2)}) collective-permute-start(bf16[128,768]{1,0:T(8,128)(2,1)} %get-tuple-element.131), channel_id=1, source_target_pairs={{0,3},{1,0},{2,1},{3,2},{4,7},{5,4},{6,5},{7,6},{8,11},{9,8},{10,9... | collective-permute-start | bytes 589832 | tf_op jit(solution)/shard_map/ppermute | solution.py:38
  105.7 1.7 collective-permute-start.19
  107.4 3.7 %shard_map.302 = (f32[1,768]{1,0:T(1,128)}, f32[1,768]{1,0:T(1,128)}, f32[128,768]{1,0:T(8,128)}, bf16[128,768]{1,0:T(8,128)(2,1)}, bf16[128,768]{1,0:T(8,128)(2,1)}, /*index=5*/bf16[128,768]{1,0:T(8,128)(2,1)}) custom-call(s32[2]{0:T(128)} %pad_add_fusion.place, bf16[512,768]{1,0:T(8,128)(2,1)} %get-tuple-element.123.active.refs_7_, ...), custom_call_target="tpu_custom_call" | custom-call | flops 30000001024 | tf_op jit(solution)/shard_map/pallas_call | solution.py:374
  111.0 5.2 %shard_map.303 = (bf16[4,96,1536]{2,1,0:T(8,128)(2,1)}, f32[4,96,1536]{2,1,0:T(8,128)}) custom-call(s32[1]{0:T(128)} %bitcast.3.refs_0_, bf16[512,768]{1,0:T(8,128)(2,1)} %get-tuple-element.127.refs_1_, bf16[512,768]{1,0:T(8,128)(2,1)} %get-tuple-element.124.hidden_back.refs_2_, bf16[128,768]{1,0:T(8,128)(2,1)} %seed.1, bf16[128,768]{1,0:T(8,128)(2,1)} %copy-done.54, ...), custom_call_target="tpu_custom_call" | custom-call | flops 30000001024 | tf_op jit(solution)/shard_map/pallas_call | solution.py:374
  116.2 8.8 %collective-permute-done.19.r2 = bf16[128,768]{1,0:T(8,128)(2,1)S(1)} collective-permute-done((bf16[128,768]{1,0:T(8,128)(2,1)}, bf16[128,768]{1,0:T(8,128)(2,1)S(1)}, u32[]{:S(2)}, u32[]{:S(2)}) %collective-permute-start.19) | collective-permute-done | bytes 196640 | tf_op jit(solution)/shard_map/ppermute | solution.py:38
  125.8 3.7 %shard_map.304 = (f32[128,768]{1,0:T(8,128)}, bf16[128,768]{1,0:T(8,128)(2,1)}, bf16[256,768]{1,0:T(8,128)(2,1)}, bf16[256,768]{1,0:T(8,128)(2,1)}, bf16[256,768...) custom-call(s32[2]{0:T(128)} %pad_add_fusion.place, ...), custom_call_target="tpu_custom_call" | custom-call | flops 30000001024 | tf_op jit(solution)/shard_map/pallas_call | solution.py:374
  130.4 3.0 %collective-permute-start.23 = (bf16[192,128]{1,0:T(8,128)(2,1)}, bf16[192,128]{1,0:T(8,128)(2,1)S(1)}, u32[]{:S(2)}, u32[]{:S(2)}) collective-permute-start(bf16[192,128]{1,0:T(8,128)(2,1)} %get-tuple-element.140), channel_id=1, source_target_pairs={{0,3},{1,0},{2,1},{3,2},{4,7},{5,4},{6,5},{7,6},{8,11},{9,8},{10,9... | collective-permute-start | bytes 147464 | tf_op jit(solution)/shard_map/ppermute | solution.py:38
  133.4 2.4 %collective-permute-done.21.g1 = bf16[192,128]{1,0:T(8,128)(2,1)S(1)} collective-permute-done((bf16[192,128]{1,0:T(8,128)(2,1)}, bf16[192,128]{1,0:T(8,128)(2,1)S(1)}, u32[]{:S(2)}, u32[]{:S(2)}) %collective-permute-start.21) | collective-permute-done | bytes 49184 | tf_op jit(solution)/shard_map/ppermute | solution.py:38
  136.9 2.2 shard_map.305
  139.2 2.0 collective-permute-start.28
  141.9 2.5 %shard_map.306 = (bf16[512,384]{1,0:T(8,128)(2,1)}, f32[192,512]{1,0:T(8,128)}) custom-call(s32[2]{0:T(128)} %pad_add_fusion.place, bf16[512,192]{1,0:T(8,128)(2,1)} %get-tuple-element.106.query, bf16[192,128]{1,0:T(8,128)(2,1)} %get-tuple-element.143.g0, bf16[192,128]{1,0:T(8,128)(2,1)} %copy-done.24, bf16[192,128]{1,0:T(8,128)(2,1)} %copy-done.25, ...), custom_call_target="tpu_custom_call" | custom-call | flops 1 | tf_op jit(solution)/shard_map/pallas_call | solution.py:374
  144.5 5.2 %shard_map.307 = (bf16[512,384]{1,0:T(8,128)(2,1)}, bf16[512,384]{1,0:T(8,128)(2,1)}, bf16[512,192]{1,0:T(8,128)(2,1)}) custom-call(s32[2]{0:T(128)} %pad_add_fusion.place, bf16[512,192]{1,0:T(8,128)(2,1)} %get-tuple-element.106.query, bf16[192,128]{1,0:T(8,128)(2,1)} %get-tuple-element.143.g0, bf16[192,128]{1,0:T(8,128)(2,1)} %copy-done.24, ...), custom_call_target="tpu_custom_call" | custom-call | flops 3000000000 | tf_op jit(solution)/shard_map/pallas_call | solution.py:374
  149.6 2.5 %collective-permute-start.26 = (bf16[512,384]{1,0:T(8,128)(2,1)}, bf16[512,384]{1,0:T(8,128)(2,1)S(1)}, u32[]{:S(2)}, u32[]{:S(2)}) collective-permute-start(bf16[512,384]{1,0:T(8,128)(2,1)} %get-tuple-element.150), channel_id=1, source_target_pairs={{0,4},{4,0},{8,12},{12,8},{1,5},{5,1},{9,13},{13,9},{2,6},{6,2},{1... | collective-permute-start | bytes 1179656 | tf_op jit(solution)/shard_map/ppermute | solution.py:47
  152.2 9.0 %collective-permute-start.27 = (bf16[512,384]{1,0:T(8,128)(2,1)S(1)}, bf16[512,384]{1,0:T(8,128)(2,1)S(1)}, u32[]{:S(2)}, u32[]{:S(2)}) collective-permute-start(bf16[512,384]{1,0:T(8,128)(2,1)S(1)} %copy-done.50), channel_id=1, source_target_pairs={{0,8},{4,12},{8,0},{12,4},{1,9},{5,13},{9,1},{13,5},{2,10},{6,14},... | collective-permute-start | bytes 1179656 | tf_op jit(solution)/shard_map/ppermute | solution.py:47
  161.1 1.8 collective-permute-start.29
  162.9 2.4 %collective-permute-start.24 = (bf16[256,768]{1,0:T(8,128)(2,1)S(1)}, bf16[256,768]{1,0:T(8,128)(2,1)S(1)}, u32[]{:S(2)}, u32[]{:S(2)}) collective-permute-start(bf16[256,768]{1,0:T(8,128)(2,1)S(1)} %copy-done.48), channel_id=1, source_target_pairs={{0,3},{1,0},{2,1},{3,2},{4,7},{5,4},{6,5},{7,6},{8,11},{9,8},{10,9... | collective-permute-start | bytes 1179656 | tf_op jit(solution)/shard_map/ppermute | solution.py:38
  165.6 4.9 %collective-permute-done.27.far = bf16[512,384]{1,0:T(8,128)(2,1)S(1)} collective-permute-done((bf16[512,384]{1,0:T(8,128)(2,1)S(1)}, bf16[512,384]{1,0:T(8,128)(2,1)S(1)}, u32[]{:S(2)}, u32[]{:S(2)}) %collective-permute-start.27) | collective-permute-done | bytes 393248 | tf_op jit(solution)/shard_map/ppermute | solution.py:47
  171.3 3.6 %shard_map.308 = (bf16[512,768]{1,0:T(8,128)(2,1)}, f32[128,768]{1,0:T(8,128)}, bf16[128,768]{1,0:T(8,128)(2,1)}, bf16[128,768]{1,0:T(8,128)(2,1)}, bf16[128,768]{1,0:T(8,128)(2,1)}) custom-call(s32[2]{0:T(128)} %pad_add_fusion.place, bf16[512,384]{1,0:T(8,128)(2,1)} %get-tuple-element.149.own, bf16[512,384]{1,0:T(8,128)(2,1)} %copy-done.15, ...), custom_call_target="tpu_custom_call" | custom-call | flops 1 | tf_op jit(solution)/shard_map/pallas_call | solution.py:374
  174.9 7.6 %collective-permute-done.29.refs_5_ = bf16[256,768]{1,0:T(8,128)(2,1)S(1)} collective-permute-done((bf16[256,768]{1,0:T(8,128)(2,1)S(1)}, bf16[256,768]{1,0:T(8,128)(2,1)S(1)}, u32[]{:S(2)}, u32[]{:S(2)}) %collective-permute-start.29) | collective-permute-done | bytes 393248 | tf_op jit(solution)/shard_map/ppermute | solution.py:38
  183.4 4.4 %shard_map.309 = (bf16[4,112,768]{2,1,0:T(8,128)(2,1)}, f32[4,112,768]{2,1,0:T(8,128)}) custom-call(s32[1]{0:T(128)} %bitcast.3.refs_0_, bf16[512,768]{1,0:T(8,128)(2,1)} %get-tuple-element.142.refs_1_, bf16[512,768]{1,0:T(8,128)(2,1)} %get-tuple-element.153.refs_2_, bf16[128,768]{1,0:T(8,128)(2,1)} %get-tuple-element.154.refs_3_, ...), custom_call_target="tpu_custom_call" | custom-call | flops 30000001024 | tf_op jit(solution)/shard_map/pallas_call | solution.py:374
  191.2 7.7 %collective-permute-start.34 = (bf16[128,768]{1,0:T(8,128)(2,1)}, bf16[128,768]{1,0:T(8,128)(2,1)S(1)}, u32[]{:S(2)}, u32[]{:S(2)}) collective-permute-start(bf16[128,768]{1,0:T(8,128)(2,1)} %get-tuple-element.172), channel_id=1, source_target_pairs={{0,1},{1,2},{2,3},{3,0},{4,5},{5,6},{6,7},{7,4},{8,9},{9,10},{10,1... | collective-permute-start | bytes 589832 | tf_op jit(solution)/shard_map/ppermute | solution.py:38
  198.9 2.8 %collective-permute-start.33 = (bf16[128,768]{1,0:T(8,128)(2,1)}, bf16[128,768]{1,0:T(8,128)(2,1)S(1)}, u32[]{:S(2)}, u32[]{:S(2)}) collective-permute-start(bf16[128,768]{1,0:T(8,128)(2,1)} %get-tuple-element.170), channel_id=1, source_target_pairs={{0,2},{1,3},{2,0},{3,1},{4,6},{5,7},{6,4},{7,5},{8,10},{9,11},{10,... | collective-permute-start | bytes 589832 | tf_op jit(solution)/shard_map/ppermute | solution.py:38
  205.5 8.5 %collective-permute-done.31 = bf16[2,112,768]{2,1,0:T(8,128)(2,1)S(1)} collective-permute-done((bf16[2,112,768]{2,1,0:T(8,128)(2,1)S(1)}, bf16[2,112,768]{2,1,0:T(8,128)(2,1)S(1)}, u32[]{:S(2)}, u32[]{:S(2)}) %collective-permute-start.31) | collective-permute-done | bytes 344096 | tf_op jit(solution)/shard_map/ppermute | solution.py:53
  217.1 2.4 %collective-permute-done.35 = bf16[112,768]{1,0:T(8,128)(2,1)S(1)} collective-permute-done((bf16[112,768]{1,0:T(8,128)(2,1)S(1)}, bf16[112,768]{1,0:T(8,128)(2,1)S(1)}, u32[]{:S(2)}, u32[]{:S(2)}) %collective-permute-start.35) | collective-permute-done | bytes 172064 | tf_op jit(solution)/shard_map/ppermute | solution.py:53
  223.9 1.9 collective-permute-start.40
  228.5 2.8 %collective-permute-done.39 = f32[1536]{0:T(1024)S(1)} collective-permute-done((f32[1536]{0:T(1024)S(1)}, f32[1536]{0:T(1024)S(1)}, u32[]{:S(2)}, u32[]{:S(2)}) %collective-permute-start.39) | collective-permute-done | bytes 6176 | tf_op jit(solution)/shard_map/ppermute | solution.py:38
  (267 shorter events, 43.7 us)
Async XLA Ops:
  0.7 30.5 %copy-start.51 = (bf16[128,768]{1,0:T(8,128)(2,1)S(1)}, bf16[128,768]{1,0:T(8,128)(2,1)}, u32[]{:S(2)}) copy-start(bf16[128,768]{1,0:T(8,128)(2,1)} %seed.1) | copy-start | bytes 589828
  2.6 11.1 %collective-permute-start = (bf16[160,768]{1,0:T(8,128)(2,1)S(1)}, bf16[160,768]{1,0:T(8,128)(2,1)S(1)}, u32[]{:S(2)}, u32[]{:S(2)}) collective-permute-start(bf16[160,768]{1,0:T(8,128)(2,1)S(1)} %pad_maximum_fusion.4), channel_id=1, source_target_pairs={{0,1},{1,2},{2,3},{3,0},{4,5},{5,6},{6,7},{7,4},{8,9},{9,10},{10,1... | collective-permute-start | bytes 737288 | tf_op jit(solution)/shard_map/ppermute | solution.py:38
  6.5 25.7 %copy-start.18 = (bf16[96,128]{1,0:T(8,128)(2,1)}, bf16[96,128]{1,0:T(8,128)(2,1)S(1)}, u32[]{:S(2)}) copy-start(bf16[96,128]{1,0:T(8,128)(2,1)S(1)} %slice.220) | copy-start | bytes 73732
  6.5 25.7 %copy-start.6 = (bf16[96,768]{1,0:T(8,128)(2,1)S(1)}, bf16[96,768]{1,0:T(8,128)(2,1)}, u32[]{:S(2)}) copy-start(bf16[96,768]{1,0:T(8,128)(2,1)} %param.22) | copy-start | bytes 442372
  6.5 25.7 %copy-start.27 = (bf16[768,96]{0,1:T(8,128)(2,1)S(1)}, bf16[768,96]{0,1:T(8,128)(2,1)}, u32[]{:S(2)}) copy-start(bf16[768,96]{0,1:T(8,128)(2,1)} %param.23) | copy-start | bytes 442372
  13.7 8.7 %collective-permute-start.2 = (bf16[160,768]{1,0:T(8,128)(2,1)S(1)}, bf16[160,768]{1,0:T(8,128)(2,1)S(1)}, u32[]{:S(2)}, u32[]{:S(2)}) collective-permute-start(bf16[160,768]{1,0:T(8,128)(2,1)S(1)} %pad_maximum_fusion.4), channel_id=1, source_target_pairs={{0,3},{1,0},{2,1},{3,2},{4,7},{5,4},{6,5},{7,6},{8,11},{9,8},{10,9... | collective-permute-start | bytes 737288 | tf_op jit(solution)/shard_map/ppermute | solution.py:38
  17.2 5.2 %collective-permute-start.3 = (bf16[112,576]{1,0:T(8,128)(2,1)S(1)}, bf16[112,576]{1,0:T(8,128)(2,1)S(1)}, u32[]{:S(2)}, u32[]{:S(2)}) collective-permute-start(bf16[112,576]{1,0:T(8,128)(2,1)S(1)} %fusion.19.refs_1_), channel_id=1, source_target_pairs={{0,16},{4,12},{8,24},{12,4},{16,0},{20,28},{24,8},{28,20},{1,17},{... | collective-permute-start | bytes 387080 | tf_op jit(solution)/shard_map/ppermute | solution.py:53
  18.7 12.4 %collective-permute-start.1 = (bf16[160,768]{1,0:T(8,128)(2,1)S(1)}, bf16[160,768]{1,0:T(8,128)(2,1)S(1)}, u32[]{:S(2)}, u32[]{:S(2)}) collective-permute-start(bf16[160,768]{1,0:T(8,128)(2,1)S(1)} %pad_maximum_fusion.4), channel_id=1, source_target_pairs={{0,2},{1,3},{2,0},{3,1},{4,6},{5,7},{6,4},{7,5},{8,10},{9,11},{10,... | collective-permute-start | bytes 737288 | tf_op jit(solution)/shard_map/ppermute | solution.py:38
  22.4 9.4 %collective-permute-start.4 = (bf16[2,112,576]{2,1,0:T(8,128)(2,1)S(1)}, bf16[2,112,576]{2,1,0:T(8,128)(2,1)S(1)}, u32[]{:S(2)}, u32[]{:S(2)}) collective-permute-start(bf16[2,112,576]{2,1,0:T(8,128)(2,1)S(1)} %pad_maximum_fusion.3), channel_id=1, source_target_pairs={{0,8},{4,20},{8,0},{12,28},{16,24},{20,4},{24,16},{28,12},{1,9},{5... | collective-permute-start | bytes 774152 | tf_op jit(solution)/shard_map/ppermute | solution.py:53
  31.1 8.5 %collective-permute-start.6 = (bf16[128,768]{1,0:T(8,128)(2,1)S(1)}, bf16[128,768]{1,0:T(8,128)(2,1)S(1)}, u32[]{:S(2)}, u32[]{:S(2)}) collective-permute-start(bf16[128,768]{1,0:T(8,128)(2,1)S(1)} %copy-done.51), channel_id=1, source_target_pairs={{0,1},{1,2},{2,3},{3,0},{4,5},{5,6},{6,7},{7,4},{8,9},{9,10},{10,1... | collective-permute-start | bytes 589832 | tf_op jit(solution)/shard_map/ppermute | solution.py:38
  31.9 2.2 collective-permute-start.5
  32.4 37.9 %copy-start.1 = (bf16[96,2304]{1,0:T(8,128)(2,1)}, bf16[96,2304]{1,0:T(8,128)(2,1)S(1)}, u32[]{:S(2)}) copy-start(bf16[96,2304]{1,0:T(8,128)(2,1)S(1)} %concatenate.52.refs_1_) | copy-start | bytes 1327108
  32.4 12.8 %collective-permute-start.12 = (bf16[96,2304]{1,0:T(8,128)(2,1)S(1)}, bf16[96,2304]{1,0:T(8,128)(2,1)S(1)}, u32[]{:S(2)}, u32[]{:S(2)}) collective-permute-start(bf16[96,2304]{1,0:T(8,128)(2,1)S(1)} %concatenate.52.refs_1_), channel_id=1, source_target_pairs={{0,16},{4,12},{8,24},{12,4},{16,0},{20,28},{24,8},{28,20},{1,17},{... | collective-permute-start | bytes 1327112 | tf_op jit(solution)/shard_map/ppermute | solution.py:53
  45.1 3.0 %collective-permute-start.8 = (bf16[512,384]{1,0:T(8,128)(2,1)}, bf16[512,384]{1,0:T(8,128)(2,1)S(1)}, u32[]{:S(2)}, u32[]{:S(2)}) collective-permute-start(bf16[512,384]{1,0:T(8,128)(2,1)} %get-tuple-element.107.kv_own), channel_id=1, source_target_pairs={{0,4},{4,0},{8,12},{12,8},{1,5},{5,1},{9,13},{13,9},{2,6},{6,2},{1... | collective-permute-start | bytes 1179656 | tf_op jit(solution)/shard_map/ppermute | solution.py:47
  45.2 25.1 %copy-start.3 = (bf16[96,2304]{1,0:T(8,128)(2,1)}, bf16[96,2304]{1,0:T(8,128)(2,1)S(1)}, u32[]{:S(2)}) copy-start(bf16[96,2304]{1,0:T(8,128)(2,1)S(1)} %collective-permute-done.12.refs_2_) | copy-start | bytes 1327108
  46.1 10.7 %collective-permute-start.7 = (bf16[512,384]{1,0:T(8,128)(2,1)S(1)}, bf16[512,384]{1,0:T(8,128)(2,1)S(1)}, u32[]{:S(2)}, u32[]{:S(2)}) collective-permute-start(bf16[512,384]{1,0:T(8,128)(2,1)S(1)} %copy-done.46), channel_id=1, source_target_pairs={{0,8},{4,12},{8,0},{12,4},{1,9},{5,13},{9,1},{13,5},{2,10},{6,14},... | collective-permute-start | bytes 1179656 | tf_op jit(solution)/shard_map/ppermute | solution.py:47
  47.6 22.6 %collective-permute-start.13 = (bf16[2,96,2304]{2,1,0:T(8,128)(2,1)S(1)}, bf16[2,96,2304]{2,1,0:T(8,128)(2,1)S(1)}, u32[]{:S(2)}, u32[]{:S(2)}) collective-permute-start(bf16[2,96,2304]{2,1,0:T(8,128)(2,1)S(1)} %pad_maximum_fusion.1), channel_id=1, source_target_pairs={{0,8},{4,20},{8,0},{12,28},{16,24},{20,4},{24,16},{28,12},{1,9},{5... | collective-permute-start | bytes 2654216 | tf_op jit(solution)/shard_map/ppermute | solution.py:53
  56.8 13.4 %collective-permute-start.9 = (bf16[512,384]{1,0:T(8,128)(2,1)S(1)}, bf16[512,384]{1,0:T(8,128)(2,1)}, u32[]{:S(2)}, u32[]{:S(2)}) collective-permute-start(bf16[512,384]{1,0:T(8,128)(2,1)S(1)} %collective-permute-done.7.kv_y), channel_id=1, source_target_pairs={{0,4},{4,0},{8,12},{12,8},{1,5},{5,1},{9,13},{13,9},{2,6},{6,2},{1... | collective-permute-start | bytes 1179656 | tf_op jit(solution)/shard_map/ppermute | solution.py:47
  56.9 11.9 %collective-permute-start.10 = (bf16[128,768]{1,0:T(8,128)(2,1)S(1)}, bf16[128,768]{1,0:T(8,128)(2,1)}, u32[]{:S(2)}, u32[]{:S(2)}) collective-permute-start(bf16[128,768]{1,0:T(8,128)(2,1)S(1)} %copy-done.52), channel_id=1, source_target_pairs={{0,2},{1,3},{2,0},{3,1},{4,6},{5,7},{6,4},{7,5},{8,10},{9,11},{10,... | collective-permute-start | bytes 589832 | tf_op jit(solution)/shard_map/ppermute | solution.py:38
  59.1 11.2 %collective-permute-start.11 = (bf16[128,768]{1,0:T(8,128)(2,1)S(1)}, bf16[128,768]{1,0:T(8,128)(2,1)}, u32[]{:S(2)}, u32[]{:S(2)}) collective-permute-start(bf16[128,768]{1,0:T(8,128)(2,1)S(1)} %copy-done.52), channel_id=1, source_target_pairs={{0,3},{1,0},{2,1},{3,2},{4,7},{5,4},{6,5},{7,6},{8,11},{9,8},{10,9... | collective-permute-start | bytes 589832 | tf_op jit(solution)/shard_map/ppermute | solution.py:38
  71.2 8.1 %collective-permute-start.17 = (bf16[4,96,2304]{2,1,0:T(8,128)(2,1)S(1)}, bf16[4,96,2304]{2,1,0:T(8,128)(2,1)S(1)}, u32[]{:S(2)}, u32[]{:S(2)}) collective-permute-start(bf16[4,96,2304]{2,1,0:T(8,128)(2,1)S(1)} %pad_maximum_fusion), channel_id=1, source_target_pairs={{0,4},{4,0},{8,12},{12,8},{16,20},{20,16},{24,28},{28,24},{1,5},{5... | collective-permute-start | bytes 5308424 | tf_op jit(solution)/shard_map/ppermute | solution.py:53
  73.4 11.4 %collective-permute-start.14 = (bf16[192,512]{1,0:T(8,128)(2,1)}, bf16[192,512]{1,0:T(8,128)(2,1)S(1)}, u32[]{:S(2)}, u32[]{:S(2)}) collective-permute-start(bf16[192,512]{1,0:T(8,128)(2,1)} %get-tuple-element.117.m0.refs_7_), channel_id=1, source_target_pairs={{0,1},{1,2},{2,3},{3,0},{4,5},{5,6},{6,7},{7,4},{8,9},{9,10},{10,1... | collective-permute-start | bytes 589832 | tf_op jit(solution)/shard_map/ppermute | solution.py:38
  76.7 16.3 %collective-permute-start.15 = (bf16[192,512]{1,0:T(8,128)(2,1)}, bf16[192,512]{1,0:T(8,128)(2,1)S(1)}, u32[]{:S(2)}, u32[]{:S(2)}) collective-permute-start(bf16[192,512]{1,0:T(8,128)(2,1)} %get-tuple-element.117.m0.refs_7_), channel_id=1, source_target_pairs={{0,2},{1,3},{2,0},{3,1},{4,6},{5,7},{6,4},{7,5},{8,10},{9,11},{10,... | collective-permute-start | bytes 589832 | tf_op jit(solution)/shard_map/ppermute | solution.py:38
  79.3 13.8 %collective-permute-start.16 = (bf16[192,512]{1,0:T(8,128)(2,1)}, bf16[192,512]{1,0:T(8,128)(2,1)S(1)}, u32[]{:S(2)}, u32[]{:S(2)}) collective-permute-start(bf16[192,512]{1,0:T(8,128)(2,1)} %get-tuple-element.117.m0.refs_7_), channel_id=1, source_target_pairs={{0,3},{1,0},{2,1},{3,2},{4,7},{5,4},{6,5},{7,6},{8,11},{9,8},{10,9... | collective-permute-start | bytes 589832 | tf_op jit(solution)/shard_map/ppermute | solution.py:38
  101.3 15.0 %collective-permute-start.18 = (bf16[128,768]{1,0:T(8,128)(2,1)}, bf16[128,768]{1,0:T(8,128)(2,1)S(1)}, u32[]{:S(2)}, u32[]{:S(2)}) collective-permute-start(bf16[128,768]{1,0:T(8,128)(2,1)} %get-tuple-element.131), channel_id=1, source_target_pairs={{0,3},{1,0},{2,1},{3,2},{4,7},{5,4},{6,5},{7,6},{8,11},{9,8},{10,9... | collective-permute-start | bytes 589832 | tf_op jit(solution)/shard_map/ppermute | solution.py:38
  105.7 19.3 %collective-permute-start.19 = (bf16[128,768]{1,0:T(8,128)(2,1)}, bf16[128,768]{1,0:T(8,128)(2,1)S(1)}, u32[]{:S(2)}, u32[]{:S(2)}) collective-permute-start(bf16[128,768]{1,0:T(8,128)(2,1)} %get-tuple-element.132), channel_id=1, source_target_pairs={{0,2},{1,3},{2,0},{3,1},{4,6},{5,7},{6,4},{7,5},{8,10},{9,11},{10,... | collective-permute-start | bytes 589832 | tf_op jit(solution)/shard_map/ppermute | solution.py:38
  107.4 17.7 %collective-permute-start.20 = (bf16[128,768]{1,0:T(8,128)(2,1)}, bf16[128,768]{1,0:T(8,128)(2,1)S(1)}, u32[]{:S(2)}, u32[]{:S(2)}) collective-permute-start(bf16[128,768]{1,0:T(8,128)(2,1)} %get-tuple-element.133), channel_id=1, source_target_pairs={{0,1},{1,2},{2,3},{3,0},{4,5},{5,6},{6,7},{7,4},{8,9},{9,10},{10,1... | collective-permute-start | bytes 589832 | tf_op jit(solution)/shard_map/ppermute | solution.py:38
  129.5 6.2 %collective-permute-start.21 = (bf16[192,128]{1,0:T(8,128)(2,1)}, bf16[192,128]{1,0:T(8,128)(2,1)S(1)}, u32[]{:S(2)}, u32[]{:S(2)}) collective-permute-start(bf16[192,128]{1,0:T(8,128)(2,1)} %get-tuple-element.138), channel_id=1, source_target_pairs={{0,1},{1,2},{2,3},{3,0},{4,5},{5,6},{6,7},{7,4},{8,9},{9,10},{10,1... | collective-permute-start | bytes 147464 | tf_op jit(solution)/shard_map/ppermute | solution.py:38
  129.6 6.2 %collective-permute-start.22 = (bf16[192,128]{1,0:T(8,128)(2,1)}, bf16[192,128]{1,0:T(8,128)(2,1)S(1)}, u32[]{:S(2)}, u32[]{:S(2)}) collective-permute-start(bf16[192,128]{1,0:T(8,128)(2,1)} %get-tuple-element.139), channel_id=1, source_target_pairs={{0,2},{1,3},{2,0},{3,1},{4,6},{5,7},{6,4},{7,5},{8,10},{9,11},{10,... | collective-permute-start | bytes 147464 | tf_op jit(solution)/shard_map/ppermute | solution.py:38
  130.4 5.9 %collective-permute-start.23 = (bf16[192,128]{1,0:T(8,128)(2,1)}, bf16[192,128]{1,0:T(8,128)(2,1)S(1)}, u32[]{:S(2)}, u32[]{:S(2)}) collective-permute-start(bf16[192,128]{1,0:T(8,128)(2,1)} %get-tuple-element.140), channel_id=1, source_target_pairs={{0,3},{1,0},{2,1},{3,2},{4,7},{5,4},{6,5},{7,6},{8,11},{9,8},{10,9... | collective-permute-start | bytes 147464 | tf_op jit(solution)/shard_map/ppermute | solution.py:38
  139.2 2.0 collective-permute-start.25
  139.2 35.7 %collective-permute-start.28 = (bf16[256,768]{1,0:T(8,128)(2,1)}, bf16[256,768]{1,0:T(8,128)(2,1)S(1)}, u32[]{:S(2)}, u32[]{:S(2)}) collective-permute-start(bf16[256,768]{1,0:T(8,128)(2,1)} %get-tuple-element.156), channel_id=1, source_target_pairs={{0,1},{1,2},{2,3},{3,0},{4,5},{5,6},{6,7},{7,4},{8,9},{9,10},{10,1... | collective-permute-start | bytes 1179656 | tf_op jit(solution)/shard_map/ppermute | solution.py:38
  149.6 15.8 %collective-permute-start.26 = (bf16[512,384]{1,0:T(8,128)(2,1)}, bf16[512,384]{1,0:T(8,128)(2,1)S(1)}, u32[]{:S(2)}, u32[]{:S(2)}) collective-permute-start(bf16[512,384]{1,0:T(8,128)(2,1)} %get-tuple-element.150), channel_id=1, source_target_pairs={{0,4},{4,0},{8,12},{12,8},{1,5},{5,1},{9,13},{13,9},{2,6},{6,2},{1... | collective-permute-start | bytes 1179656 | tf_op jit(solution)/shard_map/ppermute | solution.py:47
  152.2 18.3 %collective-permute-start.27 = (bf16[512,384]{1,0:T(8,128)(2,1)S(1)}, bf16[512,384]{1,0:T(8,128)(2,1)S(1)}, u32[]{:S(2)}, u32[]{:S(2)}) collective-permute-start(bf16[512,384]{1,0:T(8,128)(2,1)S(1)} %copy-done.50), channel_id=1, source_target_pairs={{0,8},{4,12},{8,0},{12,4},{1,9},{5,13},{9,1},{13,5},{2,10},{6,14},... | collective-permute-start | bytes 1179656 | tf_op jit(solution)/shard_map/ppermute | solution.py:47
  161.1 21.3 %collective-permute-start.29 = (bf16[256,768]{1,0:T(8,128)(2,1)S(1)}, bf16[256,768]{1,0:T(8,128)(2,1)S(1)}, u32[]{:S(2)}, u32[]{:S(2)}) collective-permute-start(bf16[256,768]{1,0:T(8,128)(2,1)S(1)} %copy-done.49), channel_id=1, source_target_pairs={{0,2},{1,3},{2,0},{3,1},{4,6},{5,7},{6,4},{7,5},{8,10},{9,11},{10,... | collective-permute-start | bytes 1179656 | tf_op jit(solution)/shard_map/ppermute | solution.py:38
  162.9 19.5 %collective-permute-start.24 = (bf16[256,768]{1,0:T(8,128)(2,1)S(1)}, bf16[256,768]{1,0:T(8,128)(2,1)S(1)}, u32[]{:S(2)}, u32[]{:S(2)}) collective-permute-start(bf16[256,768]{1,0:T(8,128)(2,1)S(1)} %copy-done.48), channel_id=1, source_target_pairs={{0,3},{1,0},{2,1},{3,2},{4,7},{5,4},{6,5},{7,6},{8,11},{9,8},{10,9... | collective-permute-start | bytes 1179656 | tf_op jit(solution)/shard_map/ppermute | solution.py:38
  165.5 22.3 %collective-permute-start.36 = (bf16[4,96,1536]{2,1,0:T(8,128)(2,1)S(1)}, bf16[4,96,1536]{2,1,0:T(8,128)(2,1)S(1)}, u32[]{:S(2)}, u32[]{:S(2)}) collective-permute-start(bf16[4,96,1536]{2,1,0:T(8,128)(2,1)S(1)} %copy-done.45), channel_id=1, source_target_pairs={{0,4},{4,0},{8,12},{12,8},{16,20},{20,16},{24,28},{28,24},{1,5},{5... | collective-permute-start | bytes 3538952 | tf_op jit(solution)/shard_map/ppermute | solution.py:53
  187.8 13.9 %collective-permute-start.30 = (bf16[4,112,768]{2,1,0:T(8,128)(2,1)}, bf16[4,112,768]{2,1,0:T(8,128)(2,1)S(1)}, u32[]{:S(2)}, u32[]{:S(2)}) collective-permute-start(bf16[4,112,768]{2,1,0:T(8,128)(2,1)} %get-tuple-element.162), channel_id=1, source_target_pairs={{0,4},{4,0},{8,12},{12,8},{16,20},{20,16},{24,28},{28,24},{1,5},{5... | collective-permute-start | bytes 2064392 | tf_op jit(solution)/shard_map/ppermute | solution.py:53
  189.1 14.7 %collective-permute-start.37 = (bf16[2,96,1536]{2,1,0:T(8,128)(2,1)}, bf16[2,96,1536]{2,1,0:T(8,128)(2,1)}, u32[]{:S(2)}, u32[]{:S(2)}) collective-permute-start(bf16[2,96,1536]{2,1,0:T(8,128)(2,1)} %slice.376), channel_id=1, source_target_pairs={{0,16},{4,12},{8,24},{12,4},{16,0},{20,28},{24,8},{28,20},{1,17},{... | collective-permute-start | bytes 1769480 | tf_op jit(solution)/shard_map/ppermute | solution.py:53
  191.2 23.4 %collective-permute-start.34 = (bf16[128,768]{1,0:T(8,128)(2,1)}, bf16[128,768]{1,0:T(8,128)(2,1)S(1)}, u32[]{:S(2)}, u32[]{:S(2)}) collective-permute-start(bf16[128,768]{1,0:T(8,128)(2,1)} %get-tuple-element.172), channel_id=1, source_target_pairs={{0,1},{1,2},{2,3},{3,0},{4,5},{5,6},{6,7},{7,4},{8,9},{9,10},{10,1... | collective-permute-start | bytes 589832 | tf_op jit(solution)/shard_map/ppermute | solution.py:38
  198.9 15.8 %collective-permute-start.33 = (bf16[128,768]{1,0:T(8,128)(2,1)}, bf16[128,768]{1,0:T(8,128)(2,1)S(1)}, u32[]{:S(2)}, u32[]{:S(2)}) collective-permute-start(bf16[128,768]{1,0:T(8,128)(2,1)} %get-tuple-element.170), channel_id=1, source_target_pairs={{0,2},{1,3},{2,0},{3,1},{4,6},{5,7},{6,4},{7,5},{8,10},{9,11},{10,... | collective-permute-start | bytes 589832 | tf_op jit(solution)/shard_map/ppermute | solution.py:38
  201.7 12.9 %collective-permute-start.32 = (bf16[128,768]{1,0:T(8,128)(2,1)S(1)}, bf16[128,768]{1,0:T(8,128)(2,1)S(1)}, u32[]{:S(2)}, u32[]{:S(2)}) collective-permute-start(bf16[128,768]{1,0:T(8,128)(2,1)S(1)} %copy-done.53), channel_id=1, source_target_pairs={{0,3},{1,0},{2,1},{3,2},{4,7},{5,4},{6,5},{7,6},{8,11},{9,8},{10,9... | collective-permute-start | bytes 589832 | tf_op jit(solution)/shard_map/ppermute | solution.py:38
  203.2 10.7 %collective-permute-start.31 = (bf16[2,112,768]{2,1,0:T(8,128)(2,1)S(1)}, bf16[2,112,768]{2,1,0:T(8,128)(2,1)S(1)}, u32[]{:S(2)}, u32[]{:S(2)}) collective-permute-start(bf16[2,112,768]{2,1,0:T(8,128)(2,1)S(1)} %slice.377), channel_id=1, source_target_pairs={{0,16},{4,12},{8,24},{12,4},{16,0},{20,28},{24,8},{28,20},{1,17},{... | collective-permute-start | bytes 1032200 | tf_op jit(solution)/shard_map/ppermute | solution.py:53
  205.1 17.1 %collective-permute-start.38 = (bf16[96,1536]{1,0:T(8,128)(2,1)S(1)}, bf16[96,1536]{1,0:T(8,128)(2,1)S(1)}, u32[]{:S(2)}, u32[]{:S(2)}) collective-permute-start(bf16[96,1536]{1,0:T(8,128)(2,1)S(1)} %fusion.14), channel_id=1, source_target_pairs={{0,8},{4,20},{8,0},{12,28},{16,24},{20,4},{24,16},{28,12},{1,9},{5... | collective-permute-start | bytes 884744 | tf_op jit(solution)/shard_map/ppermute | solution.py:53
  214.1 5.5 %collective-permute-start.35 = (bf16[112,768]{1,0:T(8,128)(2,1)S(1)}, bf16[112,768]{1,0:T(8,128)(2,1)S(1)}, u32[]{:S(2)}, u32[]{:S(2)}) collective-permute-start(bf16[112,768]{1,0:T(8,128)(2,1)S(1)} %fusion.18), channel_id=1, source_target_pairs={{0,8},{4,20},{8,0},{12,28},{16,24},{20,4},{24,16},{28,12},{1,9},{5... | collective-permute-start | bytes 516104 | tf_op jit(solution)/shard_map/ppermute | solution.py:53
  223.3 4.0 %collective-permute-start.41 = (f32[1536]{0:T(1024)S(1)}, f32[1536]{0:T(1024)S(1)}, u32[]{:S(2)}, u32[]{:S(2)}) collective-permute-start(f32[1536]{0:T(1024)S(1)} %concatenate.55), channel_id=1, source_target_pairs={{0,3},{1,0},{2,1},{3,2},{4,7},{5,4},{6,5},{7,6},{8,11},{9,8},{10,9... | collective-permute-start | bytes 18440 | tf_op jit(solution)/shard_map/ppermute | solution.py:38
  223.9 4.5 %collective-permute-start.40 = (f32[1536]{0:T(1024)S(1)}, f32[1536]{0:T(1024)S(1)}, u32[]{:S(2)}, u32[]{:S(2)}) collective-permute-start(f32[1536]{0:T(1024)S(1)} %concatenate.55), channel_id=1, source_target_pairs={{0,2},{1,3},{2,0},{3,1},{4,6},{5,7},{6,4},{7,5},{8,10},{9,11},{10,... | collective-permute-start | bytes 18440 | tf_op jit(solution)/shard_map/ppermute | solution.py:38
  225.9 5.4 %collective-permute-start.39 = (f32[1536]{0:T(1024)S(1)}, f32[1536]{0:T(1024)S(1)}, u32[]{:S(2)}, u32[]{:S(2)}) collective-permute-start(f32[1536]{0:T(1024)S(1)} %concatenate.55), channel_id=1, source_target_pairs={{0,1},{1,2},{2,3},{3,0},{4,5},{5,6},{6,7},{7,4},{8,9},{9,10},{10,1... | collective-permute-start | bytes 18440 | tf_op jit(solution)/shard_map/ppermute | solution.py:38
  (55 other events, 318.5 us)
where the time goes:
time: 234 us; the launch traced here: 233 us
  waiting for transfers between devices  79 us (34%)
  starting transfers between devices  64.3 us (27%)
  Pallas kernels  54.3 us (23%)
  local copies, waits for them, and re-layouts  22.4 us (10%)
  other arithmetic  11.7 us (5%)
    ppermute x24, waiting for transfers between devices, passed_along(): lax.ppermute(array, 'uly', [(i, (i + by) % peers) for i in range(peers)])  55.1 us
    pallas_call x14, Pallas kernels, on_core(): pl.pallas_call(kernel, out_shape=[jax.ShapeDtypeStruct(shape, dtype) for...  54.3 us
    ppermute x24, starting transfers between devices, passed_along(): lax.ppermute(array, 'uly', [(i, (i + by) % peers) for i in range(peers)])  42.8 us
    ppermute x12, waiting for transfers between devices, cube_swapped(): return lax.ppermute(array, CUBE, pairs)  14.7 us
    ppermute x6, starting transfers between devices, blk_swapped(): return lax.ppermute(array, 'blk', [(i, i ^ flip) for i in range(peers)])  13.1 us
    unnamed x124, local copies, waits for them, and re-layouts  10.5 us
    ppermute x6, waiting for transfers between devices, blk_swapped(): return lax.ppermute(array, 'blk', [(i, i ^ flip) for i in range(peers)])  9.18 us
    ppermute x12, starting transfers between devices, cube_swapped(): return lax.ppermute(array, CUBE, pairs)  8.37 us
  transfers between devices with their start and end apart: 42, of which 19 were waited for; matrix products, arithmetic and copies ran while one was open for 9% of the time, Pallas kernels for 18%

commit v1 on v0

--- a/solution.py
+++ b/solution.py
@@ -10,8 +10,6 @@
 VEC_ROWS = 16
 VMEM_LIMIT = 56 * 1024 * 1024
 KERNEL_COST = 30_000_000_000
-BRIEF_COST = 1
-NEAR_COST = 3_000_000_000
 
 KEY_GROUP, KEY_HALF = (0, 0, 1), (0, 1, 0)
 VALUE_GROUP, VALUE_HALF = (2, 2, 1), (0, 1, 1)
@@ -98,33 +96,28 @@
 def grads_kernel(pairs, spread, index, *refs):
     ins, (sent, kept), (whole, extra) = refs[:-4], refs[-4:-2], refs[-2:]
     at = 0
-    lefts = []
-    for count, last, pad, column, columns in pairs:
-        left, right = stacked_slots(ins[at : at + count], last), ins[at + count][...]
+    for count, flipped, column, columns in pairs:
+        left, right = stacked_slots(ins[at : at + count]), ins[at + count][...]
         at += count + 1
-        if pad:
-            right = jnp.concatenate([jnp.zeros((pad, right.shape[1]), right.dtype), right], axis=0).T
-        term = dot_plain(left.T, right)
-        if pad:
-            whole[:, column : column + columns] += term
-        else:
-            whole[:, column : column + columns] = term
-        lefts.append((left, right))
+        whole[:, column : column + columns] = dot_plain(left.T, right.T if flipped else right)
     rows = kept.shape[1]
-    depth = whole.shape[0] // 8
+    model, wide = whole.shape
+    depth = model // 8
     if spread:
-        hidden_sum, seed_sum = ins[at][...], ins[at + 1][...]
-        qkv_sum = jnp.sum(lefts[0][1].astype(jnp.float32), axis=0, keepdims=True)
-        branch_sum = jnp.sum(lefts[1][0].astype(jnp.float32), axis=0, keepdims=True)
-        wide = whole.shape[1]
-        stacked = jnp.concatenate(
-            [qkv_sum, hidden_sum, branch_sum, seed_sum, jnp.zeros((4, wide), jnp.float32)], axis=0
+        hidden_sum, seed_sum, branch = ins[at], ins[at + 1], ins[at + 2]
+        half = hidden_sum.shape[1] // 2
+        right_sum = jnp.sum(right.astype(jnp.float32), axis=0, keepdims=True)
+        branch_sum = jnp.sum(branch[...].astype(jnp.float32), axis=0, keepdims=True)
+        whole_rows = jnp.concatenate([right_sum, jnp.zeros((7, wide), jnp.float32)], axis=0)
+        part_rows = jnp.concatenate(
+            [branch_sum, seed_sum[...], jnp.zeros((6, model), jnp.float32)], axis=0
         )
-        line = lax.broadcasted_iota(jnp.int32, stacked.shape, 0)
         for block in range(8):
-            turned = stacked if block == 0 else pltpu.roll(stacked, wide - depth * block, 1)
-            extra[block, 0:8] = jnp.where(line < 2, stacked, turned)
-            extra[block, 8:16] = jnp.zeros((8, wide), jnp.float32)
+            turned = part_rows if block == 0 else pltpu.roll(part_rows, model - depth * block, 1)
+            extra[block, 0:8] = whole_rows
+            extra[block, 1:2, 0:half] = hidden_sum[:, :half]
+            extra[block, 2:3, 0:half] = hidden_sum[:, half:]
+            extra[block, 8:16] = turned[:, :wide]
     me = index[0]
     near, far = cube_flips(me)
     for slot, flip in enumerate((0, near, far, 6)):
@@ -139,44 +132,40 @@
             kept[slot, depth:rows] = extra[block]
 
 
-def grads_sent(pairs, columns, depth, sums):
+def grads_sent(pairs, columns, depth):
     plan = [
-        (len(left), last, pad, column, right.shape[0] + pad if pad else right.shape[1])
-        for left, last, right, pad, column in pairs
-    ]
-    operands = [item for left, _, right, _, _ in pairs for item in [*left, right]]
-    rows = depth + (VEC_ROWS if sums else 0)
+        (len(left), flipped, column, right.shape[0 if flipped else 1])
+        for left, flipped, right, column in pairs
+    ]
+    operands = [item for left, _, right, _ in pairs for item in [*left, right]]
     index = cube_index().astype(jnp.int32).reshape(1)
     return on_core(
-        lambda *refs: grads_kernel(plan, bool(sums), *refs),
+        lambda *refs: grads_kernel(plan, False, *refs),
         index,
-        operands + list(sums),
-        [((4, rows, columns), jnp.bfloat16), ((4, rows, columns), jnp.float32)],
+        operands,
+        [((4, depth, columns), jnp.bfloat16), ((4, depth, columns), jnp.float32)],
         [((8 * depth, columns), jnp.float32), ((8, VEC_ROWS, columns), jnp.float32)],
     )
 
 
 def grads_scattered(pairs, columns, owners, sums):
-    model = pairs[0][0][0].shape[1]
+    blocks = []
+    for left, flipped, right, _ in pairs:
+        right = right.T if flipped else right
+        blocks.append(dot_rows(stacked_slots(left), right))
+    model = blocks[0].shape[0]
     depth = model // owners
-    whole = jnp.zeros((model, columns), jnp.float32)
-
-    pairs = [(stacked_slots(left, last), *rest) for left, last, *rest in pairs]
-    for left, right, pad, column in pairs:
-        if pad:
-            column += pad
-            right = right.T
-        term = dot_rows(left, right)
-        whole = whole.at[:, column : column + term.shape[1]].add(term)
-    blocks = whole.reshape(owners, depth, columns)
+    blocks = jnp.concatenate(blocks, axis=1).reshape(owners, depth, columns)
     if sums:
-        hidden_sum, seed_sum = sums
-        branch_sum = jnp.sum(pairs[1][0].astype(jnp.float32), axis=0)
+        hidden_sum, seed_sum, branch = sums
+        half = hidden_sum.shape[1] // 2
+        branch_sum = jnp.sum(branch.astype(jnp.float32), axis=0)
         extra = jnp.zeros((owners, VEC_ROWS, columns), jnp.float32)
-        extra = extra.at[:, 0].set(jnp.sum(pairs[0][1].astype(jnp.float32), axis=0)[None])
-        extra = extra.at[:, 1].set(hidden_sum)
-        extra = extra.at[:, 2, :depth].set(branch_sum.reshape(owners, depth))
-        extra = extra.at[:, 3, :depth].set(seed_sum.reshape(owners, depth))
+        extra = extra.at[:, 0].set(jnp.sum(pairs[0][2].astype(jnp.float32), axis=0)[None])
+        extra = extra.at[:, 1, :half].set(hidden_sum[:, :half])
+        extra = extra.at[:, 2, :half].set(hidden_sum[:, half:])
+        extra = extra.at[:, 8, :depth].set(branch_sum.reshape(owners, depth))
+        extra = extra.at[:, 9, :depth].set(seed_sum.reshape(owners, depth))
         blocks = jnp.concatenate([blocks, extra], axis=1)
     return lax.psum_scatter(blocks, CUBE, scatter_dimension=0, tiled=False)
 
@@ -369,7 +358,7 @@
     query_grad[...] = (total[...] * HEAD_DIM**-0.5).T.astype(jnp.bfloat16)
 
 
-def on_core(kernel, place, operands, outs, scratch=(), cost=KERNEL_COST):
+def on_core(kernel, place, operands, outs, scratch=()):
     vmem = pl.BlockSpec(memory_space=pltpu.VMEM)
     return pl.pallas_call(
         kernel,
@@ -378,7 +367,7 @@
         out_specs=[vmem] * len(outs),
         scratch_shapes=[pltpu.VMEM(shape, dtype) for shape, dtype in scratch],
         compiler_params=pltpu.CompilerParams(vmem_limit_bytes=VMEM_LIMIT),
-        cost_estimate=pl.CostEstimate(flops=cost, transcendentals=0, bytes_accessed=0),
+        cost_estimate=pl.CostEstimate(flops=KERNEL_COST, transcendentals=0, bytes_accessed=0),
     )(place, *operands)
 
 
@@ -396,11 +385,9 @@
     )
 
 
-def stacked_slots(refs, last=False):
+def stacked_slots(refs):
     rows = refs[0].shape[0]
-    return jnp.concatenate(
-        [ref[ref.shape[0] - rows :] if last else ref[:rows] for ref in refs], axis=0
-    )
+    return jnp.concatenate([ref[:rows] for ref in refs], axis=0)
 
 
 def project_kernel(place, t0, t1, t2, t3, weight, named, bias, query, kv, xhat_low):
@@ -438,6 +425,7 @@
     up_bias,
     middle_own,
     xhat_low,
+    mixed_own,
     active_low,
     hidden_back_low,
     part_own,
@@ -452,6 +440,7 @@
         ],
         axis=0,
     )
+    mixed_own[...] = mixed_t[:, :slot]
     branch = dot_plain(output_t[...], mixed_t).T
     middle = stacked_slots((t0, t1, t2, t3)).astype(jnp.float32) + (branch + named[0:1])
     middle_own[...] = middle[:slot]
@@ -497,14 +486,8 @@
     seed,
     gain,
     output_t,
-    o1,
-    o2,
-    o3,
     middle_back,
     branch_back,
-    s1,
-    s2,
-    s3,
     *mixed_back_t,
 ):
     second_back = part_own[...]
@@ -515,29 +498,37 @@
     middle_back[...] = grad
     low = grad.astype(jnp.bfloat16)
     branch_back[...] = low
-    slot = low.shape[0]
-    for ref, outside in ((s1, o1), (s2, o2), (s3, o3)):
-        ref[:slot] = outside[...]
-        ref[slot:] = low
     turned = dot_plain(low, output_t[...]).T.astype(jnp.bfloat16)
     width = mixed_back_t[0].shape[0]
     for by in range(4):
         mixed_back_t[by][...] = turned[by * width : (by + 1) * width]
 
 
-def gather_back_kernel(place, own, core, far, query, weight, dqkv, part_own, *parts):
+def gather_back_kernel(place, own, core, far, query, weight, o1, o2, o3, dqkv, part_own, *parts):
     wide = own.shape[1]
     width = query.shape[1]
     total = own[...].astype(jnp.float32) + core[...].astype(jnp.float32)
     kv_grad = (total + far[...].astype(jnp.float32)).astype(jnp.bfloat16)
     dqkv[:, :wide] = kv_grad
     dqkv[:, wide : wide + width] = query[...]
-    dqkv[:, wide + width :] = jnp.zeros((query.shape[0], width), jnp.bfloat16)
+    spare = dqkv.shape[1] - wide - width
+    dqkv[:, wide + width :] = jnp.zeros((query.shape[0], spare), jnp.bfloat16)
     normed_back = dot_cols(dqkv[:, : wide + width], weight[...])
     slot = part_own.shape[0]
     part_own[...] = normed_back[:slot]
-    for by in range(1, 4):
-        parts[by - 1][...] = normed_back[by * slot : (by + 1) * slot].astype(jnp.bfloat16)
+    for by, outside in ((1, o1), (2, o2), (3, o3)):
+        parts[by - 1][:slot] = normed_back[by * slot : (by + 1) * slot].astype(jnp.bfloat16)
+        parts[by - 1][slot:] = outside[...]
+
+
+def last_kernel(index, *refs):
+    ins, (xhat, hidden_sum, seed_sum, branch) = refs[:8], refs[8:12]
+    part_own, p1, p2, p3, sent, kept, dqkv, whole, extra = refs[12:]
+    gather_back_kernel(index, *ins, dqkv, part_own, p1, p2, p3)
+    plan = [(1, False, 0, dqkv.shape[1])]
+    grads_kernel(
+        plan, True, index, xhat, dqkv, hidden_sum, seed_sum, branch, sent, kept, whole, extra
+    )
 
 
 def slots_returned(parts):
@@ -636,7 +627,6 @@
         [jnp.zeros((width,), f32), value_bias_own[128:], value_bias_own[:128], query_bias_own]
     )
 
-    units_grad = 2 * units
     inner = groups * width
     rest_cuts = [
         (0, depth, 0, inner),
@@ -656,10 +646,11 @@
         rest_own = after(rest_own, qkv_second)
         rest_first = cube_swapped(rest_own, 4, 2)
 
+    qkv_ready = after(qkv_whole, cotangent_slots[1])
     query, kv_own, xhat1_low = on_core(
         project_kernel,
         place,
-        token_slots + [after(qkv_whole, cotangent_slots[1]), named[4:6], qkv_bias[None]],
+        token_slots + [qkv_ready, named[4:6], qkv_bias[None]],
         [((rows, width), bf16), ((rows, 2 * width), bf16), ((rows, model), bf16)],
     )
     kv_y = blk_swapped(kv_own, 2)
@@ -669,7 +660,7 @@
     top, total, mixed_t = on_core(
         forward_near_kernel, place, (query, kv_own, kv_core), (stats, stats, turned)
     )
-    kv_both = after(blk_swapped(after(kv_y, top), 1), *cotangent_slots[2:])
+    kv_both = blk_swapped(after(kv_y, top, *cotangent_slots[2:]), 1)
     if paired():
         rest_second = cube_swapped(after(jnp.stack([rest_own, rest_first]), kv_own), 2, 4)
         rest_second = after(rest_second, kv_both)
@@ -700,23 +691,16 @@
     slabs = [((part, model), bf16)] * (groups - 1)
     wide_low = ((rows, model), bf16)
     units_low = ((rows, units), bf16)
-    middle, xhat2_low, active, hidden_back, second_own, *second_parts = on_core(
+    middle, xhat2_low, mixed_own, active, hidden_back, second_own, *second_parts = on_core(
         middle_kernel,
         place,
         mixed_slots
         + token_slots
         + cotangent_slots
         + [output_t, up_whole, down_t, jnp.stack([output_bias_all, gain2, shift2]), up_bias_own[None]],
-        [slab, wide_low, units_low, units_low, slab] + slabs,
+        [slab, wide_low, ((inner, part), bf16), units_low, units_low, slab] + slabs,
     )
     second_returned = slots_returned(second_parts)
-    wide_pairs = [
-        ([xhat2_low], False, hidden_back, 0, 0),
-        (cotangent_slots, False, active, 0, units),
-    ]
-    if paired():
-        wide_sent, wide_kept = grads_sent(wide_pairs, units_grad, depth, ())
-        second_own = after(second_own, wide_sent)
     hidden_sum, seed_sum, outside_own, *outside_parts = on_core(
         outside_kernel,
         place,
@@ -725,99 +709,92 @@
     )
     second_own = after(second_own, outside_own)
 
-    middle_back, branch_back, s1, s2, s3, *mixed_back_t = on_core(
+    middle_back, branch_back, *mixed_back_t = on_core(
         branch_kernel,
         place,
-        [second_own] + second_returned + [middle, cotangent, gain2[None], output_t] + outside_parts,
-        [slab, ((part, model), bf16)]
-        + [((2 * part, model), bf16)] * 3
-        + [((width, part), bf16)] * groups,
+        [second_own] + second_returned + [middle, cotangent, gain2[None], output_t],
+        [slab, ((part, model), bf16)] + [((width, part), bf16)] * groups,
     )
     grad_slots = [mixed_back_t[0]] + [
         passed_along(mixed_back_t[by], -by) for by in range(groups - 1, 0, -1)
     ]
+    wide_pairs = [
+        ([xhat2_low], False, hidden_back, 0),
+        (cotangent_slots, False, active, units),
+        ([branch_back], True, mixed_own, 2 * units),
+    ]
+    wide_columns = 2 * units + inner
     if paired():
-        wide_got = cube_swapped(after(wide_sent, mixed_back_t[0]), 1, 1)
+        wide_sent, wide_kept = grads_sent(wide_pairs, wide_columns, depth)
+        wide_got = cube_swapped(wide_sent, 1, 1)
+        grad_slots[1] = after(grad_slots[1], wide_sent)
     sides = [query] + grad_slots + [mixed_t, lse]
     pair = ((rows, 2 * width), bf16)
     dkv_both, query_grad_t = on_core(
-        backward_both_kernel, place, sides + [kv_both], (pair, turned), cost=BRIEF_COST
-    )
-    shared = slots_returned([after(item, *grad_slots[1:]) for item in (s1, s2, s3)])
-    branch_slots = [branch_back] + shared[::-1]
+        backward_both_kernel, place, sides + [kv_both], (pair, turned)
+    )
     if paired():
         wide_held = wide_kept + after(wide_got, dkv_both).astype(f32)
-        wide_sent = wide_held[2:].astype(bf16)
-        wide_got = cube_swapped(wide_sent, 4, 2)
+        wide_next = wide_held[2:].astype(bf16)
+        wide_got = cube_swapped(wide_next, 4, 2)
     dkv_y, query_grad_t = on_core(
         backward_y_kernel,
         place,
         sides + [kv_y, blk_swapped(dkv_both, 1), query_grad_t],
         (pair, turned),
         [((rows, 2 * width), f32)],
-        cost=BRIEF_COST,
     )
     dkv_from_y = blk_swapped(dkv_y, 2)
-    if paired():
-        wide_got = after(wide_got, dkv_y).astype(f32)
-        wide_held = wide_held[:2] + wide_got
-        wide_sent = wide_held[1].astype(bf16)
+    kv_last = after(kv_core, wide_next) if paired() else kv_core
     dkv_own, dkv_core, query_grad = on_core(
         backward_near_kernel,
         place,
-        sides + [kv_own, kv_core, query_grad_t],
+        sides + [kv_own, kv_last, query_grad_t],
         (pair, pair, ((rows, width), bf16)),
         (turned,),
-        cost=NEAR_COST,
     )
     dkv_core = blk_swapped(dkv_core, 1)
-    dqkv, normed_own, *normed_parts = on_core(
-        gather_back_kernel,
-        place,
-        [dkv_own, dkv_core, dkv_from_y, query_grad, qkv_whole],
-        [((rows, wide + width), bf16), slab] + slabs,
-        cost=BRIEF_COST,
-    )
+    columns = -(-wide // 128) * 128
+    back_operands = [dkv_own, dkv_core, dkv_from_y, query_grad, qkv_whole] + outside_parts
+    back_outs = [slab] + [((2 * part, model), bf16)] * 3
+    sums = (hidden_sum, seed_sum, branch_back)
+    dqkv_kind = ((rows, columns), bf16)
+    if paired():
+        kinds = [((4, depth + VEC_ROWS, columns), kind) for kind in (bf16, f32)]
+        normed_own, *normed_parts, near_sent, near_kept = on_core(
+            last_kernel,
+            cube_index().astype(jnp.int32).reshape(1),
+            back_operands + [xhat1_low] + list(sums),
+            back_outs + kinds,
+            [dqkv_kind, ((model, columns), f32), ((8, VEC_ROWS, columns), f32)],
+        )
+    else:
+        dqkv, normed_own, *normed_parts = on_core(
+            gather_back_kernel, place, back_operands, [dqkv_kind] + back_outs
+        )
     normed_returned = slots_returned(normed_parts)
 
-    columns = wide + width
-    near_pairs = [
-        ([xhat1_low], False, dqkv, 0, 0),
-        (branch_slots, True, mixed_low, wide - 512, 512),
-    ]
-    sums = (hidden_sum, seed_sum)
     if paired():
-        near_sent, near_kept = grads_sent(near_pairs, columns, depth, sums)
         near_got = cube_swapped(near_sent, 1, 1).astype(f32)
+        wide_held = wide_held[:2] + after(wide_got, near_sent).astype(f32)
+        wide_last = wide_held[1].astype(bf16)
         near_held = near_kept + near_got
         near_next = near_held[2:].astype(bf16)
         near_got = cube_swapped(near_next, 4, 2).astype(f32)
         near_held = near_held[:2] + near_got
-        near_last = near_held[1].astype(bf16)
-        near_got = cube_swapped(near_last, 2, 4).astype(f32)
+        near_got = cube_swapped(near_held[1].astype(bf16), 2, 4).astype(f32)
         near_total = near_held[0] + near_got
-        wide_got = cube_swapped(after(wide_sent, near_sent), 2, 4).astype(f32)
+        wide_got = cube_swapped(wide_last, 2, 4).astype(f32)
         wide_total = wide_held[0] + wide_got
     else:
-        near_total = grads_scattered(near_pairs, columns, owners, sums)
-        wide_total = grads_scattered(wide_pairs, units_grad, owners, ())
-        near_last = near_total
-
-    normed_back = normed_own
-    for item in normed_returned:
-        normed_back = normed_back + after(item, near_last).astype(f32)
-    outside = outside_own
-    for item in shared:
-        outside = outside + after(item, near_last)[:part].astype(f32)
-    xhat1, rstd1 = normalized(tokens.astype(f32))
-    input_grad = (middle_back + norm_back(normed_back * gain1, xhat1, rstd1)).astype(bf16)
-    result = (middle + (outside + down_bias_all)).astype(bf16)
-
-    qkv_total = near_total[:depth, :wide]
-    output_total = near_total[:depth, wide:].T
-    qkv_sums, hidden_sums = near_total[depth, :wide], near_total[depth + 1, :units]
-    branch_sums, seed_sums = near_total[depth + 2, :depth], near_total[depth + 3, :depth]
-    up_total, down_total = wide_total[:, :units], wide_total[:, units:].T
+        near_total = grads_scattered([([xhat1_low], False, dqkv, 0)], columns, owners, sums)
+        wide_total = grads_scattered(wide_pairs, wide_columns, owners, ())
+
+    half = units // 2
+    qkv_total, qkv_sums = near_total[:depth, :wide], near_total[depth, :wide]
+    hidden_sums = near_total[depth + 1 : depth + 3, :half].reshape(-1)
+    branch_sums, seed_sums = near_total[depth + 8, :depth], near_total[depth + 9, :depth]
+    up_total, down_total = wide_total[:, :units], wide_total[:, units : 2 * units].T
     own_gain1, own_shift1 = first_gain.astype(f32), first_shift.astype(f32)
     own_gain2, own_shift2 = second_gain.astype(f32), second_shift.astype(f32)
     qkv_weight_grad = own_gain1[:, None] * qkv_total + own_shift1[:, None] * qkv_sums[None]
@@ -829,15 +806,24 @@
             jnp.sum(qkv_wide * qkv_sums[None], axis=1),
             jnp.sum(up_wide * up_total, axis=1),
             jnp.sum(up_wide * hidden_sums[None], axis=1),
+            branch_sums,
             qkv_sums[2 * width :],
             qkv_sums[width + 64 : 2 * width],
             qkv_sums[width : width + 64],
             hidden_sums,
         ]
     )
-    all_terms = jnp.stack(slots_of(terms))
+    term_rows = -(-terms.shape[0] // (8 * width)) * 8
+    terms = jnp.pad(terms, (0, term_rows * width - terms.shape[0])).reshape(term_rows, width)
+    blocks = [wide_total[:, 2 * units + by * width :][:, :width] for by in range(groups)]
+    final_sent = [jnp.concatenate([block, terms], axis=0).astype(bf16) for block in blocks[1:]]
+    returned = [item.astype(f32) for item in slots_returned(final_sent)]
+    output_total = blocks[0]
+    for item in returned:
+        output_total = output_total + item[:depth]
+    all_terms = jnp.stack([terms.reshape(-1)] + [item[depth:].reshape(-1) for item in returned[::-1]])
     share = depth // groups
-    added = jnp.sum(all_terms[:, : 4 * depth], axis=0).reshape(4, depth)
+    added = jnp.sum(all_terms[:, : 5 * depth], axis=0).reshape(5, depth)
     added = lax.dynamic_slice_in_dim(added, uly * share, share, axis=1)
     rank = cube_index() * groups + uly
 
@@ -846,26 +832,35 @@
         source = (uly - at // length) % groups
         return lax.dynamic_slice(all_terms, (source, start + at % length), (1, count))[0]
 
-    query_bias_grad = owned(4 * depth, width, share)
-    value_bias_grad = owned(4 * depth + width, width, share)
-    up_bias_grad = owned(4 * depth + 2 * width, units, up_bias.shape[0] // groups)
-    output_bias_grad = lax.dynamic_slice_in_dim(branch_sums, uly * share, share)
+    query_bias_grad = owned(5 * depth, width, share)
+    value_bias_grad = owned(5 * depth + width, width, share)
+    up_bias_grad = owned(5 * depth + 2 * width, units, up_bias.shape[0] // groups)
     down_bias_grad = lax.dynamic_slice_in_dim(seed_sums, uly * share, share)
     value_weight_grad = jnp.concatenate(
         [qkv_weight_grad[:, width + 64 : 2 * width], qkv_weight_grad[:, width : width + 64]], axis=1
     )
+
+    normed_back = normed_own
+    for item in normed_returned:
+        normed_back = normed_back + after(item, *final_sent)[:part].astype(f32)
+    outside = outside_own
+    for item in normed_returned:
+        outside = outside + after(item, *final_sent)[part:].astype(f32)
+    xhat1, rstd1 = normalized(tokens.astype(f32))
+    input_grad = (middle_back + norm_back(normed_back * gain1, xhat1, rstd1)).astype(bf16)
+    result = (middle + (outside + down_bias_all)).astype(bf16)
     return (
         result,
         input_grad,
         qkv_weight_grad[:, 2 * width :],
         qkv_weight_grad[:, :width],
         value_weight_grad,
-        output_total,
+        output_total.T,
         up_weight_grad,
         down_total,
         query_bias_grad,
         value_bias_grad,
-        output_bias_grad,
+        added[4],
         up_bias_grad,
         down_bias_grad,
         added[0],

time: 234 us -> 223 us (0.953)
  starting transfers between devices: 64.3 us -> 54.2 us
  other arithmetic: 11.7 us -> 15.7 us
    ppermute x24 -> x21, starting transfers between devices: 42.8 us -> 31.9 us  [passed_along(): lax.ppermute(array, 'uly', [(i, (i + by) % peers) for i in range(peers)])]
    ppermute x12, waiting for transfers between devices: 14.7 us -> 23.1 us  [cube_swapped(): return lax.ppermute(array, CUBE, pairs)]
    ppermute x6, waiting for transfers between devices: 9.18 us -> 1.36 us  [blk_swapped(): return lax.ppermute(array, 'blk', [(i, i ^ flip) for i in range(peers)])]
    pallas_call x14 -> x13, Pallas kernels: 54.3 us -> 52.1 us  [on_core(): pl.pallas_call(kernel, out_shape=[jax.ShapeDtypeStruct(shape, dtype) for...]
    ppermute x24 -> x21, waiting for transfers between devices: 55.1 us -> 53.8 us  [passed_along(): lax.ppermute(array, 'uly', [(i, (i + by) % peers) for i in range(peers)])]
    unnamed x124 -> x118, local copies, waits for them, and re-layouts: 10.5 us -> 9.33 us
  transfers between devices with their start and end apart: 42 -> 39, of which waited for: 19 -> 16; matrix products, arithmetic and copies ran while one was open for 9% -> 11% of each run, Pallas kernels for 18% -> 17%
where the time goes in v1:
time: 223 us
  waiting for transfers between devices  78.2 us (35%)
  starting transfers between devices  54.2 us (24%)
  Pallas kernels  52.1 us (23%)
  local copies, waits for them, and re-layouts  21.1 us (9%)
  other arithmetic  15.7 us (7%)
    ppermute x21, waiting for transfers between devices, passed_along(): lax.ppermute(array, 'uly', [(i, (i + by) % peers) for i in range(peers)])  53.8 us
    pallas_call x13, Pallas kernels, on_core(): pl.pallas_call(kernel, out_shape=[jax.ShapeDtypeStruct(shape, dtype) for...  52.1 us
    ppermute x21, starting transfers between devices, passed_along(): lax.ppermute(array, 'uly', [(i, (i + by) % peers) for i in range(peers)])  31.9 us
    ppermute x12, waiting for transfers between devices, cube_swapped(): return lax.ppermute(array, CUBE, pairs)  23.1 us
    ppermute x6, starting transfers between devices, blk_swapped(): return lax.ppermute(array, 'blk', [(i, i ^ flip) for i in range(peers)])  12.6 us
    ppermute x12, starting transfers between devices, cube_swapped(): return lax.ppermute(array, CUBE, pairs)  9.56 us
    unnamed x118, local copies, waits for them, and re-layouts  9.33 us
  transfers between devices with their start and end apart: 39, of which 16 were waited for; matrix products, arithmetic and copies ran while one was open for 11% of the time, Pallas kernels for 17%

profile of v1, /device:TPU:0, one launch (start us, length us, event | category | flops | bytes accessed | tf_op | source)
XLA Modules:
  0.0 222.7 jit_solution(9198934438607560020)
XLA Ops:
  2.6 3.1 %collective-permute-start = (bf16[160,768]{1,0:T(8,128)(2,1)S(1)}, bf16[160,768]{1,0:T(8,128)(2,1)S(1)}, u32[]{:S(2)}, u32[]{:S(2)}) collective-permute-start(bf16[160,768]{1,0:T(8,128)(2,1)S(1)} %pad_maximum_fusion.4), channel_id=1, source_target_pairs={{0,1},{1,2},{2,3},{3,0},{4,5},{5,6},{6,7},{7,4},{8,9},{9,10},{10,1... | collective-permute-start | bytes 737288 | tf_op jit(solution)/shard_map/ppermute | solution.py:36
  8.0 5.7 %collective-permute-done.t1 = bf16[160,768]{1,0:T(8,128)(2,1)S(1)} collective-permute-done((bf16[160,768]{1,0:T(8,128)(2,1)S(1)}, bf16[160,768]{1,0:T(8,128)(2,1)S(1)}, u32[]{:S(2)}, u32[]{:S(2)}) %collective-permute-start) | collective-permute-done | bytes 245792 | tf_op jit(solution)/shard_map/ppermute | solution.py:36
  13.7 1.7 collective-permute-start.2
  17.2 1.6 collective-permute-start.3
  18.8 3.6 %collective-permute-done.3.refs_2_ = bf16[112,576]{1,0:T(8,128)(2,1)S(1)} collective-permute-done((bf16[112,576]{1,0:T(8,128)(2,1)S(1)}, bf16[112,576]{1,0:T(8,128)(2,1)S(1)}, u32[]{:S(2)}, u32[]{:S(2)}) %collective-permute-start.3) | collective-permute-done | bytes 129056 | tf_op jit(solution)/shard_map/ppermute | solution.py:51
  22.4 1.6 collective-permute-start.4
  24.7 6.5 %collective-permute-done.1.t2 = bf16[160,768]{1,0:T(8,128)(2,1)S(1)} collective-permute-done((bf16[160,768]{1,0:T(8,128)(2,1)S(1)}, bf16[160,768]{1,0:T(8,128)(2,1)S(1)}, u32[]{:S(2)}, u32[]{:S(2)}) %collective-permute-start.1) | collective-permute-done | bytes 245792 | tf_op jit(solution)/shard_map/ppermute | solution.py:36
  32.3 1.6 collective-permute-start.12
  34.1 2.4 %shard_map.296 = (bf16[8,96,576]{2,1,0:T(8,128)(2,1)}, bf16[8,16,576]{2,1,0:T(8,128)(2,1)}) custom-call(s32[1]{0:T(128)} %bitcast.3.refs_0_.index, bf16[112,576]{1,0:T(8,128)(2,1)} %copy-done.6, bf16[112,576]{1,0:T(8,128)(2,1)} %copy-done.11, bf16[2,112,576]{2,1,0:T(8,128)(2,1)} %copy-done.16, bf16[4,112,576]{2,1,0:T(8,128)(2,1)} %collective-permute-done.5.refs_4_), custom_call_target="tpu_custom_call" | custom-call | flops 30000001024 | tf_op jit(solution)/shard_map/pallas_call | solution.py:363
  40.6 3.9 %shard_map.297 = (bf16[512,192]{1,0:T(8,128)(2,1)}, bf16[512,384]{1,0:T(8,128)(2,1)}, bf16[512,768]{1,0:T(8,128)(2,1)}) custom-call(s32[2]{0:T(128)} %pad_add_fusion.place, bf16[128,768]{1,0:T(8,128)(2,1)} %t0.3, bf16[160,768]{1,0:T(8,128)(2,1)} %copy-done.27, bf16[160,768]{1,0:T(8,128)(2,1)} %copy-done.29, bf16[160,768]{1,0:T(8,128)(2,1)} %copy-done.28, ...), custom_call_target="tpu_custom_call" | custom-call | flops 30000001024 | tf_op jit(solution)/shard_map/pallas_call | solution.py:363
  44.6 2.3 %collective-permute-start.10 = (bf16[128,768]{1,0:T(8,128)(2,1)}, bf16[128,768]{1,0:T(8,128)(2,1)S(1)}, u32[]{:S(2)}, u32[]{:S(2)}) collective-permute-start(bf16[128,768]{1,0:T(8,128)(2,1)} %refs_3_.1), channel_id=1, source_target_pairs={{0,3},{1,0},{2,1},{3,2},{4,7},{5,4},{6,5},{7,6},{8,11},{9,8},{10,9... | collective-permute-start | bytes 589832 | tf_op jit(solution)/shard_map/ppermute | solution.py:36
  47.2 1.6 collective-permute-start.7
  50.0 3.7 %shard_map.298 = (f32[8,512]{1,0:T(8,128)}, f32[8,512]{1,0:T(8,128)}, f32[192,512]{1,0:T(8,128)}) custom-call(s32[2]{0:T(128)} %pad_add_fusion.place, bf16[512,192]{1,0:T(8,128)(2,1)} %get-tuple-element.95.query, bf16[512,384]{1,0:T(8,128)(2,1)} %get-tuple-element.96.kv_own, bf16[512,384]{1,0:T(8,128)(2,1)} %copy-done.42), custom_call_target="tpu_custom_call" | custom-call | flops 30000001024 | tf_op jit(solution)/shard_map/pallas_call | solution.py:363
  53.7 7.4 %collective-permute-done.9.c2.refs_5_ = bf16[128,768]{1,0:T(8,128)(2,1)S(1)} collective-permute-done((bf16[128,768]{1,0:T(8,128)(2,1)}, bf16[128,768]{1,0:T(8,128)(2,1)S(1)}, u32[]{:S(2)}, u32[]{:S(2)}) %collective-permute-start.9) | collective-permute-done | bytes 196640 | tf_op jit(solution)/shard_map/ppermute | solution.py:36
  63.5 4.3 %collective-permute-done.13.refs_3_ = bf16[2,96,2304]{2,1,0:T(8,128)(2,1)S(1)} collective-permute-done((bf16[2,96,2304]{2,1,0:T(8,128)(2,1)S(1)}, bf16[2,96,2304]{2,1,0:T(8,128)(2,1)S(1)}, u32[]{:S(2)}, u32[]{:S(2)}) %collective-permute-start.13) | collective-permute-done | bytes 884768 | tf_op jit(solution)/shard_map/ppermute | solution.py:51
  68.7 2.2 %shard_map.299 = (bf16[192,512]{1,0:T(8,128)(2,1)}, f32[192,512]{1,0:T(8,128)}, f32[8,512]{1,0:T(8,128)}) custom-call(s32[2]{0:T(128)} %pad_add_fusion.place, bf16[512,192]{1,0:T(8,128)(2,1)} %get-tuple-element.95.query, bf16[512,384]{1,0:T(8,128)(2,1)} %copy-done.43, bf16[512,384]{1,0:T(8,128)(2,1)} %copy-done.44, f32[8,512]{1,0:T(8,128)} %get-tuple-element.97.top_in, ...), custom_call_target="tpu_custom_call" | custom-call | flops 30000001024 | tf_op jit(solution)/shard_map/pallas_call | solution.py:363
  71.0 1.7 collective-permute-start.14
  73.4 2.9 %collective-permute-start.16 = (bf16[192,512]{1,0:T(8,128)(2,1)}, bf16[192,512]{1,0:T(8,128)(2,1)S(1)}, u32[]{:S(2)}, u32[]{:S(2)}) collective-permute-start(bf16[192,512]{1,0:T(8,128)(2,1)} %get-tuple-element.105.m0), channel_id=1, source_target_pairs={{0,3},{1,0},{2,1},{3,2},{4,7},{5,4},{6,5},{7,6},{8,11},{9,8},{10,9... | collective-permute-start | bytes 589832 | tf_op jit(solution)/shard_map/ppermute | solution.py:36
  76.3 1.2 copy-done.40
  77.6 4.1 %shard_map.300 = (bf16[8,96,768]{2,1,0:T(8,128)(2,1)}, bf16[8,96,768]{2,1,0:T(8,128)(2,1)}, bf16[8,96,768]{2,1,0:T(8,128)(2,1)}) custom-call(s32[1]{0:T(128)} %bitcast.3.refs_0_.index, bf16[96,2304]{1,0:T(8,128)(2,1)} %copy-done.2, bf16[96,2304]{1,0:T(8,128)(2,1)} %copy-done.4, bf16[2,96,2304]{2,1,0:T(8,128)(2,1)} %copy-done.8, bf16[4,96,2304]{2,1,0:T(8,128)(2,1)} %copy-done.40), custom_call_target="tpu_custom_call" | custom-call | flops 30000001024 | tf_op jit(solution)/shard_map/pallas_call | solution.py:363
  81.7 7.2 %collective-permute-done.15.m2 = bf16[192,512]{1,0:T(8,128)(2,1)S(1)} collective-permute-done((bf16[192,512]{1,0:T(8,128)(2,1)}, bf16[192,512]{1,0:T(8,128)(2,1)S(1)}, u32[]{:S(2)}, u32[]{:S(2)}) %collective-permute-start.15) | collective-permute-done | bytes 196640 | tf_op jit(solution)/shard_map/ppermute | solution.py:36
  89.6 7.5 %shard_map.301 = (f32[128,768]{1,0:T(8,128)}, bf16[512,768]{1,0:T(8,128)(2,1)}, bf16[768,128]{1,0:T(8,128)(2,1)}, bf16[512,768]{1,0:T(8,128)(2,1)}, bf16[512,768...) custom-call(s32[2]{0:T(128)} %pad_add_fusion.place, ...), custom_call_target="tpu_custom_call" | custom-call | flops 30000001024 | tf_op jit(solution)/shard_map/pallas_call | solution.py:363
  97.1 5.7 %collective-permute-start.18 = (bf16[128,768]{1,0:T(8,128)(2,1)}, bf16[128,768]{1,0:T(8,128)(2,1)S(1)}, u32[]{:S(2)}, u32[]{:S(2)}) collective-permute-start(bf16[128,768]{1,0:T(8,128)(2,1)} %get-tuple-element.116), channel_id=1, source_target_pairs={{0,3},{1,0},{2,1},{3,2},{4,7},{5,4},{6,5},{7,6},{8,11},{9,8},{10,9... | collective-permute-start | bytes 589832 | tf_op jit(solution)/shard_map/ppermute | solution.py:36
  103.4 3.7 %shard_map.302 = (f32[1,768]{1,0:T(1,128)}, f32[1,768]{1,0:T(1,128)}, f32[128,768]{1,0:T(8,128)}, bf16[128,768]{1,0:T(8,128)(2,1)}, bf16[128,768]{1,0:T(8,128)(2,1)}, /*index=5*/bf16[128,768]{1,0:T(8,128)(2,1)}) custom-call(s32[2]{0:T(128)} %pad_add_fusion.place, bf16[512,768]{1,0:T(8,128)(2,1)} %get-tuple-element.111.active.refs_7_, ...), custom_call_target="tpu_custom_call" | custom-call | flops 30000001024 | tf_op jit(solution)/shard_map/pallas_call | solution.py:363
  107.0 1.4 collective-permute-done.18.r1
  108.4 12.4 %collective-permute-done.19.r2 = bf16[128,768]{1,0:T(8,128)(2,1)S(1)} collective-permute-done((bf16[128,768]{1,0:T(8,128)(2,1)}, bf16[128,768]{1,0:T(8,128)(2,1)S(1)}, u32[]{:S(2)}, u32[]{:S(2)}) %collective-permute-start.19) | collective-permute-done | bytes 196640 | tf_op jit(solution)/shard_map/ppermute | solution.py:36
  121.6 3.2 %shard_map.303 = (f32[128,768]{1,0:T(8,128)}, bf16[128,768]{1,0:T(8,128)(2,1)}, bf16[192,128]{1,0:T(8,128)(2,1)}, bf16[192,128]{1,0:T(8,128)(2,1)}, bf16[192,128]{1,0:T(8,128)(2,1)}, /*index=5*/bf16[192,128]{1,0:T(8,128)(2,1)}) custom-call(s32[2]{0:T(128)} %pad_add_fusion.place, f32[128,768]{1,0:T(8,128)} %get-tuple-element.115.part_own, ...), custom_call_target="tpu_custom_call" | custom-call | flops 30000001024 | tf_op jit(solution)/shard_map/pallas_call | solution.py:363
  124.9 1.4 collective-permute-start.22
  126.2 2.9 %collective-permute-start.23 = (bf16[192,128]{1,0:T(8,128)(2,1)}, bf16[192,128]{1,0:T(8,128)(2,1)S(1)}, u32[]{:S(2)}, u32[]{:S(2)}) collective-permute-start(bf16[192,128]{1,0:T(8,128)(2,1)} %get-tuple-element.127), channel_id=1, source_target_pairs={{0,3},{1,0},{2,1},{3,2},{4,7},{5,4},{6,5},{7,6},{8,11},{9,8},{10,9... | collective-permute-start | bytes 147464 | tf_op jit(solution)/shard_map/ppermute | solution.py:36
  129.1 6.2 %shard_map.304 = (bf16[4,96,2304]{2,1,0:T(8,128)(2,1)}, f32[4,96,2304]{2,1,0:T(8,128)}) custom-call(s32[1]{0:T(128)} %bitcast.3.refs_0_.index, bf16[512,768]{1,0:T(8,128)(2,1)} %get-tuple-element.121.refs_1_, bf16[512,768]{1,0:T(8,128)(2,1)} %get-tuple-element.112.hidden_back.refs_2_, bf16[128,768]{1,0:T(8,128)(2,1)} %refs_3_.1, ...), custom_call_target="tpu_custom_call" | custom-call | flops 30000001024 | tf_op jit(solution)/shard_map/pallas_call | solution.py:363
  135.9 2.4 %shard_map.305 = (bf16[512,384]{1,0:T(8,128)(2,1)}, f32[192,512]{1,0:T(8,128)}) custom-call(s32[2]{0:T(128)} %pad_add_fusion.place, bf16[512,192]{1,0:T(8,128)(2,1)} %get-tuple-element.95.query, bf16[192,128]{1,0:T(8,128)(2,1)} %get-tuple-element.119.g0, bf16[192,128]{1,0:T(8,128)(2,1)} %copy-done.55, bf16[192,128]{1,0:T(8,128)(2,1)} %copy-done.56, ...), custom_call_target="tpu_custom_call" | custom-call | flops 30000001024 | tf_op jit(solution)/shard_map/pallas_call | solution.py:363
  141.0 2.9 %shard_map.306 = (bf16[512,384]{1,0:T(8,128)(2,1)}, f32[192,512]{1,0:T(8,128)}) custom-call(s32[2]{0:T(128)} %pad_add_fusion.place, bf16[512,192]{1,0:T(8,128)(2,1)} %get-tuple-element.95.query, bf16[192,128]{1,0:T(8,128)(2,1)} %get-tuple-element.119.g0, bf16[192,128]{1,0:T(8,128)(2,1)} %copy-done.55, bf16[192,128]{1,0:T(8,128)(2,1)} %copy-done.56, ...), custom_call_target="tpu_custom_call" | custom-call | flops 30000001024 | tf_op jit(solution)/shard_map/pallas_call | solution.py:363
  143.9 8.8 %collective-permute-start.27 = (bf16[512,384]{1,0:T(8,128)(2,1)}, bf16[512,384]{1,0:T(8,128)(2,1)}, u32[]{:S(2)}, u32[]{:S(2)}) collective-permute-start(bf16[512,384]{1,0:T(8,128)(2,1)} %get-tuple-element.138), channel_id=1, source_target_pairs={{0,8},{4,12},{8,0},{12,4},{1,9},{5,13},{9,1},{13,5},{2,10},{6,14},... | collective-permute-start | bytes 1179656 | tf_op jit(solution)/shard_map/ppermute | solution.py:45
  152.7 1.3 copy-done.5
  153.9 1.8 convert_add_fusion
  156.8 4.8 %shard_map.307 = (bf16[512,384]{1,0:T(8,128)(2,1)}, bf16[512,384]{1,0:T(8,128)(2,1)}, bf16[512,192]{1,0:T(8,128)(2,1)}) custom-call(s32[2]{0:T(128)} %pad_add_fusion.place, bf16[512,192]{1,0:T(8,128)(2,1)} %get-tuple-element.95.query, bf16[192,128]{1,0:T(8,128)(2,1)} %get-tuple-element.119.g0, bf16[192,128]{1,0:T(8,128)(2,1)} %copy-done.55, ...), custom_call_target="tpu_custom_call" | custom-call | flops 30000001024 | tf_op jit(solution)/shard_map/pallas_call | solution.py:363
  161.6 2.2 collective-permute-start.26
  167.7 1.5 collective-permute-start.29
  169.2 5.1 %shard_map.308 = (f32[128,768]{1,0:T(8,128)}, bf16[256,768]{1,0:T(8,128)(2,1)}, bf16[256,768]{1,0:T(8,128)(2,1)}, bf16[256,768]{1,0:T(8,128)(2,1)}, bf16[4,112,6...) custom-call(s32[1]{0:T(128)} %bitcast.3.refs_0_.index, bf16[512,384]{1,0:T(8,128)(2,1)} %get-tuple-element.136.refs_0_, ...), custom_call_target="tpu_custom_call" | custom-call | flops 30000001024 | tf_op jit(solution)/shard_map/pallas_call | solution.py:363
  174.9 1.5 collective-permute-start.34
  176.4 1.9 collective-permute-start.35
  178.4 2.6 %collective-permute-done.29 = bf16[2,96,2304]{2,1,0:T(8,128)(2,1)S(1)} collective-permute-done((bf16[2,96,2304]{2,1,0:T(8,128)(2,1)}, bf16[2,96,2304]{2,1,0:T(8,128)(2,1)S(1)}, u32[]{:S(2)}, u32[]{:S(2)}) %collective-permute-start.29) | collective-permute-done | bytes 884768 | tf_op jit(solution)/shard_map/ppermute | solution.py:51
  181.2 1.6 collective-permute-start.32
  183.2 7.9 %collective-permute-done.32 = bf16[2,112,640]{2,1,0:T(8,128)(2,1)S(1)} collective-permute-done((bf16[2,112,640]{2,1,0:T(8,128)(2,1)S(1)}, bf16[2,112,640]{2,1,0:T(8,128)(2,1)S(1)}, u32[]{:S(2)}, u32[]{:S(2)}) %collective-permute-start.32) | collective-permute-done | bytes 286752 | tf_op jit(solution)/shard_map/ppermute | solution.py:51
  191.8 4.6 %collective-permute-done.33 = bf16[112,640]{1,0:T(8,128)(2,1)S(1)} collective-permute-done((bf16[112,640]{1,0:T(8,128)(2,1)S(1)}, bf16[112,640]{1,0:T(8,128)(2,1)S(1)}, u32[]{:S(2)}, u32[]{:S(2)}) %collective-permute-start.33) | collective-permute-done | bytes 143392 | tf_op jit(solution)/shard_map/ppermute | solution.py:51
  198.2 2.0 collective-permute-start.37
  202.2 12.1 %collective-permute-done.34 = bf16[256,768]{1,0:T(8,128)(2,1)} collective-permute-done((bf16[256,768]{1,0:T(8,128)(2,1)}, bf16[256,768]{1,0:T(8,128)(2,1)}, u32[]{:S(2)}, u32[]{:S(2)}) %collective-permute-start.34) | collective-permute-done | bytes 393248 | tf_op jit(solution)/shard_map/ppermute | solution.py:36
  215.1 2.4 %fusion.29 = (f32[128]{0:T(128)S(1)}, f32[128]{0:T(128)S(1)}, f32[128,768]{1,0:T(8,128)S(1)}, bf16[128,768]{1,0:T(8,128)(2,1)}) fusion(f32[128]{0:T(128)S(1)} %copy-done.30, f32[128]{0:T(128)S(1)} %broadcast_multiply_fusion.2, bf16[128,768]{1,0:T(8,128)(2,1)S(1)} %copy-done.1, f32[768]{0:T(1024)S(1)} %mul.143, bf16[256,768]{1,0:T(8,128)(2,1)} %collective-permute-done.35, ...), kind=kLoop, calls=%fused_computation.100 | loop fusion | flops 2162432 | bytes 3153920 | tf_op jit(solution)/shard_map/reduce_sum | solution.py:383
  (263 shorter events, 39.4 us)
Async XLA Ops:
  1.5 30.6 %copy-start.9 = (bf16[96,768]{1,0:T(8,128)(2,1)S(1)}, bf16[96,768]{1,0:T(8,128)(2,1)}, u32[]{:S(2)}) copy-start(bf16[96,768]{1,0:T(8,128)(2,1)} %param.22) | copy-start | bytes 442372
  1.6 30.6 %copy-start.23 = (bf16[768,96]{0,1:T(8,128)(2,1)S(1)}, bf16[768,96]{0,1:T(8,128)(2,1)}, u32[]{:S(2)}) copy-start(bf16[768,96]{0,1:T(8,128)(2,1)} %param.23) | copy-start | bytes 442372
  2.6 11.1 %collective-permute-start = (bf16[160,768]{1,0:T(8,128)(2,1)S(1)}, bf16[160,768]{1,0:T(8,128)(2,1)S(1)}, u32[]{:S(2)}, u32[]{:S(2)}) collective-permute-start(bf16[160,768]{1,0:T(8,128)(2,1)S(1)} %pad_maximum_fusion.4), channel_id=1, source_target_pairs={{0,1},{1,2},{2,3},{3,0},{4,5},{5,6},{6,7},{7,4},{8,9},{9,10},{10,1... | collective-permute-start | bytes 737288 | tf_op jit(solution)/shard_map/ppermute | solution.py:36
  13.7 8.7 %collective-permute-start.2 = (bf16[160,768]{1,0:T(8,128)(2,1)S(1)}, bf16[160,768]{1,0:T(8,128)(2,1)S(1)}, u32[]{:S(2)}, u32[]{:S(2)}) collective-permute-start(bf16[160,768]{1,0:T(8,128)(2,1)S(1)} %pad_maximum_fusion.4), channel_id=1, source_target_pairs={{0,3},{1,0},{2,1},{3,2},{4,7},{5,4},{6,5},{7,6},{8,11},{9,8},{10,9... | collective-permute-start | bytes 737288 | tf_op jit(solution)/shard_map/ppermute | solution.py:36
  17.2 5.2 %collective-permute-start.3 = (bf16[112,576]{1,0:T(8,128)(2,1)S(1)}, bf16[112,576]{1,0:T(8,128)(2,1)S(1)}, u32[]{:S(2)}, u32[]{:S(2)}) collective-permute-start(bf16[112,576]{1,0:T(8,128)(2,1)S(1)} %fusion.18.refs_1_), channel_id=1, source_target_pairs={{0,16},{4,12},{8,24},{12,4},{16,0},{20,28},{24,8},{28,20},{1,17},{... | collective-permute-start | bytes 387080 | tf_op jit(solution)/shard_map/ppermute | solution.py:51
  18.8 12.4 %collective-permute-start.1 = (bf16[160,768]{1,0:T(8,128)(2,1)S(1)}, bf16[160,768]{1,0:T(8,128)(2,1)S(1)}, u32[]{:S(2)}, u32[]{:S(2)}) collective-permute-start(bf16[160,768]{1,0:T(8,128)(2,1)S(1)} %pad_maximum_fusion.4), channel_id=1, source_target_pairs={{0,2},{1,3},{2,0},{3,1},{4,6},{5,7},{6,4},{7,5},{8,10},{9,11},{10,... | collective-permute-start | bytes 737288 | tf_op jit(solution)/shard_map/ppermute | solution.py:36
  22.4 9.4 %collective-permute-start.4 = (bf16[2,112,576]{2,1,0:T(8,128)(2,1)S(1)}, bf16[2,112,576]{2,1,0:T(8,128)(2,1)S(1)}, u32[]{:S(2)}, u32[]{:S(2)}) collective-permute-start(bf16[2,112,576]{2,1,0:T(8,128)(2,1)S(1)} %pad_maximum_fusion.3), channel_id=1, source_target_pairs={{0,8},{4,20},{8,0},{12,28},{16,24},{20,4},{24,16},{28,12},{1,9},{5... | collective-permute-start | bytes 774152 | tf_op jit(solution)/shard_map/ppermute | solution.py:51
  31.1 8.8 %collective-permute-start.6 = (bf16[128,768]{1,0:T(8,128)(2,1)}, bf16[128,768]{1,0:T(8,128)(2,1)S(1)}, u32[]{:S(2)}, u32[]{:S(2)}) collective-permute-start(bf16[128,768]{1,0:T(8,128)(2,1)} %refs_3_.1), channel_id=1, source_target_pairs={{0,1},{1,2},{2,3},{3,0},{4,5},{5,6},{6,7},{7,4},{8,9},{9,10},{10,1... | collective-permute-start | bytes 589832 | tf_op jit(solution)/shard_map/ppermute | solution.py:36
  31.9 2.2 collective-permute-start.5
  32.3 35.5 %copy-start.2 = (bf16[96,2304]{1,0:T(8,128)(2,1)}, bf16[96,2304]{1,0:T(8,128)(2,1)S(1)}, u32[]{:S(2)}) copy-start(bf16[96,2304]{1,0:T(8,128)(2,1)S(1)} %concatenate.64.refs_1_) | copy-start | bytes 1327108
  32.3 14.7 %collective-permute-start.12 = (bf16[96,2304]{1,0:T(8,128)(2,1)S(1)}, bf16[96,2304]{1,0:T(8,128)(2,1)S(1)}, u32[]{:S(2)}, u32[]{:S(2)}) collective-permute-start(bf16[96,2304]{1,0:T(8,128)(2,1)S(1)} %concatenate.64.refs_1_), channel_id=1, source_target_pairs={{0,16},{4,12},{8,24},{12,4},{16,0},{20,28},{24,8},{28,20},{1,17},{... | collective-permute-start | bytes 1327112 | tf_op jit(solution)/shard_map/ppermute | solution.py:51
  44.5 4.8 %collective-permute-start.8 = (bf16[512,384]{1,0:T(8,128)(2,1)}, bf16[512,384]{1,0:T(8,128)(2,1)S(1)}, u32[]{:S(2)}, u32[]{:S(2)}) collective-permute-start(bf16[512,384]{1,0:T(8,128)(2,1)} %get-tuple-element.96.kv_own), channel_id=1, source_target_pairs={{0,4},{4,0},{8,12},{12,8},{1,5},{5,1},{9,13},{13,9},{2,6},{6,2},{1... | collective-permute-start | bytes 1179656 | tf_op jit(solution)/shard_map/ppermute | solution.py:45
  44.6 9.1 %collective-permute-start.10 = (bf16[128,768]{1,0:T(8,128)(2,1)}, bf16[128,768]{1,0:T(8,128)(2,1)S(1)}, u32[]{:S(2)}, u32[]{:S(2)}) collective-permute-start(bf16[128,768]{1,0:T(8,128)(2,1)} %refs_3_.1), channel_id=1, source_target_pairs={{0,3},{1,0},{2,1},{3,2},{4,7},{5,4},{6,5},{7,6},{8,11},{9,8},{10,9... | collective-permute-start | bytes 589832 | tf_op jit(solution)/shard_map/ppermute | solution.py:36
  46.8 14.3 %collective-permute-start.9 = (bf16[128,768]{1,0:T(8,128)(2,1)}, bf16[128,768]{1,0:T(8,128)(2,1)S(1)}, u32[]{:S(2)}, u32[]{:S(2)}) collective-permute-start(bf16[128,768]{1,0:T(8,128)(2,1)} %refs_3_.1), channel_id=1, source_target_pairs={{0,2},{1,3},{2,0},{3,1},{4,6},{5,7},{6,4},{7,5},{8,10},{9,11},{10,... | collective-permute-start | bytes 589832 | tf_op jit(solution)/shard_map/ppermute | solution.py:36
  47.1 20.7 %copy-start.4 = (bf16[96,2304]{1,0:T(8,128)(2,1)}, bf16[96,2304]{1,0:T(8,128)(2,1)S(1)}, u32[]{:S(2)}) copy-start(bf16[96,2304]{1,0:T(8,128)(2,1)S(1)} %collective-permute-done.12.refs_2_) | copy-start | bytes 1327108
  47.2 14.0 %collective-permute-start.7 = (bf16[512,384]{1,0:T(8,128)(2,1)S(1)}, bf16[512,384]{1,0:T(8,128)(2,1)S(1)}, u32[]{:S(2)}, u32[]{:S(2)}) collective-permute-start(bf16[512,384]{1,0:T(8,128)(2,1)S(1)} %copy-done.41), channel_id=1, source_target_pairs={{0,8},{4,12},{8,0},{12,4},{1,9},{5,13},{9,1},{13,5},{2,10},{6,14},... | collective-permute-start | bytes 1179656 | tf_op jit(solution)/shard_map/ppermute | solution.py:45
  48.7 19.1 %collective-permute-start.13 = (bf16[2,96,2304]{2,1,0:T(8,128)(2,1)S(1)}, bf16[2,96,2304]{2,1,0:T(8,128)(2,1)S(1)}, u32[]{:S(2)}, u32[]{:S(2)}) collective-permute-start(bf16[2,96,2304]{2,1,0:T(8,128)(2,1)S(1)} %pad_maximum_fusion.1), channel_id=1, source_target_pairs={{0,8},{4,20},{8,0},{12,28},{16,24},{20,4},{24,16},{28,12},{1,9},{5... | collective-permute-start | bytes 2654216 | tf_op jit(solution)/shard_map/ppermute | solution.py:51
  61.8 1.7 collective-permute-start.11
  68.7 7.6 %collective-permute-start.17 = (bf16[4,96,2304]{2,1,0:T(8,128)(2,1)S(1)}, bf16[4,96,2304]{2,1,0:T(8,128)(2,1)S(1)}, u32[]{:S(2)}, u32[]{:S(2)}) collective-permute-start(bf16[4,96,2304]{2,1,0:T(8,128)(2,1)S(1)} %pad_maximum_fusion), channel_id=1, source_target_pairs={{0,4},{4,0},{8,12},{12,8},{16,20},{20,16},{24,28},{28,24},{1,5},{5... | collective-permute-start | bytes 5308424 | tf_op jit(solution)/shard_map/ppermute | solution.py:51
  71.0 10.7 %collective-permute-start.14 = (bf16[192,512]{1,0:T(8,128)(2,1)}, bf16[192,512]{1,0:T(8,128)(2,1)S(1)}, u32[]{:S(2)}, u32[]{:S(2)}) collective-permute-start(bf16[192,512]{1,0:T(8,128)(2,1)} %get-tuple-element.105.m0), channel_id=1, source_target_pairs={{0,1},{1,2},{2,3},{3,0},{4,5},{5,6},{6,7},{7,4},{8,9},{9,10},{10,1... | collective-permute-start | bytes 589832 | tf_op jit(solution)/shard_map/ppermute | solution.py:36
  72.7 16.1 %collective-permute-start.15 = (bf16[192,512]{1,0:T(8,128)(2,1)}, bf16[192,512]{1,0:T(8,128)(2,1)S(1)}, u32[]{:S(2)}, u32[]{:S(2)}) collective-permute-start(bf16[192,512]{1,0:T(8,128)(2,1)} %get-tuple-element.105.m0), channel_id=1, source_target_pairs={{0,2},{1,3},{2,0},{3,1},{4,6},{5,7},{6,4},{7,5},{8,10},{9,11},{10,... | collective-permute-start | bytes 589832 | tf_op jit(solution)/shard_map/ppermute | solution.py:36
  73.4 15.4 %collective-permute-start.16 = (bf16[192,512]{1,0:T(8,128)(2,1)}, bf16[192,512]{1,0:T(8,128)(2,1)S(1)}, u32[]{:S(2)}, u32[]{:S(2)}) collective-permute-start(bf16[192,512]{1,0:T(8,128)(2,1)} %get-tuple-element.105.m0), channel_id=1, source_target_pairs={{0,3},{1,0},{2,1},{3,2},{4,7},{5,4},{6,5},{7,6},{8,11},{9,8},{10,9... | collective-permute-start | bytes 589832 | tf_op jit(solution)/shard_map/ppermute | solution.py:36
  97.1 11.3 %collective-permute-start.18 = (bf16[128,768]{1,0:T(8,128)(2,1)}, bf16[128,768]{1,0:T(8,128)(2,1)S(1)}, u32[]{:S(2)}, u32[]{:S(2)}) collective-permute-start(bf16[128,768]{1,0:T(8,128)(2,1)} %get-tuple-element.116), channel_id=1, source_target_pairs={{0,3},{1,0},{2,1},{3,2},{4,7},{5,4},{6,5},{7,6},{8,11},{9,8},{10,9... | collective-permute-start | bytes 589832 | tf_op jit(solution)/shard_map/ppermute | solution.py:36
  102.7 18.1 %collective-permute-start.19 = (bf16[128,768]{1,0:T(8,128)(2,1)}, bf16[128,768]{1,0:T(8,128)(2,1)S(1)}, u32[]{:S(2)}, u32[]{:S(2)}) collective-permute-start(bf16[128,768]{1,0:T(8,128)(2,1)} %get-tuple-element.117), channel_id=1, source_target_pairs={{0,2},{1,3},{2,0},{3,1},{4,6},{5,7},{6,4},{7,5},{8,10},{9,11},{10,... | collective-permute-start | bytes 589832 | tf_op jit(solution)/shard_map/ppermute | solution.py:36
  103.2 17.7 %collective-permute-start.20 = (bf16[128,768]{1,0:T(8,128)(2,1)}, bf16[128,768]{1,0:T(8,128)(2,1)S(1)}, u32[]{:S(2)}, u32[]{:S(2)}) collective-permute-start(bf16[128,768]{1,0:T(8,128)(2,1)} %get-tuple-element.118), channel_id=1, source_target_pairs={{0,1},{1,2},{2,3},{3,0},{4,5},{5,6},{6,7},{7,4},{8,9},{9,10},{10,1... | collective-permute-start | bytes 589832 | tf_op jit(solution)/shard_map/ppermute | solution.py:36
  124.9 10.4 %collective-permute-start.21 = (bf16[192,128]{1,0:T(8,128)(2,1)}, bf16[192,128]{1,0:T(8,128)(2,1)S(1)}, u32[]{:S(2)}, u32[]{:S(2)}) collective-permute-start(bf16[192,128]{1,0:T(8,128)(2,1)} %get-tuple-element.120), channel_id=1, source_target_pairs={{0,1},{1,2},{2,3},{3,0},{4,5},{5,6},{6,7},{7,4},{8,9},{9,10},{10,1... | collective-permute-start | bytes 147464 | tf_op jit(solution)/shard_map/ppermute | solution.py:36
  124.9 10.4 %collective-permute-start.22 = (bf16[192,128]{1,0:T(8,128)(2,1)}, bf16[192,128]{1,0:T(8,128)(2,1)S(1)}, u32[]{:S(2)}, u32[]{:S(2)}) collective-permute-start(bf16[192,128]{1,0:T(8,128)(2,1)} %get-tuple-element.126), channel_id=1, source_target_pairs={{0,2},{1,3},{2,0},{3,1},{4,6},{5,7},{6,4},{7,5},{8,10},{9,11},{10,... | collective-permute-start | bytes 147464 | tf_op jit(solution)/shard_map/ppermute | solution.py:36
  126.2 9.1 %collective-permute-start.23 = (bf16[192,128]{1,0:T(8,128)(2,1)}, bf16[192,128]{1,0:T(8,128)(2,1)S(1)}, u32[]{:S(2)}, u32[]{:S(2)}) collective-permute-start(bf16[192,128]{1,0:T(8,128)(2,1)} %get-tuple-element.127), channel_id=1, source_target_pairs={{0,3},{1,0},{2,1},{3,2},{4,7},{5,4},{6,5},{7,6},{8,11},{9,8},{10,9... | collective-permute-start | bytes 147464 | tf_op jit(solution)/shard_map/ppermute | solution.py:36
  138.3 1.9 collective-permute-start.25
  138.5 14.2 %collective-permute-start.24 = (bf16[4,96,2304]{2,1,0:T(8,128)(2,1)S(1)}, bf16[4,96,2304]{2,1,0:T(8,128)(2,1)S(1)}, u32[]{:S(2)}, u32[]{:S(2)}) collective-permute-start(bf16[4,96,2304]{2,1,0:T(8,128)(2,1)S(1)} %copy-done.39), channel_id=1, source_target_pairs={{0,4},{4,0},{8,12},{12,8},{16,20},{20,16},{24,28},{28,24},{1,5},{5... | collective-permute-start | bytes 5308424 | tf_op jit(solution)/shard_map/ppermute | solution.py:51
  143.9 25.3 %collective-permute-start.27 = (bf16[512,384]{1,0:T(8,128)(2,1)}, bf16[512,384]{1,0:T(8,128)(2,1)}, u32[]{:S(2)}, u32[]{:S(2)}) collective-permute-start(bf16[512,384]{1,0:T(8,128)(2,1)} %get-tuple-element.138), channel_id=1, source_target_pairs={{0,8},{4,12},{8,0},{12,4},{1,9},{5,13},{9,1},{13,5},{2,10},{6,14},... | collective-permute-start | bytes 1179656 | tf_op jit(solution)/shard_map/ppermute | solution.py:45
  161.6 7.6 %collective-permute-start.26 = (bf16[512,384]{1,0:T(8,128)(2,1)}, bf16[512,384]{1,0:T(8,128)(2,1)}, u32[]{:S(2)}, u32[]{:S(2)}) collective-permute-start(bf16[512,384]{1,0:T(8,128)(2,1)} %get-tuple-element.137), channel_id=1, source_target_pairs={{0,4},{4,0},{8,12},{12,8},{1,5},{5,1},{9,13},{13,9},{2,6},{6,2},{1... | collective-permute-start | bytes 1179656 | tf_op jit(solution)/shard_map/ppermute | solution.py:45
  167.7 13.3 %collective-permute-start.29 = (bf16[2,96,2304]{2,1,0:T(8,128)(2,1)}, bf16[2,96,2304]{2,1,0:T(8,128)(2,1)S(1)}, u32[]{:S(2)}, u32[]{:S(2)}) collective-permute-start(bf16[2,96,2304]{2,1,0:T(8,128)(2,1)} %slice.459), channel_id=1, source_target_pairs={{0,16},{4,12},{8,24},{12,4},{16,0},{20,28},{24,8},{28,20},{1,17},{... | collective-permute-start | bytes 2654216 | tf_op jit(solution)/shard_map/ppermute | solution.py:51
  174.3 6.7 %collective-permute-start.31 = (bf16[4,112,640]{2,1,0:T(8,128)(2,1)}, bf16[4,112,640]{2,1,0:T(8,128)(2,1)S(1)}, u32[]{:S(2)}, u32[]{:S(2)}) collective-permute-start(bf16[4,112,640]{2,1,0:T(8,128)(2,1)} %get-tuple-element.147), channel_id=1, source_target_pairs={{0,4},{4,0},{8,12},{12,8},{16,20},{20,16},{24,28},{28,24},{1,5},{5... | collective-permute-start | bytes 1720328 | tf_op jit(solution)/shard_map/ppermute | solution.py:51
  174.3 26.8 %collective-permute-start.28 = (bf16[256,768]{1,0:T(8,128)(2,1)}, bf16[256,768]{1,0:T(8,128)(2,1)}, u32[]{:S(2)}, u32[]{:S(2)}) collective-permute-start(bf16[256,768]{1,0:T(8,128)(2,1)} %get-tuple-element.146), channel_id=1, source_target_pairs={{0,3},{1,0},{2,1},{3,2},{4,7},{5,4},{6,5},{7,6},{8,11},{9,8},{10,9... | collective-permute-start | bytes 1179656 | tf_op jit(solution)/shard_map/ppermute | solution.py:36
  174.9 39.5 %collective-permute-start.34 = (bf16[256,768]{1,0:T(8,128)(2,1)}, bf16[256,768]{1,0:T(8,128)(2,1)}, u32[]{:S(2)}, u32[]{:S(2)}) collective-permute-start(bf16[256,768]{1,0:T(8,128)(2,1)} %get-tuple-element.151), channel_id=1, source_target_pairs={{0,2},{1,3},{2,0},{3,1},{4,6},{5,7},{6,4},{7,5},{8,10},{9,11},{10,... | collective-permute-start | bytes 1179656 | tf_op jit(solution)/shard_map/ppermute | solution.py:36
  176.4 38.7 %collective-permute-start.35 = (bf16[256,768]{1,0:T(8,128)(2,1)}, bf16[256,768]{1,0:T(8,128)(2,1)}, u32[]{:S(2)}, u32[]{:S(2)}) collective-permute-start(bf16[256,768]{1,0:T(8,128)(2,1)} %get-tuple-element.153), channel_id=1, source_target_pairs={{0,1},{1,2},{2,3},{3,0},{4,5},{5,6},{6,7},{7,4},{8,9},{9,10},{10,1... | collective-permute-start | bytes 1179656 | tf_op jit(solution)/shard_map/ppermute | solution.py:36
  181.2 9.8 %collective-permute-start.32 = (bf16[2,112,640]{2,1,0:T(8,128)(2,1)S(1)}, bf16[2,112,640]{2,1,0:T(8,128)(2,1)S(1)}, u32[]{:S(2)}, u32[]{:S(2)}) collective-permute-start(bf16[2,112,640]{2,1,0:T(8,128)(2,1)S(1)} %slice.460), channel_id=1, source_target_pairs={{0,16},{4,12},{8,24},{12,4},{16,0},{20,28},{24,8},{28,20},{1,17},{... | collective-permute-start | bytes 860168 | tf_op jit(solution)/shard_map/ppermute | solution.py:51
  182.9 8.7 %collective-permute-start.30 = (bf16[96,2304]{1,0:T(8,128)(2,1)S(1)}, bf16[96,2304]{1,0:T(8,128)(2,1)S(1)}, u32[]{:S(2)}, u32[]{:S(2)}) collective-permute-start(bf16[96,2304]{1,0:T(8,128)(2,1)S(1)} %fusion.5), channel_id=1, source_target_pairs={{0,8},{4,20},{8,0},{12,28},{16,24},{20,4},{24,16},{28,12},{1,9},{5... | collective-permute-start | bytes 1327112 | tf_op jit(solution)/shard_map/ppermute | solution.py:51
  191.3 5.2 %collective-permute-start.33 = (bf16[112,640]{1,0:T(8,128)(2,1)S(1)}, bf16[112,640]{1,0:T(8,128)(2,1)S(1)}, u32[]{:S(2)}, u32[]{:S(2)}) collective-permute-start(bf16[112,640]{1,0:T(8,128)(2,1)S(1)} %fusion.19), channel_id=1, source_target_pairs={{0,8},{4,20},{8,0},{12,28},{16,24},{20,4},{24,16},{28,12},{1,9},{5... | collective-permute-start | bytes 430088 | tf_op jit(solution)/shard_map/ppermute | solution.py:51
  191.8 23.3 %copy-start.1 = (bf16[128,768]{1,0:T(8,128)(2,1)S(1)}, bf16[128,768]{1,0:T(8,128)(2,1)}, u32[]{:S(2)}) copy-start(bf16[128,768]{1,0:T(8,128)(2,1)} %t0.3) | copy-start | bytes 589828
  191.8 23.3 %copy-start.13 = (f32[128,768]{1,0:T(8,128)S(1)}, f32[128,768]{1,0:T(8,128)}, u32[]{:S(2)}) copy-start(f32[128,768]{1,0:T(8,128)} %get-tuple-element.110.middle) | copy-start | bytes 1179652
  191.8 23.3 %copy-start.14 = (f32[128,768]{1,0:T(8,128)S(1)}, f32[128,768]{1,0:T(8,128)}, u32[]{:S(2)}) copy-start(f32[128,768]{1,0:T(8,128)} %get-tuple-element.113) | copy-start | bytes 1179652
  191.8 23.3 %copy-start.15 = (f32[128,768]{1,0:T(8,128)S(1)}, f32[128,768]{1,0:T(8,128)}, u32[]{:S(2)}) copy-start(f32[128,768]{1,0:T(8,128)} %get-tuple-element.156) | copy-start | bytes 1179652
  191.8 23.3 %copy-start.30 = (f32[128]{0:T(128)S(1)}, f32[128]{0:T(128)}, u32[]{:S(2)}) copy-start(f32[128]{0:T(128)} %add_rsqrt_fusion) | copy-start | bytes 1540
  198.2 21.4 %collective-permute-start.37 = (bf16[112,192]{1,0:T(8,128)(2,1)S(1)}, bf16[112,192]{1,0:T(8,128)(2,1)S(1)}, u32[]{:S(2)}, u32[]{:S(2)}) collective-permute-start(bf16[112,192]{1,0:T(8,128)(2,1)S(1)} %get-tuple-element.222), channel_id=1, source_target_pairs={{0,2},{1,3},{2,0},{3,1},{4,6},{5,7},{6,4},{7,5},{8,10},{9,11},{10,... | collective-permute-start | bytes 129032 | tf_op jit(solution)/shard_map/ppermute | solution.py:36
  200.2 19.5 %collective-permute-start.36 = (bf16[112,192]{1,0:T(8,128)(2,1)S(1)}, bf16[112,192]{1,0:T(8,128)(2,1)S(1)}, u32[]{:S(2)}, u32[]{:S(2)}) collective-permute-start(bf16[112,192]{1,0:T(8,128)(2,1)S(1)} %get-tuple-element.223), channel_id=1, source_target_pairs={{0,3},{1,0},{2,1},{3,2},{4,7},{5,4},{6,5},{7,6},{8,11},{9,8},{10,9... | collective-permute-start | bytes 129032 | tf_op jit(solution)/shard_map/ppermute | solution.py:36
  201.1 18.7 %collective-permute-start.38 = (bf16[112,192]{1,0:T(8,128)(2,1)S(1)}, bf16[112,192]{1,0:T(8,128)(2,1)S(1)}, u32[]{:S(2)}, u32[]{:S(2)}) collective-permute-start(bf16[112,192]{1,0:T(8,128)(2,1)S(1)} %get-tuple-element.221), channel_id=1, source_target_pairs={{0,1},{1,2},{2,3},{3,0},{4,5},{5,6},{6,7},{7,4},{8,9},{9,10},{10,1... | collective-permute-start | bytes 129032 | tf_op jit(solution)/shard_map/ppermute | solution.py:36
  (49 other events, 290.0 us)

commit v2 on v1

--- a/solution.py
+++ b/solution.py
@@ -94,13 +94,13 @@
 
 
 def grads_kernel(pairs, spread, index, *refs):
-    ins, (sent, kept), (whole, extra) = refs[:-4], refs[-4:-2], refs[-2:]
+    ins, (sent, kept_low, kept_high), (whole, extra) = refs[:-5], refs[-5:-2], refs[-2:]
     at = 0
     for count, flipped, column, columns in pairs:
         left, right = stacked_slots(ins[at : at + count]), ins[at + count][...]
         at += count + 1
         whole[:, column : column + columns] = dot_plain(left.T, right.T if flipped else right)
-    rows = kept.shape[1]
+    rows = sent.shape[1]
     model, wide = whole.shape
     depth = model // 8
     if spread:
@@ -127,9 +127,10 @@
             sent[slot, depth:rows] = extra[block].astype(sent.dtype)
     for slot, flip in enumerate((0, far, near, 6)):
         block = me ^ flip
-        kept[slot, 0:depth] = whole[pl.ds(pl.multiple_of(block * depth, 8), depth)]
+        kept = (kept_low if slot < 2 else kept_high).at[slot % 2]
+        kept[0:depth] = whole[pl.ds(pl.multiple_of(block * depth, 8), depth)]
         if spread:
-            kept[slot, depth:rows] = extra[block]
+            kept[depth:rows] = extra[block]
 
 
 def grads_sent(pairs, columns, depth):
@@ -143,7 +144,7 @@
         lambda *refs: grads_kernel(plan, False, *refs),
         index,
         operands,
-        [((4, depth, columns), jnp.bfloat16), ((4, depth, columns), jnp.float32)],
+        [((4, depth, columns), jnp.bfloat16)] + [((2, depth, columns), jnp.float32)] * 2,
         [((8 * depth, columns), jnp.float32), ((8, VEC_ROWS, columns), jnp.float32)],
     )
 
@@ -504,7 +505,9 @@
         mixed_back_t[by][...] = turned[by * width : (by + 1) * width]
 
 
-def gather_back_kernel(place, own, core, far, query, weight, o1, o2, o3, dqkv, part_own, *parts):
+def gather_back_kernel(
+    place, own, core, far, query, weight, outside, dqkv, part_own, *parts
+):
     wide = own.shape[1]
     width = query.shape[1]
     total = own[...].astype(jnp.float32) + core[...].astype(jnp.float32)
@@ -516,19 +519,60 @@
     normed_back = dot_cols(dqkv[:, : wide + width], weight[...])
     slot = part_own.shape[0]
     part_own[...] = normed_back[:slot]
-    for by, outside in ((1, o1), (2, o2), (3, o3)):
+    for by in range(1, 4):
         parts[by - 1][:slot] = normed_back[by * slot : (by + 1) * slot].astype(jnp.bfloat16)
-        parts[by - 1][slot:] = outside[...]
+    parts[1][slot:] = outside[...]
 
 
 def last_kernel(index, *refs):
-    ins, (xhat, hidden_sum, seed_sum, branch) = refs[:8], refs[8:12]
-    part_own, p1, p2, p3, sent, kept, dqkv, whole, extra = refs[12:]
+    ins, (xhat, hidden_sum, seed_sum, branch) = refs[:6], refs[6:10]
+    part_own, p1, p2, p3, sent, kept_low, kept_high, dqkv, whole, extra = refs[10:]
     gather_back_kernel(index, *ins, dqkv, part_own, p1, p2, p3)
     plan = [(1, False, 0, dqkv.shape[1])]
     grads_kernel(
-        plan, True, index, xhat, dqkv, hidden_sum, seed_sum, branch, sent, kept, whole, extra
-    )
+        plan,
+        True,
+        index,
+        xhat,
+        dqkv,
+        hidden_sum,
+        seed_sum,
+        branch,
+        sent,
+        kept_low,
+        kept_high,
+        whole,
+        extra,
+    )
+
+
+def own_rows_kernel(
+    place,
+    normed_own,
+    n1,
+    n2,
+    n3,
+    outside_own,
+    o1,
+    o3,
+    tokens,
+    middle_back,
+    middle,
+    gain,
+    bias,
+    result,
+    input_grad,
+):
+    normed_back, outside = normed_own[...], outside_own[...]
+    slot = normed_back.shape[0]
+    for ref in (n1, n2, n3):
+        normed_back = normed_back + ref[:slot].astype(jnp.float32)
+    for ref in (o1, n2.at[slot:], o3):
+        outside = outside + ref[...].astype(jnp.float32)
+    xhat, rstd = normalized(tokens[...].astype(jnp.float32))
+    grad = middle_back[...] + norm_back(normed_back * gain[...], xhat, rstd)
+    input_grad[...] = grad.astype(jnp.bfloat16)
+    result[...] = (middle[...] + (outside + bias[...])).astype(jnp.bfloat16)
 
 
 def slots_returned(parts):
@@ -657,12 +701,14 @@
     kv_core = blk_swapped(kv_own, 1)
     stats = ((8, rows), f32)
     turned = ((width, rows), f32)
+    if paired():
+        rest_second = cube_swapped(jnp.stack([rest_own, rest_first]), 2, 4)
+        kv_core = after(kv_core, rest_second)
     top, total, mixed_t = on_core(
         forward_near_kernel, place, (query, kv_own, kv_core), (stats, stats, turned)
     )
     kv_both = blk_swapped(after(kv_y, top, *cotangent_slots[2:]), 1)
     if paired():
-        rest_second = cube_swapped(after(jnp.stack([rest_own, rest_first]), kv_own), 2, 4)
         rest_second = after(rest_second, kv_both)
         rest_held = jnp.concatenate([rest_own[None], rest_first[None], rest_second])
         rest_other = cube_swapped(rest_held, 1, 1)
@@ -725,18 +771,22 @@
     ]
     wide_columns = 2 * units + inner
     if paired():
-        wide_sent, wide_kept = grads_sent(wide_pairs, wide_columns, depth)
+        wide_sent, wide_low_part, wide_high_part = grads_sent(wide_pairs, wide_columns, depth)
         wide_got = cube_swapped(wide_sent, 1, 1)
         grad_slots[1] = after(grad_slots[1], wide_sent)
+    outside_returned = [
+        passed_along(after(outside_parts[by - 1], *mixed_back_t), -by) for by in (1, 3)
+    ]
+    grad_slots[1] = after(grad_slots[1], *outside_returned)
     sides = [query] + grad_slots + [mixed_t, lse]
     pair = ((rows, 2 * width), bf16)
     dkv_both, query_grad_t = on_core(
         backward_both_kernel, place, sides + [kv_both], (pair, turned)
     )
     if paired():
-        wide_held = wide_kept + after(wide_got, dkv_both).astype(f32)
-        wide_next = wide_held[2:].astype(bf16)
-        wide_got = cube_swapped(wide_next, 4, 2)
+        wide_got = after(wide_got, dkv_both)
+        wide_next = (wide_high_part + wide_got[2:].astype(f32)).astype(bf16)
+        wide_more = cube_swapped(wide_next, 4, 2)
     dkv_y, query_grad_t = on_core(
         backward_y_kernel,
         place,
@@ -755,13 +805,14 @@
     )
     dkv_core = blk_swapped(dkv_core, 1)
     columns = -(-wide // 128) * 128
-    back_operands = [dkv_own, dkv_core, dkv_from_y, query_grad, qkv_whole] + outside_parts
-    back_outs = [slab] + [((2 * part, model), bf16)] * 3
+    back_operands = [dkv_own, dkv_core, dkv_from_y, query_grad, qkv_whole, outside_parts[1]]
+    back_outs = [slab, slabs[0], ((2 * part, model), bf16), slabs[0]]
     sums = (hidden_sum, seed_sum, branch_back)
     dqkv_kind = ((rows, columns), bf16)
     if paired():
-        kinds = [((4, depth + VEC_ROWS, columns), kind) for kind in (bf16, f32)]
-        normed_own, *normed_parts, near_sent, near_kept = on_core(
+        kinds = [((4, depth + VEC_ROWS, columns), bf16)]
+        kinds += [((2, depth + VEC_ROWS, columns), f32)] * 2
+        normed_own, *normed_parts, near_sent, near_low, near_high = on_core(
             last_kernel,
             cube_index().astype(jnp.int32).reshape(1),
             back_operands + [xhat1_low] + list(sums),
@@ -775,17 +826,18 @@
     normed_returned = slots_returned(normed_parts)
 
     if paired():
-        near_got = cube_swapped(near_sent, 1, 1).astype(f32)
-        wide_held = wide_held[:2] + after(wide_got, near_sent).astype(f32)
-        wide_last = wide_held[1].astype(bf16)
-        near_held = near_kept + near_got
-        near_next = near_held[2:].astype(bf16)
-        near_got = cube_swapped(near_next, 4, 2).astype(f32)
-        near_held = near_held[:2] + near_got
-        near_got = cube_swapped(near_held[1].astype(bf16), 2, 4).astype(f32)
-        near_total = near_held[0] + near_got
-        wide_got = cube_swapped(wide_last, 2, 4).astype(f32)
-        wide_total = wide_held[0] + wide_got
+        near_got = cube_swapped(near_sent, 1, 1)
+        wide_more = after(wide_more, near_sent)
+        wide_last = wide_low_part[1] + wide_got[1].astype(f32) + wide_more[1].astype(f32)
+        wide_end = cube_swapped(wide_last.astype(bf16), 2, 4)
+        near_next = (near_high + near_got[2:].astype(f32)).astype(bf16)
+        near_more = cube_swapped(near_next, 4, 2)
+        near_last = near_low[1] + near_got[1].astype(f32) + near_more[1].astype(f32)
+        near_end = cube_swapped(near_last.astype(bf16), 2, 4)
+        near_total = near_low[0] + near_got[0].astype(f32) + near_more[0].astype(f32)
+        near_total = near_total + near_end.astype(f32)
+        wide_total = wide_low_part[0] + wide_got[0].astype(f32) + wide_more[0].astype(f32)
+        wide_total = wide_total + wide_end.astype(f32)
     else:
         near_total = grads_scattered([([xhat1_low], False, dqkv, 0)], columns, owners, sums)
         wide_total = grads_scattered(wide_pairs, wide_columns, owners, ())
@@ -840,15 +892,16 @@
         [qkv_weight_grad[:, width + 64 : 2 * width], qkv_weight_grad[:, width : width + 64]], axis=1
     )
 
-    normed_back = normed_own
-    for item in normed_returned:
-        normed_back = normed_back + after(item, *final_sent)[:part].astype(f32)
-    outside = outside_own
-    for item in normed_returned:
-        outside = outside + after(item, *final_sent)[part:].astype(f32)
-    xhat1, rstd1 = normalized(tokens.astype(f32))
-    input_grad = (middle_back + norm_back(normed_back * gain1, xhat1, rstd1)).astype(bf16)
-    result = (middle + (outside + down_bias_all)).astype(bf16)
+    result, input_grad = on_core(
+        own_rows_kernel,
+        place,
+        [normed_own]
+        + [after(item, *final_sent) for item in normed_returned]
+        + [outside_own]
+        + outside_returned
+        + [tokens, middle_back, middle, gain1[None], down_bias_all[None]],
+        [((part, model), bf16)] * 2,
+    )
     return (
         result,
         input_grad,

time: 223 us -> 221 us (level)
  waiting for transfers between devices: 78.2 us -> 66.4 us
  starting transfers between devices: 54.2 us -> 63.7 us
  other arithmetic: 15.7 us -> 12.2 us
  Pallas kernels: 52.1 us -> 55.4 us
    ppermute x21 -> x23, starting transfers between devices: 31.9 us -> 41.4 us  [passed_along(): lax.ppermute(array, 'uly', [(i, (i + by) % peers) for i in range(peers)])]
    ppermute x21 -> x23, waiting for transfers between devices: 53.8 us -> 44.6 us  [passed_along(): lax.ppermute(array, 'uly', [(i, (i + by) % peers) for i in range(peers)])]
    ppermute x12, waiting for transfers between devices: 23.1 us -> 16.6 us  [cube_swapped(): return lax.ppermute(array, CUBE, pairs)]
    ppermute x6, waiting for transfers between devices: 1.36 us -> 5.21 us  [blk_swapped(): return lax.ppermute(array, 'blk', [(i, i ^ flip) for i in range(peers)])]
    reduce_sum x3 -> x0, other arithmetic: 3.59 us -> none  [the longest x1 2.37 us: norm_back(): jnp.mean(grad, axis=-1, keepdims=True)]
    pallas_call x13 -> x14, Pallas kernels: 52.1 us -> 55.4 us  [on_core(): pl.pallas_call(kernel, out_shape=[jax.ShapeDtypeStruct(shape, dtype) for...]
    convert_element_type x1 -> x4, other arithmetic: 0.86 us -> 3.42 us  [the longest x1 1.34 us: shards(): near_next = (near_high + near_got[2:].astype(f32)).astype(bf16)]
    unnamed x118 -> x108, local copies, waits for them, and re-layouts: 9.33 us -> 8.45 us
  transfers between devices with their start and end apart: 39 -> 41, of which waited for: 16 -> 19; matrix products, arithmetic and copies ran while one was open for 11% -> 9% of each run, Pallas kernels for 17% -> 19%
where the time goes in v2:
time: 221 us; the launch traced here: 219 us
  waiting for transfers between devices  66.4 us (30%)
  starting transfers between devices  63.7 us (29%)
  Pallas kernels  55.4 us (25%)
  local copies, waits for them, and re-layouts  20.3 us (9%)
  other arithmetic  12.2 us (6%)
    pallas_call x14, Pallas kernels, on_core(): pl.pallas_call(kernel, out_shape=[jax.ShapeDtypeStruct(shape, dtype) for...  55.4 us
    ppermute x23, waiting for transfers between devices, passed_along(): lax.ppermute(array, 'uly', [(i, (i + by) % peers) for i in range(peers)])  44.6 us
    ppermute x23, starting transfers between devices, passed_along(): lax.ppermute(array, 'uly', [(i, (i + by) % peers) for i in range(peers)])  41.4 us
    ppermute x12, waiting for transfers between devices, cube_swapped(): return lax.ppermute(array, CUBE, pairs)  16.6 us
    ppermute x12, starting transfers between devices, cube_swapped(): return lax.ppermute(array, CUBE, pairs)  11.4 us
    ppermute x6, starting transfers between devices, blk_swapped(): return lax.ppermute(array, 'blk', [(i, i ^ flip) for i in range(peers)])  10.9 us
    unnamed x108, local copies, waits for them, and re-layouts  8.45 us
    ppermute x6, waiting for transfers between devices, blk_swapped(): return lax.ppermute(array, 'blk', [(i, i ^ flip) for i in range(peers)])  5.21 us
  transfers between devices with their start and end apart: 41, of which 19 were waited for; matrix products, arithmetic and copies ran while one was open for 9% of the time, Pallas kernels for 19%

profile of v2, /device:TPU:0, one launch (start us, length us, event | category | flops | bytes accessed | tf_op | source)
XLA Modules:
  0.0 219.4 jit_solution(13352509970707237573)
XLA Ops:
  2.7 3.1 %collective-permute-start = (bf16[160,768]{1,0:T(8,128)(2,1)S(1)}, bf16[160,768]{1,0:T(8,128)(2,1)S(1)}, u32[]{:S(2)}, u32[]{:S(2)}) collective-permute-start(bf16[160,768]{1,0:T(8,128)(2,1)S(1)} %pad_maximum_fusion.4), channel_id=1, source_target_pairs={{0,1},{1,2},{2,3},{3,0},{4,5},{5,6},{6,7},{7,4},{8,9},{9,10},{10,1... | collective-permute-start | bytes 737288 | tf_op jit(solution)/shard_map/ppermute | solution.py:36
  8.8 4.9 %collective-permute-done.t1 = bf16[160,768]{1,0:T(8,128)(2,1)S(1)} collective-permute-done((bf16[160,768]{1,0:T(8,128)(2,1)S(1)}, bf16[160,768]{1,0:T(8,128)(2,1)S(1)}, u32[]{:S(2)}, u32[]{:S(2)}) %collective-permute-start) | collective-permute-done | bytes 245792 | tf_op jit(solution)/shard_map/ppermute | solution.py:36
  13.7 1.7 collective-permute-start.2
  16.5 1.6 collective-permute-start.3
  18.1 3.5 %collective-permute-done.3.refs_2_ = bf16[112,576]{1,0:T(8,128)(2,1)S(1)} collective-permute-done((bf16[112,576]{1,0:T(8,128)(2,1)S(1)}, bf16[112,576]{1,0:T(8,128)(2,1)S(1)}, u32[]{:S(2)}, u32[]{:S(2)}) %collective-permute-start.3) | collective-permute-done | bytes 129056 | tf_op jit(solution)/shard_map/ppermute | solution.py:51
  21.9 1.6 collective-permute-start.4
  23.6 6.6 %collective-permute-done.1.t2 = bf16[160,768]{1,0:T(8,128)(2,1)S(1)} collective-permute-done((bf16[160,768]{1,0:T(8,128)(2,1)S(1)}, bf16[160,768]{1,0:T(8,128)(2,1)S(1)}, u32[]{:S(2)}, u32[]{:S(2)}) %collective-permute-start.1) | collective-permute-done | bytes 245792 | tf_op jit(solution)/shard_map/ppermute | solution.py:36
  30.9 1.5 collective-permute-start.9
  33.2 1.6 collective-permute-start.6
  34.8 4.5 %collective-permute-done.9.refs_2_ = bf16[96,2304]{1,0:T(8,128)(2,1)S(1)} collective-permute-done((bf16[96,2304]{1,0:T(8,128)(2,1)S(1)}, bf16[96,2304]{1,0:T(8,128)(2,1)S(1)}, u32[]{:S(2)}, u32[]{:S(2)}) %collective-permute-start.9) | collective-permute-done | bytes 442400 | tf_op jit(solution)/shard_map/ppermute | solution.py:51
  39.3 1.6 collective-permute-start.10
  40.9 2.4 %shard_map.296 = (bf16[8,96,576]{2,1,0:T(8,128)(2,1)}, bf16[8,16,576]{2,1,0:T(8,128)(2,1)}) custom-call(s32[1]{0:T(128)} %bitcast.2.refs_0_.index, bf16[112,576]{1,0:T(8,128)(2,1)} %copy-done.5, bf16[112,576]{1,0:T(8,128)(2,1)} %copy-done.9, bf16[2,112,576]{2,1,0:T(8,128)(2,1)} %copy-done.13, bf16[4,112,576]{2,1,0:T(8,128)(2,1)} %collective-permute-done.5.refs_4_), custom_call_target="tpu_custom_call" | custom-call | flops 30000001024 | tf_op jit(solution)/shard_map/pallas_call | solution.py:364
  46.4 3.9 %shard_map.297 = (bf16[512,192]{1,0:T(8,128)(2,1)}, bf16[512,384]{1,0:T(8,128)(2,1)}, bf16[512,768]{1,0:T(8,128)(2,1)}) custom-call(s32[2]{0:T(128)} %pad_add_fusion.place, bf16[128,768]{1,0:T(8,128)(2,1)} %tokens.1, bf16[160,768]{1,0:T(8,128)(2,1)} %copy-done.24, bf16[160,768]{1,0:T(8,128)(2,1)} %copy-done.26, bf16[160,768]{1,0:T(8,128)(2,1)} %copy-done.25, ...), custom_call_target="tpu_custom_call" | custom-call | flops 30000001024 | tf_op jit(solution)/shard_map/pallas_call | solution.py:364
  50.7 4.1 %collective-permute-start.12 = (bf16[128,768]{1,0:T(8,128)(2,1)}, bf16[128,768]{1,0:T(8,128)(2,1)S(1)}, u32[]{:S(2)}, u32[]{:S(2)}) collective-permute-start(bf16[128,768]{1,0:T(8,128)(2,1)} %refs_3_.1), channel_id=1, source_target_pairs={{0,3},{1,0},{2,1},{3,2},{4,7},{5,4},{6,5},{7,6},{8,11},{9,8},{10,9... | collective-permute-start | bytes 589832 | tf_op jit(solution)/shard_map/ppermute | solution.py:36
  56.0 3.7 %shard_map.298 = (f32[8,512]{1,0:T(8,128)}, f32[8,512]{1,0:T(8,128)}, f32[192,512]{1,0:T(8,128)}) custom-call(s32[2]{0:T(128)} %pad_add_fusion.place, bf16[512,192]{1,0:T(8,128)(2,1)} %get-tuple-element.102.query, bf16[512,384]{1,0:T(8,128)(2,1)} %get-tuple-element.103.kv_own, bf16[512,384]{1,0:T(8,128)(2,1)} %copy-done.33), custom_call_target="tpu_custom_call" | custom-call | flops 30000001024 | tf_op jit(solution)/shard_map/pallas_call | solution.py:364
  59.7 3.7 %collective-permute-done.11.c2.refs_5_ = bf16[128,768]{1,0:T(8,128)(2,1)S(1)} collective-permute-done((bf16[128,768]{1,0:T(8,128)(2,1)}, bf16[128,768]{1,0:T(8,128)(2,1)S(1)}, u32[]{:S(2)}, u32[]{:S(2)}) %collective-permute-start.11) | collective-permute-done | bytes 196640 | tf_op jit(solution)/shard_map/ppermute | solution.py:36
  63.4 2.9 %collective-permute-done.7.kv_y = bf16[512,384]{1,0:T(8,128)(2,1)} collective-permute-done((bf16[512,384]{1,0:T(8,128)(2,1)}, bf16[512,384]{1,0:T(8,128)(2,1)}, u32[]{:S(2)}, u32[]{:S(2)}) %collective-permute-start.7) | collective-permute-done | bytes 393248 | tf_op jit(solution)/shard_map/ppermute | solution.py:45
  69.1 2.2 %shard_map.299 = (bf16[192,512]{1,0:T(8,128)(2,1)}, f32[192,512]{1,0:T(8,128)}, f32[8,512]{1,0:T(8,128)}) custom-call(s32[2]{0:T(128)} %pad_add_fusion.place, bf16[512,192]{1,0:T(8,128)(2,1)} %get-tuple-element.102.query, bf16[512,384]{1,0:T(8,128)(2,1)} %collective-permute-done.7.kv_y, bf16[512,384]{1,0:T(8,128)(2,1)} %copy-done.34, ...), custom_call_target="tpu_custom_call" | custom-call | flops 30000001024 | tf_op jit(solution)/shard_map/pallas_call | solution.py:364
  71.4 2.2 %collective-permute-start.14 = (bf16[192,512]{1,0:T(8,128)(2,1)}, bf16[192,512]{1,0:T(8,128)(2,1)S(1)}, u32[]{:S(2)}, u32[]{:S(2)}) collective-permute-start(bf16[192,512]{1,0:T(8,128)(2,1)} %get-tuple-element.112.m0), channel_id=1, source_target_pairs={{0,1},{1,2},{2,3},{3,0},{4,5},{5,6},{6,7},{7,4},{8,9},{9,10},{10,1... | collective-permute-start | bytes 589832 | tf_op jit(solution)/shard_map/ppermute | solution.py:36
  77.2 4.1 %shard_map.300 = (bf16[8,96,768]{2,1,0:T(8,128)(2,1)}, bf16[8,96,768]{2,1,0:T(8,128)(2,1)}, bf16[8,96,768]{2,1,0:T(8,128)(2,1)}) custom-call(s32[1]{0:T(128)} %bitcast.2.refs_0_.index, bf16[96,2304]{1,0:T(8,128)(2,1)} %copy-done, bf16[96,2304]{1,0:T(8,128)(2,1)} %copy-done.2, bf16[2,96,2304]{2,1,0:T(8,128)(2,1)} %copy-done.6, bf16[4,96,2304]{2,1,0:T(8,128)(2,1)} %copy-done.32), custom_call_target="tpu_custom_call" | custom-call | flops 30000001024 | tf_op jit(solution)/shard_map/pallas_call | solution.py:364
  81.3 7.7 %collective-permute-done.15.m2 = bf16[192,512]{1,0:T(8,128)(2,1)S(1)} collective-permute-done((bf16[192,512]{1,0:T(8,128)(2,1)}, bf16[192,512]{1,0:T(8,128)(2,1)S(1)}, u32[]{:S(2)}, u32[]{:S(2)}) %collective-permute-start.15) | collective-permute-done | bytes 196640 | tf_op jit(solution)/shard_map/ppermute | solution.py:36
  89.8 7.4 %shard_map.301 = (f32[128,768]{1,0:T(8,128)}, bf16[512,768]{1,0:T(8,128)(2,1)}, bf16[768,128]{1,0:T(8,128)(2,1)}, bf16[512,768]{1,0:T(8,128)(2,1)}, bf16[512,768...) custom-call(s32[2]{0:T(128)} %pad_add_fusion.place, ...), custom_call_target="tpu_custom_call" | custom-call | flops 30000001024 | tf_op jit(solution)/shard_map/pallas_call | solution.py:364
  97.2 5.1 %collective-permute-start.18 = (bf16[128,768]{1,0:T(8,128)(2,1)}, bf16[128,768]{1,0:T(8,128)(2,1)S(1)}, u32[]{:S(2)}, u32[]{:S(2)}) collective-permute-start(bf16[128,768]{1,0:T(8,128)(2,1)} %get-tuple-element.122), channel_id=1, source_target_pairs={{0,3},{1,0},{2,1},{3,2},{4,7},{5,4},{6,5},{7,6},{8,11},{9,8},{10,9... | collective-permute-start | bytes 589832 | tf_op jit(solution)/shard_map/ppermute | solution.py:36
  103.3 3.7 %shard_map.302 = (f32[1,768]{1,0:T(1,128)}, f32[1,768]{1,0:T(1,128)}, f32[128,768]{1,0:T(8,128)}, bf16[128,768]{1,0:T(8,128)(2,1)}, bf16[128,768]{1,0:T(8,128)(2,1)}, /*index=5*/bf16[128,768]{1,0:T(8,128)(2,1)}) custom-call(s32[2]{0:T(128)} %pad_add_fusion.place, bf16[512,768]{1,0:T(8,128)(2,1)} %get-tuple-element.118.active.refs_7_, ...), custom_call_target="tpu_custom_call" | custom-call | flops 30000001024 | tf_op jit(solution)/shard_map/pallas_call | solution.py:364
  108.0 12.9 %collective-permute-done.19.r2 = bf16[128,768]{1,0:T(8,128)(2,1)S(1)} collective-permute-done((bf16[128,768]{1,0:T(8,128)(2,1)}, bf16[128,768]{1,0:T(8,128)(2,1)S(1)}, u32[]{:S(2)}, u32[]{:S(2)}) %collective-permute-start.19) | collective-permute-done | bytes 196640 | tf_op jit(solution)/shard_map/ppermute | solution.py:36
  121.7 3.3 %shard_map.303 = (f32[128,768]{1,0:T(8,128)}, bf16[128,768]{1,0:T(8,128)(2,1)}, bf16[192,128]{1,0:T(8,128)(2,1)}, bf16[192,128]{1,0:T(8,128)(2,1)}, bf16[192,128]{1,0:T(8,128)(2,1)}, /*index=5*/bf16[192,128]{1,0:T(8,128)(2,1)}) custom-call(s32[2]{0:T(128)} %pad_add_fusion.place, f32[128,768]{1,0:T(8,128)} %get-tuple-element.121.part_own, ...), custom_call_target="tpu_custom_call" | custom-call | flops 30000001024 | tf_op jit(solution)/shard_map/pallas_call | solution.py:364
  125.9 3.0 %collective-permute-start.25 = (bf16[192,128]{1,0:T(8,128)(2,1)}, bf16[192,128]{1,0:T(8,128)(2,1)S(1)}, u32[]{:S(2)}, u32[]{:S(2)}) collective-permute-start(bf16[192,128]{1,0:T(8,128)(2,1)} %get-tuple-element.134), channel_id=1, source_target_pairs={{0,3},{1,0},{2,1},{3,2},{4,7},{5,4},{6,5},{7,6},{8,11},{9,8},{10,9... | collective-permute-start | bytes 147464 | tf_op jit(solution)/shard_map/ppermute | solution.py:36
  129.4 3.3 %collective-permute-start.22 = (bf16[128,768]{1,0:T(8,128)(2,1)S(1)}, bf16[128,768]{1,0:T(8,128)(2,1)S(1)}, u32[]{:S(2)}, u32[]{:S(2)}) collective-permute-start(bf16[128,768]{1,0:T(8,128)(2,1)S(1)} %copy-done.42), channel_id=1, source_target_pairs={{0,3},{1,0},{2,1},{3,2},{4,7},{5,4},{6,5},{7,6},{8,11},{9,8},{10,9... | collective-permute-start | bytes 589832 | tf_op jit(solution)/shard_map/ppermute | solution.py:36
  132.7 6.2 %shard_map.304 = (bf16[4,96,2304]{2,1,0:T(8,128)(2,1)}, f32[2,96,2304]{2,1,0:T(8,128)}, f32[2,96,2304]{2,1,0:T(8,128)}) custom-call(s32[1]{0:T(128)} %bitcast.2.refs_0_.index, bf16[512,768]{1,0:T(8,128)(2,1)} %get-tuple-element.128.refs_1_, bf16[512,768]{1,0:T(8,128)(2,1)} %get-tuple-element.119.hidden_back.refs_2_, bf16[128,768]{1,0:T(8,128)(2,1)} %refs_3_.1, ...), custom_call_target="tpu_custom_call" | custom-call | flops 30000001024 | tf_op jit(solution)/shard_map/pallas_call | solution.py:364
  140.6 2.4 %shard_map.305 = (bf16[512,384]{1,0:T(8,128)(2,1)}, f32[192,512]{1,0:T(8,128)}) custom-call(s32[2]{0:T(128)} %pad_add_fusion.place, bf16[512,192]{1,0:T(8,128)(2,1)} %get-tuple-element.102.query, bf16[192,128]{1,0:T(8,128)(2,1)} %get-tuple-element.126.g0, bf16[192,128]{1,0:T(8,128)(2,1)} %copy-done.50, bf16[192,128]{1,0:T(8,128)(2,1)} %copy-done.51, ...), custom_call_target="tpu_custom_call" | custom-call | flops 30000001024 | tf_op jit(solution)/shard_map/pallas_call | solution.py:364
  143.6 1.4 collective-permute-done.27.dkv_core
  145.8 2.9 %shard_map.306 = (bf16[512,384]{1,0:T(8,128)(2,1)}, f32[192,512]{1,0:T(8,128)}) custom-call(s32[2]{0:T(128)} %pad_add_fusion.place, bf16[512,192]{1,0:T(8,128)(2,1)} %get-tuple-element.102.query, bf16[192,128]{1,0:T(8,128)(2,1)} %get-tuple-element.126.g0, bf16[192,128]{1,0:T(8,128)(2,1)} %copy-done.50, bf16[192,128]{1,0:T(8,128)(2,1)} %copy-done.51, ...), custom_call_target="tpu_custom_call" | custom-call | flops 30000001024 | tf_op jit(solution)/shard_map/pallas_call | solution.py:364
  148.7 8.2 %collective-permute-start.29 = (bf16[512,384]{1,0:T(8,128)(2,1)}, bf16[512,384]{1,0:T(8,128)(2,1)S(1)}, u32[]{:S(2)}, u32[]{:S(2)}) collective-permute-start(bf16[512,384]{1,0:T(8,128)(2,1)} %get-tuple-element.150), channel_id=1, source_target_pairs={{0,8},{4,12},{8,0},{12,4},{1,9},{5,13},{9,1},{13,5},{2,10},{6,14},... | collective-permute-start | bytes 1179656 | tf_op jit(solution)/shard_map/ppermute | solution.py:45
  157.0 5.3 %shard_map.307 = (bf16[512,384]{1,0:T(8,128)(2,1)}, bf16[512,384]{1,0:T(8,128)(2,1)}, bf16[512,192]{1,0:T(8,128)(2,1)}) custom-call(s32[2]{0:T(128)} %pad_add_fusion.place, bf16[512,192]{1,0:T(8,128)(2,1)} %get-tuple-element.102.query, bf16[192,128]{1,0:T(8,128)(2,1)} %get-tuple-element.126.g0, bf16[192,128]{1,0:T(8,128)(2,1)} %copy-done.50, ...), custom_call_target="tpu_custom_call" | custom-call | flops 30000001024 | tf_op jit(solution)/shard_map/pallas_call | solution.py:364
  162.3 2.2 collective-permute-start.28
  164.5 1.5 collective-permute-start.31
  167.4 4.8 %shard_map.308 = (f32[128,768]{1,0:T(8,128)}, bf16[128,768]{1,0:T(8,128)(2,1)}, bf16[256,768]{1,0:T(8,128)(2,1)}, bf16[128,768]{1,0:T(8,128)(2,1)}, bf16[4,112,6...) custom-call(s32[1]{0:T(128)} %bitcast.2.refs_0_.index, ...), custom_call_target="tpu_custom_call" | custom-call | flops 30000001024 | tf_op jit(solution)/shard_map/pallas_call | solution.py:364
  172.4 5.1 %collective-permute-done.31 = bf16[2,96,2304]{2,1,0:T(8,128)(2,1)S(1)} collective-permute-done((bf16[2,96,2304]{2,1,0:T(8,128)(2,1)S(1)}, bf16[2,96,2304]{2,1,0:T(8,128)(2,1)S(1)}, u32[]{:S(2)}, u32[]{:S(2)}) %collective-permute-start.31) | collective-permute-done | bytes 884768 | tf_op jit(solution)/shard_map/ppermute | solution.py:51
  177.5 1.3 add_convert_fusion.2
  178.9 1.6 collective-permute-start.34
  183.1 1.5 collective-permute-start.37
  185.8 2.0 collective-permute-start.30
  192.1 2.7 %collective-permute-done.35 = bf16[112,640]{1,0:T(8,128)(2,1)S(1)} collective-permute-done((bf16[112,640]{1,0:T(8,128)(2,1)S(1)}, bf16[112,640]{1,0:T(8,128)(2,1)S(1)}, u32[]{:S(2)}, u32[]{:S(2)}) %collective-permute-start.35) | collective-permute-done | bytes 143392 | tf_op jit(solution)/shard_map/ppermute | solution.py:51
  197.6 1.8 collective-permute-start.39
  199.3 2.2 collective-permute-start.38
  201.5 3.4 %collective-permute-start.40 = (bf16[112,192]{1,0:T(8,128)(2,1)S(1)}, bf16[112,192]{1,0:T(8,128)(2,1)S(1)}, u32[]{:S(2)}, u32[]{:S(2)}) collective-permute-start(bf16[112,192]{1,0:T(8,128)(2,1)S(1)} %get-tuple-element.231), channel_id=1, source_target_pairs={{0,1},{1,2},{2,3},{3,0},{4,5},{5,6},{6,7},{7,4},{8,9},{9,10},{10,1... | collective-permute-start | bytes 129032 | tf_op jit(solution)/shard_map/ppermute | solution.py:36
  204.9 6.1 %collective-permute-done.36.n2 = bf16[256,768]{1,0:T(8,128)(2,1)} collective-permute-done((bf16[256,768]{1,0:T(8,128)(2,1)}, bf16[256,768]{1,0:T(8,128)(2,1)}, u32[]{:S(2)}, u32[]{:S(2)}) %collective-permute-start.36) | collective-permute-done | bytes 393248 | tf_op jit(solution)/shard_map/ppermute | solution.py:36
  212.3 3.1 %shard_map.309 = (bf16[128,768]{1,0:T(8,128)(2,1)}, bf16[128,768]{1,0:T(8,128)(2,1)}) custom-call(s32[2]{0:T(128)} %pad_add_fusion.place, f32[128,768]{1,0:T(8,128)} %get-tuple-element.156.normed_own, bf16[128,768]{1,0:T(8,128)(2,1)} %collective-permute-done.30.n1, bf16[256,768]{1,0:T(8,128)(2,1)} %collective-permute-done.36.n2, ...), custom_call_target="tpu_custom_call" | custom-call | flops 30000001024 | tf_op jit(solution)/shard_map/pallas_call | solution.py:364
  (246 shorter events, 44.7 us)
Async XLA Ops:
  0.7 29.7 %copy-start.20 = (bf16[768,96]{0,1:T(8,128)(2,1)S(1)}, bf16[768,96]{0,1:T(8,128)(2,1)}, u32[]{:S(2)}) copy-start(bf16[768,96]{0,1:T(8,128)(2,1)} %param.23) | copy-start | bytes 442372
  0.7 29.7 %copy-start.7 = (bf16[96,768]{1,0:T(8,128)(2,1)S(1)}, bf16[96,768]{1,0:T(8,128)(2,1)}, u32[]{:S(2)}) copy-start(bf16[96,768]{1,0:T(8,128)(2,1)} %param.22) | copy-start | bytes 442372
  2.7 11.1 %collective-permute-start = (bf16[160,768]{1,0:T(8,128)(2,1)S(1)}, bf16[160,768]{1,0:T(8,128)(2,1)S(1)}, u32[]{:S(2)}, u32[]{:S(2)}) collective-permute-start(bf16[160,768]{1,0:T(8,128)(2,1)S(1)} %pad_maximum_fusion.4), channel_id=1, source_target_pairs={{0,1},{1,2},{2,3},{3,0},{4,5},{5,6},{6,7},{7,4},{8,9},{9,10},{10,1... | collective-permute-start | bytes 737288 | tf_op jit(solution)/shard_map/ppermute | solution.py:36
  6.5 23.9 %copy-start.14 = (bf16[96,64]{1,0:T(8,128)(2,1)}, bf16[96,64]{1,0:T(8,128)(2,1)S(1)}, u32[]{:S(2)}) copy-start(bf16[96,64]{1,0:T(8,128)(2,1)S(1)} %slice.267) | copy-start | bytes 36868
  7.2 23.1 %copy-start.16 = (bf16[96,128]{1,0:T(8,128)(2,1)}, bf16[96,128]{1,0:T(8,128)(2,1)S(1)}, u32[]{:S(2)}) copy-start(bf16[96,128]{1,0:T(8,128)(2,1)S(1)} %slice.268) | copy-start | bytes 73732
  13.7 8.2 %collective-permute-start.2 = (bf16[160,768]{1,0:T(8,128)(2,1)S(1)}, bf16[160,768]{1,0:T(8,128)(2,1)S(1)}, u32[]{:S(2)}, u32[]{:S(2)}) collective-permute-start(bf16[160,768]{1,0:T(8,128)(2,1)S(1)} %pad_maximum_fusion.4), channel_id=1, source_target_pairs={{0,3},{1,0},{2,1},{3,2},{4,7},{5,4},{6,5},{7,6},{8,11},{9,8},{10,9... | collective-permute-start | bytes 737288 | tf_op jit(solution)/shard_map/ppermute | solution.py:36
  16.4 13.8 %collective-permute-start.1 = (bf16[160,768]{1,0:T(8,128)(2,1)S(1)}, bf16[160,768]{1,0:T(8,128)(2,1)S(1)}, u32[]{:S(2)}, u32[]{:S(2)}) collective-permute-start(bf16[160,768]{1,0:T(8,128)(2,1)S(1)} %pad_maximum_fusion.4), channel_id=1, source_target_pairs={{0,2},{1,3},{2,0},{3,1},{4,6},{5,7},{6,4},{7,5},{8,10},{9,11},{10,... | collective-permute-start | bytes 737288 | tf_op jit(solution)/shard_map/ppermute | solution.py:36
  16.5 5.2 %collective-permute-start.3 = (bf16[112,576]{1,0:T(8,128)(2,1)S(1)}, bf16[112,576]{1,0:T(8,128)(2,1)S(1)}, u32[]{:S(2)}, u32[]{:S(2)}) collective-permute-start(bf16[112,576]{1,0:T(8,128)(2,1)S(1)} %fusion.6.refs_1_), channel_id=1, source_target_pairs={{0,16},{4,12},{8,24},{12,4},{16,0},{20,28},{24,8},{28,20},{1,17},{... | collective-permute-start | bytes 387080 | tf_op jit(solution)/shard_map/ppermute | solution.py:51
  21.9 8.6 %collective-permute-start.4 = (bf16[2,112,576]{2,1,0:T(8,128)(2,1)S(1)}, bf16[2,112,576]{2,1,0:T(8,128)(2,1)S(1)}, u32[]{:S(2)}, u32[]{:S(2)}) collective-permute-start(bf16[2,112,576]{2,1,0:T(8,128)(2,1)S(1)} %pad_maximum_fusion.3), channel_id=1, source_target_pairs={{0,8},{4,20},{8,0},{12,28},{16,24},{20,4},{24,16},{28,12},{1,9},{5... | collective-permute-start | bytes 774152 | tf_op jit(solution)/shard_map/ppermute | solution.py:51
  30.5 37.7 %copy-start = (bf16[96,2304]{1,0:T(8,128)(2,1)}, bf16[96,2304]{1,0:T(8,128)(2,1)S(1)}, u32[]{:S(2)}) copy-start(bf16[96,2304]{1,0:T(8,128)(2,1)S(1)} %concatenate.64.refs_1_) | copy-start | bytes 1327108
  30.9 8.3 %collective-permute-start.9 = (bf16[96,2304]{1,0:T(8,128)(2,1)S(1)}, bf16[96,2304]{1,0:T(8,128)(2,1)S(1)}, u32[]{:S(2)}, u32[]{:S(2)}) collective-permute-start(bf16[96,2304]{1,0:T(8,128)(2,1)S(1)} %concatenate.64.refs_1_), channel_id=1, source_target_pairs={{0,16},{4,12},{8,24},{12,4},{16,0},{20,28},{24,8},{28,20},{1,17},{... | collective-permute-start | bytes 1327112 | tf_op jit(solution)/shard_map/ppermute | solution.py:51
  32.5 8.4 %collective-permute-start.5 = (bf16[4,112,576]{2,1,0:T(8,128)(2,1)S(1)}, bf16[4,112,576]{2,1,0:T(8,128)(2,1)}, u32[]{:S(2)}, u32[]{:S(2)}) collective-permute-start(bf16[4,112,576]{2,1,0:T(8,128)(2,1)S(1)} %pad_maximum_fusion.2), channel_id=1, source_target_pairs={{0,4},{4,0},{8,12},{12,8},{16,20},{20,16},{24,28},{28,24},{1,5},{5... | collective-permute-start | bytes 1548296 | tf_op jit(solution)/shard_map/ppermute | solution.py:51
  33.2 12.5 %collective-permute-start.6 = (bf16[128,768]{1,0:T(8,128)(2,1)}, bf16[128,768]{1,0:T(8,128)(2,1)}, u32[]{:S(2)}, u32[]{:S(2)}) collective-permute-start(bf16[128,768]{1,0:T(8,128)(2,1)} %refs_3_.1), channel_id=1, source_target_pairs={{0,1},{1,2},{2,3},{3,0},{4,5},{5,6},{6,7},{7,4},{8,9},{9,10},{10,1... | collective-permute-start | bytes 589832 | tf_op jit(solution)/shard_map/ppermute | solution.py:36
  39.2 28.9 %copy-start.2 = (bf16[96,2304]{1,0:T(8,128)(2,1)}, bf16[96,2304]{1,0:T(8,128)(2,1)S(1)}, u32[]{:S(2)}) copy-start(bf16[96,2304]{1,0:T(8,128)(2,1)S(1)} %collective-permute-done.9.refs_2_) | copy-start | bytes 1327108
  39.3 15.9 %collective-permute-start.10 = (bf16[2,96,2304]{2,1,0:T(8,128)(2,1)S(1)}, bf16[2,96,2304]{2,1,0:T(8,128)(2,1)S(1)}, u32[]{:S(2)}, u32[]{:S(2)}) collective-permute-start(bf16[2,96,2304]{2,1,0:T(8,128)(2,1)S(1)} %pad_maximum_fusion.1), channel_id=1, source_target_pairs={{0,8},{4,20},{8,0},{12,28},{16,24},{20,4},{24,16},{28,12},{1,9},{5... | collective-permute-start | bytes 2654216 | tf_op jit(solution)/shard_map/ppermute | solution.py:51
  50.3 5.0 %collective-permute-start.8 = (bf16[512,384]{1,0:T(8,128)(2,1)}, bf16[512,384]{1,0:T(8,128)(2,1)S(1)}, u32[]{:S(2)}, u32[]{:S(2)}) collective-permute-start(bf16[512,384]{1,0:T(8,128)(2,1)} %get-tuple-element.103.kv_own), channel_id=1, source_target_pairs={{0,4},{4,0},{8,12},{12,8},{1,5},{5,1},{9,13},{13,9},{2,6},{6,2},{1... | collective-permute-start | bytes 1179656 | tf_op jit(solution)/shard_map/ppermute | solution.py:45
  50.3 13.1 %collective-permute-start.11 = (bf16[128,768]{1,0:T(8,128)(2,1)}, bf16[128,768]{1,0:T(8,128)(2,1)S(1)}, u32[]{:S(2)}, u32[]{:S(2)}) collective-permute-start(bf16[128,768]{1,0:T(8,128)(2,1)} %refs_3_.1), channel_id=1, source_target_pairs={{0,2},{1,3},{2,0},{3,1},{4,6},{5,7},{6,4},{7,5},{8,10},{9,11},{10,... | collective-permute-start | bytes 589832 | tf_op jit(solution)/shard_map/ppermute | solution.py:36
  50.7 12.7 %collective-permute-start.12 = (bf16[128,768]{1,0:T(8,128)(2,1)}, bf16[128,768]{1,0:T(8,128)(2,1)S(1)}, u32[]{:S(2)}, u32[]{:S(2)}) collective-permute-start(bf16[128,768]{1,0:T(8,128)(2,1)} %refs_3_.1), channel_id=1, source_target_pairs={{0,3},{1,0},{2,1},{3,2},{4,7},{5,4},{6,5},{7,6},{8,11},{9,8},{10,9... | collective-permute-start | bytes 589832 | tf_op jit(solution)/shard_map/ppermute | solution.py:36
  54.7 11.5 %collective-permute-start.7 = (bf16[512,384]{1,0:T(8,128)(2,1)}, bf16[512,384]{1,0:T(8,128)(2,1)}, u32[]{:S(2)}, u32[]{:S(2)}) collective-permute-start(bf16[512,384]{1,0:T(8,128)(2,1)} %get-tuple-element.103.kv_own), channel_id=1, source_target_pairs={{0,8},{4,12},{8,0},{12,4},{1,9},{5,13},{9,1},{13,5},{2,10},{6,14},... | collective-permute-start | bytes 1179656 | tf_op jit(solution)/shard_map/ppermute | solution.py:45
  66.2 1.9 collective-permute-start.13
  68.9 7.1 %collective-permute-start.17 = (bf16[4,96,2304]{2,1,0:T(8,128)(2,1)S(1)}, bf16[4,96,2304]{2,1,0:T(8,128)(2,1)S(1)}, u32[]{:S(2)}, u32[]{:S(2)}) collective-permute-start(bf16[4,96,2304]{2,1,0:T(8,128)(2,1)S(1)} %pad_maximum_fusion), channel_id=1, source_target_pairs={{0,4},{4,0},{8,12},{12,8},{16,20},{20,16},{24,28},{28,24},{1,5},{5... | collective-permute-start | bytes 5308424 | tf_op jit(solution)/shard_map/ppermute | solution.py:51
  71.4 9.9 %collective-permute-start.14 = (bf16[192,512]{1,0:T(8,128)(2,1)}, bf16[192,512]{1,0:T(8,128)(2,1)S(1)}, u32[]{:S(2)}, u32[]{:S(2)}) collective-permute-start(bf16[192,512]{1,0:T(8,128)(2,1)} %get-tuple-element.112.m0), channel_id=1, source_target_pairs={{0,1},{1,2},{2,3},{3,0},{4,5},{5,6},{6,7},{7,4},{8,9},{9,10},{10,1... | collective-permute-start | bytes 589832 | tf_op jit(solution)/shard_map/ppermute | solution.py:36
  73.6 15.5 %collective-permute-start.15 = (bf16[192,512]{1,0:T(8,128)(2,1)}, bf16[192,512]{1,0:T(8,128)(2,1)S(1)}, u32[]{:S(2)}, u32[]{:S(2)}) collective-permute-start(bf16[192,512]{1,0:T(8,128)(2,1)} %get-tuple-element.112.m0), channel_id=1, source_target_pairs={{0,2},{1,3},{2,0},{3,1},{4,6},{5,7},{6,4},{7,5},{8,10},{9,11},{10,... | collective-permute-start | bytes 589832 | tf_op jit(solution)/shard_map/ppermute | solution.py:36
  74.8 14.2 %collective-permute-start.16 = (bf16[192,512]{1,0:T(8,128)(2,1)}, bf16[192,512]{1,0:T(8,128)(2,1)S(1)}, u32[]{:S(2)}, u32[]{:S(2)}) collective-permute-start(bf16[192,512]{1,0:T(8,128)(2,1)} %get-tuple-element.112.m0), channel_id=1, source_target_pairs={{0,3},{1,0},{2,1},{3,2},{4,7},{5,4},{6,5},{7,6},{8,11},{9,8},{10,9... | collective-permute-start | bytes 589832 | tf_op jit(solution)/shard_map/ppermute | solution.py:36
  97.2 10.8 %collective-permute-start.18 = (bf16[128,768]{1,0:T(8,128)(2,1)}, bf16[128,768]{1,0:T(8,128)(2,1)S(1)}, u32[]{:S(2)}, u32[]{:S(2)}) collective-permute-start(bf16[128,768]{1,0:T(8,128)(2,1)} %get-tuple-element.122), channel_id=1, source_target_pairs={{0,3},{1,0},{2,1},{3,2},{4,7},{5,4},{6,5},{7,6},{8,11},{9,8},{10,9... | collective-permute-start | bytes 589832 | tf_op jit(solution)/shard_map/ppermute | solution.py:36
  102.4 18.6 %collective-permute-start.19 = (bf16[128,768]{1,0:T(8,128)(2,1)}, bf16[128,768]{1,0:T(8,128)(2,1)S(1)}, u32[]{:S(2)}, u32[]{:S(2)}) collective-permute-start(bf16[128,768]{1,0:T(8,128)(2,1)} %get-tuple-element.123), channel_id=1, source_target_pairs={{0,2},{1,3},{2,0},{3,1},{4,6},{5,7},{6,4},{7,5},{8,10},{9,11},{10,... | collective-permute-start | bytes 589832 | tf_op jit(solution)/shard_map/ppermute | solution.py:36
  103.3 17.7 %collective-permute-start.20 = (bf16[128,768]{1,0:T(8,128)(2,1)}, bf16[128,768]{1,0:T(8,128)(2,1)S(1)}, u32[]{:S(2)}, u32[]{:S(2)}) collective-permute-start(bf16[128,768]{1,0:T(8,128)(2,1)} %get-tuple-element.124), channel_id=1, source_target_pairs={{0,1},{1,2},{2,3},{3,0},{4,5},{5,6},{6,7},{7,4},{8,9},{9,10},{10,1... | collective-permute-start | bytes 589832 | tf_op jit(solution)/shard_map/ppermute | solution.py:36
  125.0 13.8 %collective-permute-start.21 = (bf16[192,128]{1,0:T(8,128)(2,1)}, bf16[192,128]{1,0:T(8,128)(2,1)S(1)}, u32[]{:S(2)}, u32[]{:S(2)}) collective-permute-start(bf16[192,128]{1,0:T(8,128)(2,1)} %get-tuple-element.127), channel_id=1, source_target_pairs={{0,1},{1,2},{2,3},{3,0},{4,5},{5,6},{6,7},{7,4},{8,9},{9,10},{10,1... | collective-permute-start | bytes 147464 | tf_op jit(solution)/shard_map/ppermute | solution.py:36
  125.0 14.9 %collective-permute-start.24 = (bf16[192,128]{1,0:T(8,128)(2,1)}, bf16[192,128]{1,0:T(8,128)(2,1)S(1)}, u32[]{:S(2)}, u32[]{:S(2)}) collective-permute-start(bf16[192,128]{1,0:T(8,128)(2,1)} %get-tuple-element.135), channel_id=1, source_target_pairs={{0,2},{1,3},{2,0},{3,1},{4,6},{5,7},{6,4},{7,5},{8,10},{9,11},{10,... | collective-permute-start | bytes 147464 | tf_op jit(solution)/shard_map/ppermute | solution.py:36
  125.9 14.1 %collective-permute-start.25 = (bf16[192,128]{1,0:T(8,128)(2,1)}, bf16[192,128]{1,0:T(8,128)(2,1)S(1)}, u32[]{:S(2)}, u32[]{:S(2)}) collective-permute-start(bf16[192,128]{1,0:T(8,128)(2,1)} %get-tuple-element.134), channel_id=1, source_target_pairs={{0,3},{1,0},{2,1},{3,2},{4,7},{5,4},{6,5},{7,6},{8,11},{9,8},{10,9... | collective-permute-start | bytes 147464 | tf_op jit(solution)/shard_map/ppermute | solution.py:36
  128.9 10.0 %collective-permute-start.23 = (bf16[128,768]{1,0:T(8,128)(2,1)S(1)}, bf16[128,768]{1,0:T(8,128)(2,1)S(1)}, u32[]{:S(2)}, u32[]{:S(2)}) collective-permute-start(bf16[128,768]{1,0:T(8,128)(2,1)S(1)} %copy-done.43), channel_id=1, source_target_pairs={{0,1},{1,2},{2,3},{3,0},{4,5},{5,6},{6,7},{7,4},{8,9},{9,10},{10,1... | collective-permute-start | bytes 589832 | tf_op jit(solution)/shard_map/ppermute | solution.py:36
  129.4 10.5 %collective-permute-start.22 = (bf16[128,768]{1,0:T(8,128)(2,1)S(1)}, bf16[128,768]{1,0:T(8,128)(2,1)S(1)}, u32[]{:S(2)}, u32[]{:S(2)}) collective-permute-start(bf16[128,768]{1,0:T(8,128)(2,1)S(1)} %copy-done.42), channel_id=1, source_target_pairs={{0,3},{1,0},{2,1},{3,2},{4,7},{5,4},{6,5},{7,6},{8,11},{9,8},{10,9... | collective-permute-start | bytes 589832 | tf_op jit(solution)/shard_map/ppermute | solution.py:36
  143.0 2.0 collective-permute-start.27
  143.1 13.7 %collective-permute-start.26 = (bf16[4,96,2304]{2,1,0:T(8,128)(2,1)S(1)}, bf16[4,96,2304]{2,1,0:T(8,128)(2,1)S(1)}, u32[]{:S(2)}, u32[]{:S(2)}) collective-permute-start(bf16[4,96,2304]{2,1,0:T(8,128)(2,1)S(1)} %copy-done.31), channel_id=1, source_target_pairs={{0,4},{4,0},{8,12},{12,8},{16,20},{20,16},{24,28},{28,24},{1,5},{5... | collective-permute-start | bytes 5308424 | tf_op jit(solution)/shard_map/ppermute | solution.py:51
  148.7 17.9 %collective-permute-start.29 = (bf16[512,384]{1,0:T(8,128)(2,1)}, bf16[512,384]{1,0:T(8,128)(2,1)S(1)}, u32[]{:S(2)}, u32[]{:S(2)}) collective-permute-start(bf16[512,384]{1,0:T(8,128)(2,1)} %get-tuple-element.150), channel_id=1, source_target_pairs={{0,8},{4,12},{8,0},{12,4},{1,9},{5,13},{9,1},{13,5},{2,10},{6,14},... | collective-permute-start | bytes 1179656 | tf_op jit(solution)/shard_map/ppermute | solution.py:45
  156.8 23.6 %copy-start.3 = (bf16[4,96,2304]{2,1,0:T(8,128)(2,1)}, bf16[4,96,2304]{2,1,0:T(8,128)(2,1)S(1)}, u32[]{:S(2)}) copy-start(bf16[4,96,2304]{2,1,0:T(8,128)(2,1)S(1)} %collective-permute-done.26) | copy-start | bytes 5308420
  162.3 4.3 %collective-permute-start.28 = (bf16[512,384]{1,0:T(8,128)(2,1)}, bf16[512,384]{1,0:T(8,128)(2,1)S(1)}, u32[]{:S(2)}, u32[]{:S(2)}) collective-permute-start(bf16[512,384]{1,0:T(8,128)(2,1)} %get-tuple-element.149), channel_id=1, source_target_pairs={{0,4},{4,0},{8,12},{12,8},{1,5},{5,1},{9,13},{13,9},{2,6},{6,2},{1... | collective-permute-start | bytes 1179656 | tf_op jit(solution)/shard_map/ppermute | solution.py:45
  164.5 13.0 %collective-permute-start.31 = (bf16[2,96,2304]{2,1,0:T(8,128)(2,1)S(1)}, bf16[2,96,2304]{2,1,0:T(8,128)(2,1)S(1)}, u32[]{:S(2)}, u32[]{:S(2)}) collective-permute-start(bf16[2,96,2304]{2,1,0:T(8,128)(2,1)S(1)} %add_convert_fusion), channel_id=1, source_target_pairs={{0,16},{4,12},{8,24},{12,4},{16,0},{20,28},{24,8},{28,20},{1,17},{... | collective-permute-start | bytes 2654216 | tf_op jit(solution)/shard_map/ppermute | solution.py:51
  172.3 5.2 %collective-permute-start.33 = (bf16[4,112,640]{2,1,0:T(8,128)(2,1)}, bf16[4,112,640]{2,1,0:T(8,128)(2,1)S(1)}, u32[]{:S(2)}, u32[]{:S(2)}) collective-permute-start(bf16[4,112,640]{2,1,0:T(8,128)(2,1)} %get-tuple-element.159), channel_id=1, source_target_pairs={{0,4},{4,0},{8,12},{12,8},{16,20},{20,16},{24,28},{28,24},{1,5},{5... | collective-permute-start | bytes 1720328 | tf_op jit(solution)/shard_map/ppermute | solution.py:51
  178.9 9.7 %collective-permute-start.34 = (bf16[2,112,640]{2,1,0:T(8,128)(2,1)S(1)}, bf16[2,112,640]{2,1,0:T(8,128)(2,1)}, u32[]{:S(2)}, u32[]{:S(2)}) collective-permute-start(bf16[2,112,640]{2,1,0:T(8,128)(2,1)S(1)} %add_convert_fusion.2), channel_id=1, source_target_pairs={{0,16},{4,12},{8,24},{12,4},{16,0},{20,28},{24,8},{28,20},{1,17},{... | collective-permute-start | bytes 860168 | tf_op jit(solution)/shard_map/ppermute | solution.py:51
  181.3 9.3 %collective-permute-start.32 = (bf16[96,2304]{1,0:T(8,128)(2,1)}, bf16[96,2304]{1,0:T(8,128)(2,1)}, u32[]{:S(2)}, u32[]{:S(2)}) collective-permute-start(bf16[96,2304]{1,0:T(8,128)(2,1)} %fusion), channel_id=1, source_target_pairs={{0,8},{4,20},{8,0},{12,28},{16,24},{20,4},{24,16},{28,12},{1,9},{5... | collective-permute-start | bytes 1327112 | tf_op jit(solution)/shard_map/ppermute | solution.py:51
  183.1 18.4 %collective-permute-start.37 = (bf16[128,768]{1,0:T(8,128)(2,1)}, bf16[128,768]{1,0:T(8,128)(2,1)}, u32[]{:S(2)}, u32[]{:S(2)}) collective-permute-start(bf16[128,768]{1,0:T(8,128)(2,1)} %get-tuple-element.166), channel_id=1, source_target_pairs={{0,1},{1,2},{2,3},{3,0},{4,5},{5,6},{6,7},{7,4},{8,9},{9,10},{10,1... | collective-permute-start | bytes 589832 | tf_op jit(solution)/shard_map/ppermute | solution.py:36
  184.7 26.3 %collective-permute-start.36 = (bf16[256,768]{1,0:T(8,128)(2,1)}, bf16[256,768]{1,0:T(8,128)(2,1)}, u32[]{:S(2)}, u32[]{:S(2)}) collective-permute-start(bf16[256,768]{1,0:T(8,128)(2,1)} %get-tuple-element.164), channel_id=1, source_target_pairs={{0,2},{1,3},{2,0},{3,1},{4,6},{5,7},{6,4},{7,5},{8,10},{9,11},{10,... | collective-permute-start | bytes 1179656 | tf_op jit(solution)/shard_map/ppermute | solution.py:36
  185.8 25.9 %collective-permute-start.30 = (bf16[128,768]{1,0:T(8,128)(2,1)}, bf16[128,768]{1,0:T(8,128)(2,1)}, u32[]{:S(2)}, u32[]{:S(2)}) collective-permute-start(bf16[128,768]{1,0:T(8,128)(2,1)} %get-tuple-element.157), channel_id=1, source_target_pairs={{0,3},{1,0},{2,1},{3,2},{4,7},{5,4},{6,5},{7,6},{8,11},{9,8},{10,9... | collective-permute-start | bytes 589832 | tf_op jit(solution)/shard_map/ppermute | solution.py:36
  189.7 5.2 %collective-permute-start.35 = (bf16[112,640]{1,0:T(8,128)(2,1)S(1)}, bf16[112,640]{1,0:T(8,128)(2,1)S(1)}, u32[]{:S(2)}, u32[]{:S(2)}) collective-permute-start(bf16[112,640]{1,0:T(8,128)(2,1)S(1)} %fusion.7), channel_id=1, source_target_pairs={{0,8},{4,20},{8,0},{12,28},{16,24},{20,4},{24,16},{28,12},{1,9},{5... | collective-permute-start | bytes 430088 | tf_op jit(solution)/shard_map/ppermute | solution.py:51
  197.6 18.8 %collective-permute-start.39 = (bf16[112,192]{1,0:T(8,128)(2,1)S(1)}, bf16[112,192]{1,0:T(8,128)(2,1)S(1)}, u32[]{:S(2)}, u32[]{:S(2)}) collective-permute-start(bf16[112,192]{1,0:T(8,128)(2,1)S(1)} %get-tuple-element.232), channel_id=1, source_target_pairs={{0,2},{1,3},{2,0},{3,1},{4,6},{5,7},{6,4},{7,5},{8,10},{9,11},{10,... | collective-permute-start | bytes 129032 | tf_op jit(solution)/shard_map/ppermute | solution.py:36
  199.3 17.1 %collective-permute-start.38 = (bf16[112,192]{1,0:T(8,128)(2,1)S(1)}, bf16[112,192]{1,0:T(8,128)(2,1)S(1)}, u32[]{:S(2)}, u32[]{:S(2)}) collective-permute-start(bf16[112,192]{1,0:T(8,128)(2,1)S(1)} %get-tuple-element.233), channel_id=1, source_target_pairs={{0,3},{1,0},{2,1},{3,2},{4,7},{5,4},{6,5},{7,6},{8,11},{9,8},{10,9... | collective-permute-start | bytes 129032 | tf_op jit(solution)/shard_map/ppermute | solution.py:36
  201.5 15.0 %collective-permute-start.40 = (bf16[112,192]{1,0:T(8,128)(2,1)S(1)}, bf16[112,192]{1,0:T(8,128)(2,1)S(1)}, u32[]{:S(2)}, u32[]{:S(2)}) collective-permute-start(bf16[112,192]{1,0:T(8,128)(2,1)S(1)} %get-tuple-element.231), channel_id=1, source_target_pairs={{0,1},{1,2},{2,3},{3,0},{4,5},{5,6},{6,7},{7,4},{8,9},{9,10},{10,1... | collective-permute-start | bytes 129032 | tf_op jit(solution)/shard_map/ppermute | solution.py:36
  (46 other events, 284.7 us)

commit v3 on v2

--- a/solution.py
+++ b/solution.py
@@ -55,11 +55,10 @@
     return lax.axis_index("fsdp") * lax.axis_size("blk") + lax.axis_index("blk")
 
 
-def place_kernel(cuts, index_ref, own, first, second, other, *outs):
-    me = index_ref[0]
+def cube_pieces(me, own, first, second, other):
     odd = me & 1
     near, far = jnp.where(odd == 1, 2, 4), jnp.where(odd == 1, 4, 2)
-    pieces = [
+    return [
         (own, 0),
         (first, near),
         (second.at[0], far),
@@ -69,7 +68,11 @@
         (other.at[2], near ^ 1),
         (other.at[3], 7),
     ]
-    for piece, flip in pieces:
+
+
+def place_kernel(cuts, index_ref, own, first, second, other, *outs):
+    me = index_ref[0]
+    for piece, flip in cube_pieces(me, own, first, second, other):
         for out, (row, rows, column, columns) in zip(outs, cuts):
             out[me ^ flip] = piece[row : row + rows, column : column + columns]
 
@@ -391,15 +394,68 @@
     return jnp.concatenate([ref[:rows] for ref in refs], axis=0)
 
 
-def project_kernel(place, t0, t1, t2, t3, weight, named, bias, query, kv, xhat_low):
-    rows = stacked_slots((t0, t1, t2, t3)).astype(jnp.float32)
-    xhat, _ = normalized(rows)
+def project(rows, weight, gain, shift, bias, query, kv, xhat_low):
+    xhat, _ = normalized(rows.astype(jnp.float32))
     xhat_low[...] = xhat.astype(jnp.bfloat16)
-    normed = (xhat * named[0:1] + named[1:2]).astype(jnp.bfloat16)
-    qkv = dot_plain(normed, weight[...]) + bias[...]
+    normed = (xhat * gain + shift).astype(jnp.bfloat16)
+    qkv = dot_plain(normed, weight) + bias
     wide = kv.shape[1]
     kv[...] = qkv[:, :wide].astype(jnp.bfloat16)
     query[...] = qkv[:, wide:].astype(jnp.bfloat16) * jnp.asarray(HEAD_DIM**-0.5, jnp.bfloat16)
+
+
+def project_kernel(place, t0, t1, t2, t3, weight, named, bias, query, kv, xhat_low):
+    rows = stacked_slots((t0, t1, t2, t3))
+    project(rows, weight[...], named[0:1], named[1:2], bias[...], query, kv, xhat_low)
+
+
+def entry_kernel(
+    index,
+    own,
+    first,
+    second,
+    other,
+    t0,
+    t1,
+    t2,
+    t3,
+    weight,
+    named_out,
+    up_own,
+    query,
+    kv,
+    xhat_low,
+):
+    me, uly = index[0], index[1]
+    model, wide = weight.shape
+    depth, width = model // 8, wide // 3
+    rows = named_out.shape[0]
+    lane = lax.broadcasted_iota(jnp.int32, (rows, model), 1)
+    named = jnp.zeros((rows, model), jnp.float32)
+    for piece, flip in cube_pieces(me, own, first, second, other):
+        at = me ^ flip
+        weight[pl.ds(pl.multiple_of(at * depth, 16), depth), :] = piece[:depth, :]
+        vector = piece[depth : depth + rows, :128].astype(jnp.float32)
+        vector = jnp.concatenate([vector, jnp.zeros((rows, model - 128), jnp.float32)], axis=1)
+        named = named + pltpu.roll(jnp.where(lane < depth, vector, 0.0), at * depth, 1)
+    named_out[...] = named
+    turned = pltpu.roll(named, ((4 - uly) & 3) * width, 1)
+
+    def moved(row, by, low, high):
+        block = row // 8 * 8
+        item = pltpu.roll(turned[block : block + 8], by, 1) if by else turned[block : block + 8]
+        inside = (lane[:8] >= low) & (lane[:8] < high)
+        return jnp.where(inside, item, 0.0)[row - block : row - block + 1]
+
+    bias = moved(1, 64, width, width + 64) + moved(1, width + 64, width + 64, 2 * width)
+    bias = bias + moved(0, 2 * width, 2 * width, 3 * width)
+    up = jnp.zeros((1, model), jnp.float32)
+    for row in range(4):
+        up = up + moved(8 + row, depth * row, depth * row, depth * (row + 1))
+        up = up + moved(8 + row, depth * (3 + row), depth * (4 + row), depth * (5 + row))
+    up_own[...] = up
+    rows = stacked_slots((t0, t1, t2, t3))
+    project(rows, weight[...], named[4:5], named[5:6], bias[:, :wide], query, kv, xhat_low)
 
 
 GELU_A, GELU_B = 0.7978845608028654, 0.044715
@@ -638,7 +694,6 @@
     token_sent = jnp.concatenate([tokens, jnp.pad(output_rows, ((0, spare), (0, 0)))], axis=0)
     token_slots = [tokens, passed_along(token_sent, 1), None, None]
     qkv_sent = jnp.concatenate([qkv_own, vector_rows], axis=0)
-    qkv_cuts = [(0, depth, 0, wide), (depth, VEC_ROWS, 0, wide)]
     if paired():
         qkv_sent = after(qkv_sent, token_slots[1])
         token_later = after(token_sent, token_slots[1])
@@ -650,26 +705,10 @@
         qkv_other = cube_swapped(
             jnp.concatenate([qkv_sent[None], qkv_first[None], qkv_second]), 1, 1
         )
-        qkv_whole, vector_whole = cube_placed(
-            qkv_cuts, (qkv_sent, qkv_first, qkv_second, qkv_other)
-        )
     else:
         token_slots = [tokens] + slots_of(token_sent)[1:]
         whole = lax.all_gather(qkv_sent, CUBE, axis=0, tiled=False)
         qkv_whole, vector_whole = whole[:, :depth], whole[:, depth:]
-    qkv_whole = qkv_whole.reshape(model, wide)
-    vector_whole = vector_whole[:, :named, :depth].astype(f32)
-    up_bias_whole = vector_whole[:, len(vectors) :].reshape(-1)
-    named = vector_whole.transpose(1, 0, 2).reshape(named, model)
-    query_bias_own = lax.dynamic_slice_in_dim(named[0], uly * width, width)
-    value_bias_own = lax.dynamic_slice_in_dim(named[1], uly * width, width)
-    up_bias_own = lax.dynamic_slice_in_dim(up_bias_whole, uly * units, units)
-    output_bias_all, down_bias_all = named[2], named[3]
-    gain1, gain2, shift2 = named[4], named[6], named[7]
-
-    qkv_bias = jnp.concatenate(
-        [jnp.zeros((width,), f32), value_bias_own[128:], value_bias_own[:128], query_bias_own]
-    )
 
     inner = groups * width
     rest_cuts = [
@@ -690,24 +729,44 @@
         rest_own = after(rest_own, qkv_second)
         rest_first = cube_swapped(rest_own, 4, 2)
 
-    qkv_ready = after(qkv_whole, cotangent_slots[1])
-    query, kv_own, xhat1_low = on_core(
-        project_kernel,
-        place,
-        token_slots + [qkv_ready, named[4:6], qkv_bias[None]],
-        [((rows, width), bf16), ((rows, 2 * width), bf16), ((rows, model), bf16)],
-    )
+    project_outs = [((rows, width), bf16), ((rows, 2 * width), bf16), ((rows, model), bf16)]
+    if paired():
+        qkv_whole, named, up_bias_own, query, kv_own, xhat1_low = on_core(
+            entry_kernel,
+            jnp.stack([cube_index(), uly]).astype(jnp.int32),
+            [qkv_sent, qkv_first, qkv_second, qkv_other] + token_slots,
+            [((model, wide), bf16), ((VEC_ROWS, model), f32), ((1, units), f32)] + project_outs,
+        )
+    else:
+        qkv_whole = qkv_whole.reshape(model, wide)
+        vector_whole = vector_whole[:, :named, :depth].astype(f32)
+        up_bias_whole = vector_whole[:, len(vectors) :].reshape(-1)
+        named = vector_whole.transpose(1, 0, 2).reshape(named, model)
+        query_bias_own = lax.dynamic_slice_in_dim(named[0], uly * width, width)
+        value_bias_own = lax.dynamic_slice_in_dim(named[1], uly * width, width)
+        up_bias_own = lax.dynamic_slice_in_dim(up_bias_whole, uly * units, units)
+        qkv_bias = jnp.concatenate(
+            [jnp.zeros((width,), f32), value_bias_own[128:], value_bias_own[:128], query_bias_own]
+        )
+        up_bias_own = up_bias_own[None]
+        query, kv_own, xhat1_low = on_core(
+            project_kernel,
+            place,
+            token_slots + [qkv_whole, named[4:6], qkv_bias[None]],
+            project_outs,
+        )
+    output_bias_all, down_bias_all = named[2], named[3]
+    gain1, gain2, shift2 = named[4], named[6], named[7]
     kv_y = blk_swapped(kv_own, 2)
     kv_core = blk_swapped(kv_own, 1)
     stats = ((8, rows), f32)
     turned = ((width, rows), f32)
     if paired():
-        rest_second = cube_swapped(jnp.stack([rest_own, rest_first]), 2, 4)
-        kv_core = after(kv_core, rest_second)
+        rest_second = cube_swapped(after(jnp.stack([rest_own, rest_first]), kv_own), 2, 4)
     top, total, mixed_t = on_core(
         forward_near_kernel, place, (query, kv_own, kv_core), (stats, stats, turned)
     )
-    kv_both = blk_swapped(after(kv_y, top, *cotangent_slots[2:]), 1)
+    kv_both = blk_swapped(after(kv_y, top, *cotangent_slots[1:]), 1)
     if paired():
         rest_second = after(rest_second, kv_both)
         rest_held = jnp.concatenate([rest_own[None], rest_first[None], rest_second])
@@ -743,7 +802,7 @@
         mixed_slots
         + token_slots
         + cotangent_slots
-        + [output_t, up_whole, down_t, jnp.stack([output_bias_all, gain2, shift2]), up_bias_own[None]],
+        + [output_t, up_whole, down_t, jnp.stack([output_bias_all, gain2, shift2]), up_bias_own],
         [slab, wide_low, ((inner, part), bf16), units_low, units_low, slab] + slabs,
     )
     second_returned = slots_returned(second_parts)

time: 221 us -> 217 us (0.982)
  Pallas kernels: 55.4 us -> 53 us
  starting transfers between devices: 63.7 us -> 66 us
    ppermute x6, waiting for transfers between devices: 5.21 us -> 2.02 us  [blk_swapped(): return lax.ppermute(array, 'blk', [(i, i ^ flip) for i in range(peers)])]
    pallas_call x14 -> x13, Pallas kernels: 55.4 us -> 53 us  [on_core(): pl.pallas_call(kernel, out_shape=[jax.ShapeDtypeStruct(shape, dtype) for...]
    ppermute x23, waiting for transfers between devices: 44.6 us -> 46.9 us  [passed_along(): lax.ppermute(array, 'uly', [(i, (i + by) % peers) for i in range(peers)])]
    ppermute x6, starting transfers between devices: 10.9 us -> 13.2 us  [blk_swapped(): return lax.ppermute(array, 'blk', [(i, i ^ flip) for i in range(peers)])]
    unnamed x108 -> x112, local copies, waits for them, and re-layouts: 8.45 us -> 8.63 us
  transfers between devices with their start and end apart: 41 -> 41, of which waited for: 19 -> 18; matrix products, arithmetic and copies ran while one was open for 9% -> 8% of each run, Pallas kernels for 19% -> 18%
where the time goes in v3:
time: 217 us; the launch traced here: 215 us
  starting transfers between devices  66 us (30%)
  waiting for transfers between devices  64.8 us (30%)
  Pallas kernels  53 us (24%)
  local copies, waits for them, and re-layouts  18.2 us (8%)
  other arithmetic  11.9 us (5%)
    pallas_call x13, Pallas kernels, on_core(): pl.pallas_call(kernel, out_shape=[jax.ShapeDtypeStruct(shape, dtype) for...  53 us
    ppermute x23, waiting for transfers between devices, passed_along(): lax.ppermute(array, 'uly', [(i, (i + by) % peers) for i in range(peers)])  46.9 us
    ppermute x23, starting transfers between devices, passed_along(): lax.ppermute(array, 'uly', [(i, (i + by) % peers) for i in range(peers)])  43.4 us
    ppermute x12, waiting for transfers between devices, cube_swapped(): return lax.ppermute(array, CUBE, pairs)  15.9 us
    ppermute x6, starting transfers between devices, blk_swapped(): return lax.ppermute(array, 'blk', [(i, i ^ flip) for i in range(peers)])  13.2 us
    ppermute x12, starting transfers between devices, cube_swapped(): return lax.ppermute(array, CUBE, pairs)  9.37 us
    unnamed x112, local copies, waits for them, and re-layouts  8.63 us
  transfers between devices with their start and end apart: 41, of which 18 were waited for; matrix products, arithmetic and copies ran while one was open for 8% of the time, Pallas kernels for 18%

profile of v3, /device:TPU:0, one launch (start us, length us, event | category | flops | bytes accessed | tf_op | source)
XLA Modules:
  0.0 215.3 jit_solution(5665190164192072566)
XLA Ops:
  2.7 3.1 %collective-permute-start = (bf16[160,768]{1,0:T(8,128)(2,1)S(1)}, bf16[160,768]{1,0:T(8,128)(2,1)S(1)}, u32[]{:S(2)}, u32[]{:S(2)}) collective-permute-start(bf16[160,768]{1,0:T(8,128)(2,1)S(1)} %pad_maximum_fusion.4), channel_id=1, source_target_pairs={{0,1},{1,2},{2,3},{3,0},{4,5},{5,6},{6,7},{7,4},{8,9},{9,10},{10,1... | collective-permute-start | bytes 737288 | tf_op jit(solution)/shard_map/ppermute | solution.py:36
  8.0 5.7 %collective-permute-done.t1 = bf16[160,768]{1,0:T(8,128)(2,1)S(1)} collective-permute-done((bf16[160,768]{1,0:T(8,128)(2,1)S(1)}, bf16[160,768]{1,0:T(8,128)(2,1)S(1)}, u32[]{:S(2)}, u32[]{:S(2)}) %collective-permute-start) | collective-permute-done | bytes 245792 | tf_op jit(solution)/shard_map/ppermute | solution.py:36
  13.7 1.7 collective-permute-start.2
  17.2 1.6 collective-permute-start.1
  18.8 3.6 %collective-permute-done.1.first = bf16[112,576]{1,0:T(8,128)(2,1)S(1)} collective-permute-done((bf16[112,576]{1,0:T(8,128)(2,1)S(1)}, bf16[112,576]{1,0:T(8,128)(2,1)S(1)}, u32[]{:S(2)}, u32[]{:S(2)}) %collective-permute-start.1) | collective-permute-done | bytes 129056 | tf_op jit(solution)/shard_map/ppermute | solution.py:51
  22.4 1.6 collective-permute-start.3
  24.7 6.5 %collective-permute-done.4.t2 = bf16[160,768]{1,0:T(8,128)(2,1)S(1)} collective-permute-done((bf16[160,768]{1,0:T(8,128)(2,1)S(1)}, bf16[160,768]{1,0:T(8,128)(2,1)S(1)}, u32[]{:S(2)}, u32[]{:S(2)}) %collective-permute-start.4) | collective-permute-done | bytes 245792 | tf_op jit(solution)/shard_map/ppermute | solution.py:36
  31.7 1.6 collective-permute-start.12
  34.2 3.8 %shard_map.296 = (bf16[768,576]{1,0:T(8,128)(2,1)}, f32[16,768]{1,0:T(8,128)}, f32[1,768]{1,0:T(1,128)}, bf16[512,192]{1,0:T(8,128)(2,1)}, bf16[512,384]{1,0:T(8,128)(2,1)}, /*index=5*/bf16[512,768]{1,0:T(8,128)(2,1)}) custom-call(s32[2]{0:T(128)} %pad_add_fusion.1.index, bf16[112,576]{1,0:T(8,128)(2,1)} %copy-done.5, bf16[112,576]{1,0:T(8,128)(2,1)} %copy-done.9, ...), custom_call_target="tpu_custom_call" | custom-call | flops 30000001024 | tf_op jit(solution)/shard_map/pallas_call | solution.py:367
  38.7 3.5 %collective-permute-start.10 = (bf16[128,768]{1,0:T(8,128)(2,1)S(1)}, bf16[128,768]{1,0:T(8,128)(2,1)S(1)}, u32[]{:S(2)}, u32[]{:S(2)}) collective-permute-start(bf16[128,768]{1,0:T(8,128)(2,1)S(1)} %copy-done.38), channel_id=1, source_target_pairs={{0,3},{1,0},{2,1},{3,2},{4,7},{5,4},{6,5},{7,6},{8,11},{9,8},{10,9... | collective-permute-start | bytes 589832 | tf_op jit(solution)/shard_map/ppermute | solution.py:36
  42.9 1.5 collective-permute-start.6
  45.2 3.7 %shard_map.297 = (f32[8,512]{1,0:T(8,128)}, f32[8,512]{1,0:T(8,128)}, f32[192,512]{1,0:T(8,128)}) custom-call(s32[2]{0:T(128)} %pad_add_fusion.place, bf16[512,192]{1,0:T(8,128)(2,1)} %get-tuple-element.98.query, bf16[512,384]{1,0:T(8,128)(2,1)} %get-tuple-element.99.kv_own, bf16[512,384]{1,0:T(8,128)(2,1)} %copy-done.32), custom_call_target="tpu_custom_call" | custom-call | flops 30000001024 | tf_op jit(solution)/shard_map/pallas_call | solution.py:367
  48.9 3.3 %collective-permute-done.8.c1.refs_4_ = bf16[128,768]{1,0:T(8,128)(2,1)S(1)} collective-permute-done((bf16[128,768]{1,0:T(8,128)(2,1)S(1)}, bf16[128,768]{1,0:T(8,128)(2,1)S(1)}, u32[]{:S(2)}, u32[]{:S(2)}) %collective-permute-start.8) | collective-permute-done | bytes 196640 | tf_op jit(solution)/shard_map/ppermute | solution.py:36
  52.3 6.4 %collective-permute-done.9.c2.refs_5_ = bf16[128,768]{1,0:T(8,128)(2,1)S(1)} collective-permute-done((bf16[128,768]{1,0:T(8,128)(2,1)S(1)}, bf16[128,768]{1,0:T(8,128)(2,1)S(1)}, u32[]{:S(2)}, u32[]{:S(2)}) %collective-permute-start.9) | collective-permute-done | bytes 196640 | tf_op jit(solution)/shard_map/ppermute | solution.py:36
  61.6 1.7 collective-permute-done.13.refs_3_
  64.3 2.2 %shard_map.298 = (bf16[192,512]{1,0:T(8,128)(2,1)}, f32[192,512]{1,0:T(8,128)}, f32[8,512]{1,0:T(8,128)}) custom-call(s32[2]{0:T(128)} %pad_add_fusion.place, bf16[512,192]{1,0:T(8,128)(2,1)} %get-tuple-element.98.query, bf16[512,384]{1,0:T(8,128)(2,1)} %copy-done.33, bf16[512,384]{1,0:T(8,128)(2,1)} %copy-done.34, f32[8,512]{1,0:T(8,128)} %get-tuple-element.100.top_in, ...), custom_call_target="tpu_custom_call" | custom-call | flops 30000001024 | tf_op jit(solution)/shard_map/pallas_call | solution.py:367
  66.5 3.5 %collective-permute-start.14 = (bf16[192,512]{1,0:T(8,128)(2,1)}, bf16[192,512]{1,0:T(8,128)(2,1)S(1)}, u32[]{:S(2)}, u32[]{:S(2)}) collective-permute-start(bf16[192,512]{1,0:T(8,128)(2,1)} %get-tuple-element.109.m0), channel_id=1, source_target_pairs={{0,1},{1,2},{2,3},{3,0},{4,5},{5,6},{6,7},{7,4},{8,9},{9,10},{10,1... | collective-permute-start | bytes 589832 | tf_op jit(solution)/shard_map/ppermute | solution.py:36
  70.3 2.1 collective-permute-start.16
  73.6 4.1 %shard_map.299 = (bf16[8,96,768]{2,1,0:T(8,128)(2,1)}, bf16[8,96,768]{2,1,0:T(8,128)(2,1)}, bf16[8,96,768]{2,1,0:T(8,128)(2,1)}) custom-call(s32[1]{0:T(128)} %bitcast.2.refs_0_.index, bf16[96,2304]{1,0:T(8,128)(2,1)} %copy-done, bf16[96,2304]{1,0:T(8,128)(2,1)} %copy-done.2, bf16[2,96,2304]{2,1,0:T(8,128)(2,1)} %copy-done.6, bf16[4,96,2304]{2,1,0:T(8,128)(2,1)} %copy-done.29), custom_call_target="tpu_custom_call" | custom-call | flops 30000001024 | tf_op jit(solution)/shard_map/pallas_call | solution.py:367
  77.7 6.6 %collective-permute-done.15.m2 = bf16[192,512]{1,0:T(8,128)(2,1)S(1)} collective-permute-done((bf16[192,512]{1,0:T(8,128)(2,1)}, bf16[192,512]{1,0:T(8,128)(2,1)S(1)}, u32[]{:S(2)}, u32[]{:S(2)}) %collective-permute-start.15) | collective-permute-done | bytes 196640 | tf_op jit(solution)/shard_map/ppermute | solution.py:36
  85.1 7.5 %shard_map.300 = (f32[128,768]{1,0:T(8,128)}, bf16[512,768]{1,0:T(8,128)(2,1)}, bf16[768,128]{1,0:T(8,128)(2,1)}, bf16[512,768]{1,0:T(8,128)(2,1)}, bf16[512,768...) custom-call(s32[2]{0:T(128)} %pad_add_fusion.place, ...), custom_call_target="tpu_custom_call" | custom-call | flops 30000001024 | tf_op jit(solution)/shard_map/pallas_call | solution.py:367
  92.6 6.5 %collective-permute-start.18 = (bf16[128,768]{1,0:T(8,128)(2,1)}, bf16[128,768]{1,0:T(8,128)(2,1)S(1)}, u32[]{:S(2)}, u32[]{:S(2)}) collective-permute-start(bf16[128,768]{1,0:T(8,128)(2,1)} %get-tuple-element.121), channel_id=1, source_target_pairs={{0,3},{1,0},{2,1},{3,2},{4,7},{5,4},{6,5},{7,6},{8,11},{9,8},{10,9... | collective-permute-start | bytes 589832 | tf_op jit(solution)/shard_map/ppermute | solution.py:36
  99.7 3.7 %shard_map.301 = (f32[1,768]{1,0:T(1,128)}, f32[1,768]{1,0:T(1,128)}, f32[128,768]{1,0:T(8,128)}, bf16[128,768]{1,0:T(8,128)(2,1)}, bf16[128,768]{1,0:T(8,128)(2,1)}, /*index=5*/bf16[128,768]{1,0:T(8,128)(2,1)}) custom-call(s32[2]{0:T(128)} %pad_add_fusion.place, bf16[512,768]{1,0:T(8,128)(2,1)} %get-tuple-element.117.active.refs_7_, ...), custom_call_target="tpu_custom_call" | custom-call | flops 30000001024 | tf_op jit(solution)/shard_map/pallas_call | solution.py:367
  104.7 11.7 %collective-permute-done.19.r2 = bf16[128,768]{1,0:T(8,128)(2,1)S(1)} collective-permute-done((bf16[128,768]{1,0:T(8,128)(2,1)}, bf16[128,768]{1,0:T(8,128)(2,1)S(1)}, u32[]{:S(2)}, u32[]{:S(2)}) %collective-permute-start.19) | collective-permute-done | bytes 196640 | tf_op jit(solution)/shard_map/ppermute | solution.py:36
  117.1 3.3 %shard_map.302 = (f32[128,768]{1,0:T(8,128)}, bf16[128,768]{1,0:T(8,128)(2,1)}, bf16[192,128]{1,0:T(8,128)(2,1)}, bf16[192,128]{1,0:T(8,128)(2,1)}, bf16[192,128]{1,0:T(8,128)(2,1)}, /*index=5*/bf16[192,128]{1,0:T(8,128)(2,1)}) custom-call(s32[2]{0:T(128)} %pad_add_fusion.place, f32[128,768]{1,0:T(8,128)} %get-tuple-element.120.part_own, ...), custom_call_target="tpu_custom_call" | custom-call | flops 30000001024 | tf_op jit(solution)/shard_map/pallas_call | solution.py:367
  120.9 1.9 collective-permute-start.24
  122.8 2.9 %collective-permute-start.25 = (bf16[192,128]{1,0:T(8,128)(2,1)}, bf16[192,128]{1,0:T(8,128)(2,1)S(1)}, u32[]{:S(2)}, u32[]{:S(2)}) collective-permute-start(bf16[192,128]{1,0:T(8,128)(2,1)} %get-tuple-element.133), channel_id=1, source_target_pairs={{0,3},{1,0},{2,1},{3,2},{4,7},{5,4},{6,5},{7,6},{8,11},{9,8},{10,9... | collective-permute-start | bytes 147464 | tf_op jit(solution)/shard_map/ppermute | solution.py:36
  125.7 3.8 %collective-permute-start.22 = (bf16[128,768]{1,0:T(8,128)(2,1)S(1)}, bf16[128,768]{1,0:T(8,128)(2,1)S(1)}, u32[]{:S(2)}, u32[]{:S(2)}) collective-permute-start(bf16[128,768]{1,0:T(8,128)(2,1)S(1)} %copy-done.44), channel_id=1, source_target_pairs={{0,3},{1,0},{2,1},{3,2},{4,7},{5,4},{6,5},{7,6},{8,11},{9,8},{10,9... | collective-permute-start | bytes 589832 | tf_op jit(solution)/shard_map/ppermute | solution.py:36
  129.5 6.2 %shard_map.303 = (bf16[4,96,2304]{2,1,0:T(8,128)(2,1)}, f32[2,96,2304]{2,1,0:T(8,128)}, f32[2,96,2304]{2,1,0:T(8,128)}) custom-call(s32[1]{0:T(128)} %bitcast.2.refs_0_.index, bf16[512,768]{1,0:T(8,128)(2,1)} %get-tuple-element.127.refs_1_, bf16[512,768]{1,0:T(8,128)(2,1)} %get-tuple-element.118.hidden_back.refs_2_, bf16[128,768]{1,0:T(8,128)(2,1)} %refs_3_.1, ...), custom_call_target="tpu_custom_call" | custom-call | flops 30000001024 | tf_op jit(solution)/shard_map/pallas_call | solution.py:367
  136.8 2.4 %shard_map.304 = (bf16[512,384]{1,0:T(8,128)(2,1)}, f32[192,512]{1,0:T(8,128)}) custom-call(s32[2]{0:T(128)} %pad_add_fusion.place, bf16[512,192]{1,0:T(8,128)(2,1)} %get-tuple-element.98.query, bf16[192,128]{1,0:T(8,128)(2,1)} %get-tuple-element.125.g0, bf16[192,128]{1,0:T(8,128)(2,1)} %copy-done.52, bf16[192,128]{1,0:T(8,128)(2,1)} %copy-done.53, ...), custom_call_target="tpu_custom_call" | custom-call | flops 30000001024 | tf_op jit(solution)/shard_map/pallas_call | solution.py:367
  141.9 2.9 %shard_map.305 = (bf16[512,384]{1,0:T(8,128)(2,1)}, f32[192,512]{1,0:T(8,128)}) custom-call(s32[2]{0:T(128)} %pad_add_fusion.place, bf16[512,192]{1,0:T(8,128)(2,1)} %get-tuple-element.98.query, bf16[192,128]{1,0:T(8,128)(2,1)} %get-tuple-element.125.g0, bf16[192,128]{1,0:T(8,128)(2,1)} %copy-done.52, bf16[192,128]{1,0:T(8,128)(2,1)} %copy-done.53, ...), custom_call_target="tpu_custom_call" | custom-call | flops 30000001024 | tf_op jit(solution)/shard_map/pallas_call | solution.py:367
  144.9 9.2 %collective-permute-start.29 = (bf16[512,384]{1,0:T(8,128)(2,1)}, bf16[512,384]{1,0:T(8,128)(2,1)S(1)}, u32[]{:S(2)}, u32[]{:S(2)}) collective-permute-start(bf16[512,384]{1,0:T(8,128)(2,1)} %get-tuple-element.149), channel_id=1, source_target_pairs={{0,8},{4,12},{8,0},{12,4},{1,9},{5,13},{9,1},{13,5},{2,10},{6,14},... | collective-permute-start | bytes 1179656 | tf_op jit(solution)/shard_map/ppermute | solution.py:45
  154.2 5.3 %shard_map.306 = (bf16[512,384]{1,0:T(8,128)(2,1)}, bf16[512,384]{1,0:T(8,128)(2,1)}, bf16[512,192]{1,0:T(8,128)(2,1)}) custom-call(s32[2]{0:T(128)} %pad_add_fusion.place, bf16[512,192]{1,0:T(8,128)(2,1)} %get-tuple-element.98.query, bf16[192,128]{1,0:T(8,128)(2,1)} %get-tuple-element.125.g0, bf16[192,128]{1,0:T(8,128)(2,1)} %copy-done.52, ...), custom_call_target="tpu_custom_call" | custom-call | flops 30000001024 | tf_op jit(solution)/shard_map/pallas_call | solution.py:367
  159.5 2.1 collective-permute-start.28
  161.7 1.5 collective-permute-start.31
  164.7 4.8 %shard_map.307 = (f32[128,768]{1,0:T(8,128)}, bf16[128,768]{1,0:T(8,128)(2,1)}, bf16[256,768]{1,0:T(8,128)(2,1)}, bf16[128,768]{1,0:T(8,128)(2,1)}, bf16[4,112,6...) custom-call(s32[1]{0:T(128)} %bitcast.2.refs_0_.index, ...), custom_call_target="tpu_custom_call" | custom-call | flops 30000001024 | tf_op jit(solution)/shard_map/pallas_call | solution.py:367
  169.6 5.1 %collective-permute-done.31 = bf16[2,96,2304]{2,1,0:T(8,128)(2,1)S(1)} collective-permute-done((bf16[2,96,2304]{2,1,0:T(8,128)(2,1)S(1)}, bf16[2,96,2304]{2,1,0:T(8,128)(2,1)S(1)}, u32[]{:S(2)}, u32[]{:S(2)}) %collective-permute-start.31) | collective-permute-done | bytes 884768 | tf_op jit(solution)/shard_map/ppermute | solution.py:51
  176.0 1.6 collective-permute-start.34
  179.0 1.5 collective-permute-start.37
  180.5 1.5 collective-permute-start.36
  182.0 1.9 collective-permute-start.30
  183.9 1.8 collective-permute-done.34
  188.6 3.4 %collective-permute-done.35 = bf16[112,640]{1,0:T(8,128)(2,1)S(1)} collective-permute-done((bf16[112,640]{1,0:T(8,128)(2,1)S(1)}, bf16[112,640]{1,0:T(8,128)(2,1)S(1)}, u32[]{:S(2)}, u32[]{:S(2)}) %collective-permute-start.35) | collective-permute-done | bytes 143392 | tf_op jit(solution)/shard_map/ppermute | solution.py:51
  194.7 2.0 collective-permute-start.39
  196.7 1.8 collective-permute-start.38
  198.5 3.6 %collective-permute-start.40 = (bf16[112,192]{1,0:T(8,128)(2,1)S(1)}, bf16[112,192]{1,0:T(8,128)(2,1)S(1)}, u32[]{:S(2)}, u32[]{:S(2)}) collective-permute-start(bf16[112,192]{1,0:T(8,128)(2,1)S(1)} %get-tuple-element.226), channel_id=1, source_target_pairs={{0,1},{1,2},{2,3},{3,0},{4,5},{5,6},{6,7},{7,4},{8,9},{9,10},{10,1... | collective-permute-start | bytes 129032 | tf_op jit(solution)/shard_map/ppermute | solution.py:36
  202.2 4.7 %collective-permute-done.36.n2 = bf16[256,768]{1,0:T(8,128)(2,1)} collective-permute-done((bf16[256,768]{1,0:T(8,128)(2,1)}, bf16[256,768]{1,0:T(8,128)(2,1)}, u32[]{:S(2)}, u32[]{:S(2)}) %collective-permute-start.36) | collective-permute-done | bytes 393248 | tf_op jit(solution)/shard_map/ppermute | solution.py:36
  208.2 3.1 %shard_map.308 = (bf16[128,768]{1,0:T(8,128)(2,1)}, bf16[128,768]{1,0:T(8,128)(2,1)}) custom-call(s32[2]{0:T(128)} %pad_add_fusion.place, f32[128,768]{1,0:T(8,128)} %get-tuple-element.156.normed_own, bf16[128,768]{1,0:T(8,128)(2,1)} %collective-permute-done.30.n1, bf16[256,768]{1,0:T(8,128)(2,1)} %collective-permute-done.36.n2, ...), custom_call_target="tpu_custom_call" | custom-call | flops 30000001024 | tf_op jit(solution)/shard_map/pallas_call | solution.py:367
  (229 shorter events, 38.4 us)
Async XLA Ops:
  0.7 30.9 %copy-start.20 = (bf16[768,96]{0,1:T(8,128)(2,1)S(1)}, bf16[768,96]{0,1:T(8,128)(2,1)}, u32[]{:S(2)}) copy-start(bf16[768,96]{0,1:T(8,128)(2,1)} %param.23) | copy-start | bytes 442372
  0.7 30.9 %copy-start.7 = (bf16[96,768]{1,0:T(8,128)(2,1)S(1)}, bf16[96,768]{1,0:T(8,128)(2,1)}, u32[]{:S(2)}) copy-start(bf16[96,768]{1,0:T(8,128)(2,1)} %param.22) | copy-start | bytes 442372
  2.7 11.1 %collective-permute-start = (bf16[160,768]{1,0:T(8,128)(2,1)S(1)}, bf16[160,768]{1,0:T(8,128)(2,1)S(1)}, u32[]{:S(2)}, u32[]{:S(2)}) collective-permute-start(bf16[160,768]{1,0:T(8,128)(2,1)S(1)} %pad_maximum_fusion.4), channel_id=1, source_target_pairs={{0,1},{1,2},{2,3},{3,0},{4,5},{5,6},{6,7},{7,4},{8,9},{9,10},{10,1... | collective-permute-start | bytes 737288 | tf_op jit(solution)/shard_map/ppermute | solution.py:36
  13.7 18.0 %copy-start.21 = (bf16[160,768]{1,0:T(8,128)(2,1)}, bf16[160,768]{1,0:T(8,128)(2,1)S(1)}, u32[]{:S(2)}) copy-start(bf16[160,768]{1,0:T(8,128)(2,1)S(1)} %collective-permute-done.t1) | copy-start | bytes 737284
  13.7 8.7 %collective-permute-start.2 = (bf16[160,768]{1,0:T(8,128)(2,1)S(1)}, bf16[160,768]{1,0:T(8,128)(2,1)S(1)}, u32[]{:S(2)}, u32[]{:S(2)}) collective-permute-start(bf16[160,768]{1,0:T(8,128)(2,1)S(1)} %pad_maximum_fusion.4), channel_id=1, source_target_pairs={{0,3},{1,0},{2,1},{3,2},{4,7},{5,4},{6,5},{7,6},{8,11},{9,8},{10,9... | collective-permute-start | bytes 737288 | tf_op jit(solution)/shard_map/ppermute | solution.py:36
  17.2 5.2 %collective-permute-start.1 = (bf16[112,576]{1,0:T(8,128)(2,1)S(1)}, bf16[112,576]{1,0:T(8,128)(2,1)S(1)}, u32[]{:S(2)}, u32[]{:S(2)}) collective-permute-start(bf16[112,576]{1,0:T(8,128)(2,1)S(1)} %fusion.6.own), channel_id=1, source_target_pairs={{0,16},{4,12},{8,24},{12,4},{16,0},{20,28},{24,8},{28,20},{1,17},{... | collective-permute-start | bytes 387080 | tf_op jit(solution)/shard_map/ppermute | solution.py:51
  18.8 12.4 %collective-permute-start.4 = (bf16[160,768]{1,0:T(8,128)(2,1)S(1)}, bf16[160,768]{1,0:T(8,128)(2,1)S(1)}, u32[]{:S(2)}, u32[]{:S(2)}) collective-permute-start(bf16[160,768]{1,0:T(8,128)(2,1)S(1)} %pad_maximum_fusion.4), channel_id=1, source_target_pairs={{0,2},{1,3},{2,0},{3,1},{4,6},{5,7},{6,4},{7,5},{8,10},{9,11},{10,... | collective-permute-start | bytes 737288 | tf_op jit(solution)/shard_map/ppermute | solution.py:36
  22.4 8.7 %collective-permute-start.3 = (bf16[2,112,576]{2,1,0:T(8,128)(2,1)S(1)}, bf16[2,112,576]{2,1,0:T(8,128)(2,1)S(1)}, u32[]{:S(2)}, u32[]{:S(2)}) collective-permute-start(bf16[2,112,576]{2,1,0:T(8,128)(2,1)S(1)} %pad_maximum_fusion.3), channel_id=1, source_target_pairs={{0,8},{4,20},{8,0},{12,28},{16,24},{20,4},{24,16},{28,12},{1,9},{5... | collective-permute-start | bytes 774152 | tf_op jit(solution)/shard_map/ppermute | solution.py:51
  31.3 2.0 collective-permute-start.5
  31.7 31.6 %copy-start = (bf16[96,2304]{1,0:T(8,128)(2,1)}, bf16[96,2304]{1,0:T(8,128)(2,1)S(1)}, u32[]{:S(2)}) copy-start(bf16[96,2304]{1,0:T(8,128)(2,1)S(1)} %concatenate.60.refs_1_) | copy-start | bytes 1327108
  31.7 11.1 %collective-permute-start.12 = (bf16[96,2304]{1,0:T(8,128)(2,1)S(1)}, bf16[96,2304]{1,0:T(8,128)(2,1)S(1)}, u32[]{:S(2)}, u32[]{:S(2)}) collective-permute-start(bf16[96,2304]{1,0:T(8,128)(2,1)S(1)} %concatenate.60.refs_1_), channel_id=1, source_target_pairs={{0,16},{4,12},{8,24},{12,4},{16,0},{20,28},{24,8},{28,20},{1,17},{... | collective-permute-start | bytes 1327112 | tf_op jit(solution)/shard_map/ppermute | solution.py:51
  38.0 6.5 %collective-permute-start.7 = (bf16[512,384]{1,0:T(8,128)(2,1)}, bf16[512,384]{1,0:T(8,128)(2,1)S(1)}, u32[]{:S(2)}, u32[]{:S(2)}) collective-permute-start(bf16[512,384]{1,0:T(8,128)(2,1)} %get-tuple-element.99.kv_own), channel_id=1, source_target_pairs={{0,4},{4,0},{8,12},{12,8},{1,5},{5,1},{9,13},{13,9},{2,6},{6,2},{1... | collective-permute-start | bytes 1179656 | tf_op jit(solution)/shard_map/ppermute | solution.py:45
  38.7 10.2 %collective-permute-start.10 = (bf16[128,768]{1,0:T(8,128)(2,1)S(1)}, bf16[128,768]{1,0:T(8,128)(2,1)S(1)}, u32[]{:S(2)}, u32[]{:S(2)}) collective-permute-start(bf16[128,768]{1,0:T(8,128)(2,1)S(1)} %copy-done.38), channel_id=1, source_target_pairs={{0,3},{1,0},{2,1},{3,2},{4,7},{5,4},{6,5},{7,6},{8,11},{9,8},{10,9... | collective-permute-start | bytes 589832 | tf_op jit(solution)/shard_map/ppermute | solution.py:36
  42.3 10.0 %collective-permute-start.8 = (bf16[128,768]{1,0:T(8,128)(2,1)S(1)}, bf16[128,768]{1,0:T(8,128)(2,1)S(1)}, u32[]{:S(2)}, u32[]{:S(2)}) collective-permute-start(bf16[128,768]{1,0:T(8,128)(2,1)S(1)} %copy-done.38), channel_id=1, source_target_pairs={{0,1},{1,2},{2,3},{3,0},{4,5},{5,6},{6,7},{7,4},{8,9},{9,10},{10,1... | collective-permute-start | bytes 589832 | tf_op jit(solution)/shard_map/ppermute | solution.py:36
  42.3 16.4 %collective-permute-start.9 = (bf16[128,768]{1,0:T(8,128)(2,1)S(1)}, bf16[128,768]{1,0:T(8,128)(2,1)S(1)}, u32[]{:S(2)}, u32[]{:S(2)}) collective-permute-start(bf16[128,768]{1,0:T(8,128)(2,1)S(1)} %copy-done.38), channel_id=1, source_target_pairs={{0,2},{1,3},{2,0},{3,1},{4,6},{5,7},{6,4},{7,5},{8,10},{9,11},{10,... | collective-permute-start | bytes 589832 | tf_op jit(solution)/shard_map/ppermute | solution.py:36
  42.8 20.4 %copy-start.2 = (bf16[96,2304]{1,0:T(8,128)(2,1)}, bf16[96,2304]{1,0:T(8,128)(2,1)S(1)}, u32[]{:S(2)}) copy-start(bf16[96,2304]{1,0:T(8,128)(2,1)S(1)} %collective-permute-done.12.refs_2_) | copy-start | bytes 1327108
  42.9 15.7 %collective-permute-start.6 = (bf16[512,384]{1,0:T(8,128)(2,1)S(1)}, bf16[512,384]{1,0:T(8,128)(2,1)S(1)}, u32[]{:S(2)}, u32[]{:S(2)}) collective-permute-start(bf16[512,384]{1,0:T(8,128)(2,1)S(1)} %copy-done.31), channel_id=1, source_target_pairs={{0,8},{4,12},{8,0},{12,4},{1,9},{5,13},{9,1},{13,5},{2,10},{6,14},... | collective-permute-start | bytes 1179656 | tf_op jit(solution)/shard_map/ppermute | solution.py:45
  44.5 18.8 %collective-permute-start.13 = (bf16[2,96,2304]{2,1,0:T(8,128)(2,1)S(1)}, bf16[2,96,2304]{2,1,0:T(8,128)(2,1)S(1)}, u32[]{:S(2)}, u32[]{:S(2)}) collective-permute-start(bf16[2,96,2304]{2,1,0:T(8,128)(2,1)S(1)} %pad_maximum_fusion.1), channel_id=1, source_target_pairs={{0,8},{4,20},{8,0},{12,28},{16,24},{20,4},{24,16},{28,12},{1,9},{5... | collective-permute-start | bytes 2654216 | tf_op jit(solution)/shard_map/ppermute | solution.py:51
  58.6 2.9 %collective-permute-start.11 = (bf16[512,384]{1,0:T(8,128)(2,1)S(1)}, bf16[512,384]{1,0:T(8,128)(2,1)S(1)}, u32[]{:S(2)}, u32[]{:S(2)}) collective-permute-start(bf16[512,384]{1,0:T(8,128)(2,1)S(1)} %collective-permute-done.6.kv_y), channel_id=1, source_target_pairs={{0,4},{4,0},{8,12},{12,8},{1,5},{5,1},{9,13},{13,9},{2,6},{6,2},{1... | collective-permute-start | bytes 1179656 | tf_op jit(solution)/shard_map/ppermute | solution.py:45
  64.3 8.1 %collective-permute-start.17 = (bf16[4,96,2304]{2,1,0:T(8,128)(2,1)S(1)}, bf16[4,96,2304]{2,1,0:T(8,128)(2,1)S(1)}, u32[]{:S(2)}, u32[]{:S(2)}) collective-permute-start(bf16[4,96,2304]{2,1,0:T(8,128)(2,1)S(1)} %pad_maximum_fusion), channel_id=1, source_target_pairs={{0,4},{4,0},{8,12},{12,8},{16,20},{20,16},{24,28},{28,24},{1,5},{5... | collective-permute-start | bytes 5308424 | tf_op jit(solution)/shard_map/ppermute | solution.py:51
  66.5 11.2 %collective-permute-start.14 = (bf16[192,512]{1,0:T(8,128)(2,1)}, bf16[192,512]{1,0:T(8,128)(2,1)S(1)}, u32[]{:S(2)}, u32[]{:S(2)}) collective-permute-start(bf16[192,512]{1,0:T(8,128)(2,1)} %get-tuple-element.109.m0), channel_id=1, source_target_pairs={{0,1},{1,2},{2,3},{3,0},{4,5},{5,6},{6,7},{7,4},{8,9},{9,10},{10,1... | collective-permute-start | bytes 589832 | tf_op jit(solution)/shard_map/ppermute | solution.py:36
  70.0 14.3 %collective-permute-start.15 = (bf16[192,512]{1,0:T(8,128)(2,1)}, bf16[192,512]{1,0:T(8,128)(2,1)S(1)}, u32[]{:S(2)}, u32[]{:S(2)}) collective-permute-start(bf16[192,512]{1,0:T(8,128)(2,1)} %get-tuple-element.109.m0), channel_id=1, source_target_pairs={{0,2},{1,3},{2,0},{3,1},{4,6},{5,7},{6,4},{7,5},{8,10},{9,11},{10,... | collective-permute-start | bytes 589832 | tf_op jit(solution)/shard_map/ppermute | solution.py:36
  70.3 14.0 %collective-permute-start.16 = (bf16[192,512]{1,0:T(8,128)(2,1)}, bf16[192,512]{1,0:T(8,128)(2,1)S(1)}, u32[]{:S(2)}, u32[]{:S(2)}) collective-permute-start(bf16[192,512]{1,0:T(8,128)(2,1)} %get-tuple-element.109.m0), channel_id=1, source_target_pairs={{0,3},{1,0},{2,1},{3,2},{4,7},{5,4},{6,5},{7,6},{8,11},{9,8},{10,9... | collective-permute-start | bytes 589832 | tf_op jit(solution)/shard_map/ppermute | solution.py:36
  92.6 12.1 %collective-permute-start.18 = (bf16[128,768]{1,0:T(8,128)(2,1)}, bf16[128,768]{1,0:T(8,128)(2,1)S(1)}, u32[]{:S(2)}, u32[]{:S(2)}) collective-permute-start(bf16[128,768]{1,0:T(8,128)(2,1)} %get-tuple-element.121), channel_id=1, source_target_pairs={{0,3},{1,0},{2,1},{3,2},{4,7},{5,4},{6,5},{7,6},{8,11},{9,8},{10,9... | collective-permute-start | bytes 589832 | tf_op jit(solution)/shard_map/ppermute | solution.py:36
  99.0 17.3 %collective-permute-start.19 = (bf16[128,768]{1,0:T(8,128)(2,1)}, bf16[128,768]{1,0:T(8,128)(2,1)S(1)}, u32[]{:S(2)}, u32[]{:S(2)}) collective-permute-start(bf16[128,768]{1,0:T(8,128)(2,1)} %get-tuple-element.122), channel_id=1, source_target_pairs={{0,2},{1,3},{2,0},{3,1},{4,6},{5,7},{6,4},{7,5},{8,10},{9,11},{10,... | collective-permute-start | bytes 589832 | tf_op jit(solution)/shard_map/ppermute | solution.py:36
  99.0 17.3 %collective-permute-start.20 = (bf16[128,768]{1,0:T(8,128)(2,1)}, bf16[128,768]{1,0:T(8,128)(2,1)S(1)}, u32[]{:S(2)}, u32[]{:S(2)}) collective-permute-start(bf16[128,768]{1,0:T(8,128)(2,1)} %get-tuple-element.123), channel_id=1, source_target_pairs={{0,1},{1,2},{2,3},{3,0},{4,5},{5,6},{6,7},{7,4},{8,9},{9,10},{10,1... | collective-permute-start | bytes 589832 | tf_op jit(solution)/shard_map/ppermute | solution.py:36
  120.4 15.3 %collective-permute-start.21 = (bf16[192,128]{1,0:T(8,128)(2,1)}, bf16[192,128]{1,0:T(8,128)(2,1)S(1)}, u32[]{:S(2)}, u32[]{:S(2)}) collective-permute-start(bf16[192,128]{1,0:T(8,128)(2,1)} %get-tuple-element.126), channel_id=1, source_target_pairs={{0,1},{1,2},{2,3},{3,0},{4,5},{5,6},{6,7},{7,4},{8,9},{9,10},{10,1... | collective-permute-start | bytes 147464 | tf_op jit(solution)/shard_map/ppermute | solution.py:36
  120.9 15.1 %collective-permute-start.24 = (bf16[192,128]{1,0:T(8,128)(2,1)}, bf16[192,128]{1,0:T(8,128)(2,1)S(1)}, u32[]{:S(2)}, u32[]{:S(2)}) collective-permute-start(bf16[192,128]{1,0:T(8,128)(2,1)} %get-tuple-element.134), channel_id=1, source_target_pairs={{0,2},{1,3},{2,0},{3,1},{4,6},{5,7},{6,4},{7,5},{8,10},{9,11},{10,... | collective-permute-start | bytes 147464 | tf_op jit(solution)/shard_map/ppermute | solution.py:36
  122.8 13.3 %collective-permute-start.25 = (bf16[192,128]{1,0:T(8,128)(2,1)}, bf16[192,128]{1,0:T(8,128)(2,1)S(1)}, u32[]{:S(2)}, u32[]{:S(2)}) collective-permute-start(bf16[192,128]{1,0:T(8,128)(2,1)} %get-tuple-element.133), channel_id=1, source_target_pairs={{0,3},{1,0},{2,1},{3,2},{4,7},{5,4},{6,5},{7,6},{8,11},{9,8},{10,9... | collective-permute-start | bytes 147464 | tf_op jit(solution)/shard_map/ppermute | solution.py:36
  125.6 10.0 %collective-permute-start.23 = (bf16[128,768]{1,0:T(8,128)(2,1)S(1)}, bf16[128,768]{1,0:T(8,128)(2,1)S(1)}, u32[]{:S(2)}, u32[]{:S(2)}) collective-permute-start(bf16[128,768]{1,0:T(8,128)(2,1)S(1)} %copy-done.45), channel_id=1, source_target_pairs={{0,1},{1,2},{2,3},{3,0},{4,5},{5,6},{6,7},{7,4},{8,9},{9,10},{10,1... | collective-permute-start | bytes 589832 | tf_op jit(solution)/shard_map/ppermute | solution.py:36
  125.7 10.4 %collective-permute-start.22 = (bf16[128,768]{1,0:T(8,128)(2,1)S(1)}, bf16[128,768]{1,0:T(8,128)(2,1)S(1)}, u32[]{:S(2)}, u32[]{:S(2)}) collective-permute-start(bf16[128,768]{1,0:T(8,128)(2,1)S(1)} %copy-done.44), channel_id=1, source_target_pairs={{0,3},{1,0},{2,1},{3,2},{4,7},{5,4},{6,5},{7,6},{8,11},{9,8},{10,9... | collective-permute-start | bytes 589832 | tf_op jit(solution)/shard_map/ppermute | solution.py:36
  139.2 2.0 collective-permute-start.27
  139.3 14.8 %collective-permute-start.26 = (bf16[4,96,2304]{2,1,0:T(8,128)(2,1)S(1)}, bf16[4,96,2304]{2,1,0:T(8,128)(2,1)S(1)}, u32[]{:S(2)}, u32[]{:S(2)}) collective-permute-start(bf16[4,96,2304]{2,1,0:T(8,128)(2,1)S(1)} %copy-done.28), channel_id=1, source_target_pairs={{0,4},{4,0},{8,12},{12,8},{16,20},{20,16},{24,28},{28,24},{1,5},{5... | collective-permute-start | bytes 5308424 | tf_op jit(solution)/shard_map/ppermute | solution.py:51
  144.9 18.9 %collective-permute-start.29 = (bf16[512,384]{1,0:T(8,128)(2,1)}, bf16[512,384]{1,0:T(8,128)(2,1)S(1)}, u32[]{:S(2)}, u32[]{:S(2)}) collective-permute-start(bf16[512,384]{1,0:T(8,128)(2,1)} %get-tuple-element.149), channel_id=1, source_target_pairs={{0,8},{4,12},{8,0},{12,4},{1,9},{5,13},{9,1},{13,5},{2,10},{6,14},... | collective-permute-start | bytes 1179656 | tf_op jit(solution)/shard_map/ppermute | solution.py:45
  154.1 23.6 %copy-start.3 = (bf16[4,96,2304]{2,1,0:T(8,128)(2,1)}, bf16[4,96,2304]{2,1,0:T(8,128)(2,1)S(1)}, u32[]{:S(2)}) copy-start(bf16[4,96,2304]{2,1,0:T(8,128)(2,1)S(1)} %collective-permute-done.26) | copy-start | bytes 5308420
  159.5 4.3 %collective-permute-start.28 = (bf16[512,384]{1,0:T(8,128)(2,1)}, bf16[512,384]{1,0:T(8,128)(2,1)S(1)}, u32[]{:S(2)}, u32[]{:S(2)}) collective-permute-start(bf16[512,384]{1,0:T(8,128)(2,1)} %get-tuple-element.148), channel_id=1, source_target_pairs={{0,4},{4,0},{8,12},{12,8},{1,5},{5,1},{9,13},{13,9},{2,6},{6,2},{1... | collective-permute-start | bytes 1179656 | tf_op jit(solution)/shard_map/ppermute | solution.py:45
  161.7 13.0 %collective-permute-start.31 = (bf16[2,96,2304]{2,1,0:T(8,128)(2,1)S(1)}, bf16[2,96,2304]{2,1,0:T(8,128)(2,1)S(1)}, u32[]{:S(2)}, u32[]{:S(2)}) collective-permute-start(bf16[2,96,2304]{2,1,0:T(8,128)(2,1)S(1)} %add_convert_fusion), channel_id=1, source_target_pairs={{0,16},{4,12},{8,24},{12,4},{16,0},{20,28},{24,8},{28,20},{1,17},{... | collective-permute-start | bytes 2654216 | tf_op jit(solution)/shard_map/ppermute | solution.py:51
  169.5 16.2 %copy-start.10 = (f32[2,112,640]{2,1,0:T(8,128)S(1)}, f32[2,112,640]{2,1,0:T(8,128)}, u32[]{:S(2)}) copy-start(f32[2,112,640]{2,1,0:T(8,128)} %get-tuple-element.161) | copy-start | bytes 1720324
  169.5 5.2 %collective-permute-start.33 = (bf16[4,112,640]{2,1,0:T(8,128)(2,1)}, bf16[4,112,640]{2,1,0:T(8,128)(2,1)S(1)}, u32[]{:S(2)}, u32[]{:S(2)}) collective-permute-start(bf16[4,112,640]{2,1,0:T(8,128)(2,1)} %get-tuple-element.159), channel_id=1, source_target_pairs={{0,4},{4,0},{8,12},{12,8},{16,20},{20,16},{24,28},{28,24},{1,5},{5... | collective-permute-start | bytes 1720328 | tf_op jit(solution)/shard_map/ppermute | solution.py:51
  176.0 9.7 %collective-permute-start.34 = (bf16[2,112,640]{2,1,0:T(8,128)(2,1)S(1)}, bf16[2,112,640]{2,1,0:T(8,128)(2,1)}, u32[]{:S(2)}, u32[]{:S(2)}) collective-permute-start(bf16[2,112,640]{2,1,0:T(8,128)(2,1)S(1)} %add_convert_fusion.2), channel_id=1, source_target_pairs={{0,16},{4,12},{8,24},{12,4},{16,0},{20,28},{24,8},{28,20},{1,17},{... | collective-permute-start | bytes 860168 | tf_op jit(solution)/shard_map/ppermute | solution.py:51
  178.5 8.6 %collective-permute-start.32 = (bf16[96,2304]{1,0:T(8,128)(2,1)}, bf16[96,2304]{1,0:T(8,128)(2,1)}, u32[]{:S(2)}, u32[]{:S(2)}) collective-permute-start(bf16[96,2304]{1,0:T(8,128)(2,1)} %fusion), channel_id=1, source_target_pairs={{0,8},{4,20},{8,0},{12,28},{16,24},{20,4},{24,16},{28,12},{1,9},{5... | collective-permute-start | bytes 1327112 | tf_op jit(solution)/shard_map/ppermute | solution.py:51
  179.0 19.6 %collective-permute-start.37 = (bf16[128,768]{1,0:T(8,128)(2,1)}, bf16[128,768]{1,0:T(8,128)(2,1)}, u32[]{:S(2)}, u32[]{:S(2)}) collective-permute-start(bf16[128,768]{1,0:T(8,128)(2,1)} %get-tuple-element.166), channel_id=1, source_target_pairs={{0,1},{1,2},{2,3},{3,0},{4,5},{5,6},{6,7},{7,4},{8,9},{9,10},{10,1... | collective-permute-start | bytes 589832 | tf_op jit(solution)/shard_map/ppermute | solution.py:36
  180.5 26.4 %collective-permute-start.36 = (bf16[256,768]{1,0:T(8,128)(2,1)}, bf16[256,768]{1,0:T(8,128)(2,1)}, u32[]{:S(2)}, u32[]{:S(2)}) collective-permute-start(bf16[256,768]{1,0:T(8,128)(2,1)} %get-tuple-element.164), channel_id=1, source_target_pairs={{0,2},{1,3},{2,0},{3,1},{4,6},{5,7},{6,4},{7,5},{8,10},{9,11},{10,... | collective-permute-start | bytes 1179656 | tf_op jit(solution)/shard_map/ppermute | solution.py:36
  182.0 25.6 %collective-permute-start.30 = (bf16[128,768]{1,0:T(8,128)(2,1)}, bf16[128,768]{1,0:T(8,128)(2,1)}, u32[]{:S(2)}, u32[]{:S(2)}) collective-permute-start(bf16[128,768]{1,0:T(8,128)(2,1)} %get-tuple-element.157), channel_id=1, source_target_pairs={{0,3},{1,0},{2,1},{3,2},{4,7},{5,4},{6,5},{7,6},{8,11},{9,8},{10,9... | collective-permute-start | bytes 589832 | tf_op jit(solution)/shard_map/ppermute | solution.py:36
  186.8 5.2 %collective-permute-start.35 = (bf16[112,640]{1,0:T(8,128)(2,1)S(1)}, bf16[112,640]{1,0:T(8,128)(2,1)S(1)}, u32[]{:S(2)}, u32[]{:S(2)}) collective-permute-start(bf16[112,640]{1,0:T(8,128)(2,1)S(1)} %fusion.7), channel_id=1, source_target_pairs={{0,8},{4,20},{8,0},{12,28},{16,24},{20,4},{24,16},{28,12},{1,9},{5... | collective-permute-start | bytes 430088 | tf_op jit(solution)/shard_map/ppermute | solution.py:51
  194.7 17.5 %collective-permute-start.39 = (bf16[112,192]{1,0:T(8,128)(2,1)S(1)}, bf16[112,192]{1,0:T(8,128)(2,1)S(1)}, u32[]{:S(2)}, u32[]{:S(2)}) collective-permute-start(bf16[112,192]{1,0:T(8,128)(2,1)S(1)} %get-tuple-element.227), channel_id=1, source_target_pairs={{0,2},{1,3},{2,0},{3,1},{4,6},{5,7},{6,4},{7,5},{8,10},{9,11},{10,... | collective-permute-start | bytes 129032 | tf_op jit(solution)/shard_map/ppermute | solution.py:36
  196.7 15.6 %collective-permute-start.38 = (bf16[112,192]{1,0:T(8,128)(2,1)S(1)}, bf16[112,192]{1,0:T(8,128)(2,1)S(1)}, u32[]{:S(2)}, u32[]{:S(2)}) collective-permute-start(bf16[112,192]{1,0:T(8,128)(2,1)S(1)} %get-tuple-element.228), channel_id=1, source_target_pairs={{0,3},{1,0},{2,1},{3,2},{4,7},{5,4},{6,5},{7,6},{8,11},{9,8},{10,9... | collective-permute-start | bytes 129032 | tf_op jit(solution)/shard_map/ppermute | solution.py:36
  198.5 13.9 %collective-permute-start.40 = (bf16[112,192]{1,0:T(8,128)(2,1)S(1)}, bf16[112,192]{1,0:T(8,128)(2,1)S(1)}, u32[]{:S(2)}, u32[]{:S(2)}) collective-permute-start(bf16[112,192]{1,0:T(8,128)(2,1)S(1)} %get-tuple-element.226), channel_id=1, source_target_pairs={{0,1},{1,2},{2,3},{3,0},{4,5},{5,6},{6,7},{7,4},{8,9},{9,10},{10,1... | collective-permute-start | bytes 129032 | tf_op jit(solution)/shard_map/ppermute | solution.py:36
  (48 other events, 268.0 us)

commit v4 on v3

--- a/solution.py
+++ b/solution.py
@@ -812,7 +812,6 @@
         [active, down_t, hidden_back] + cotangent_slots,
         [((1, units), f32), ((1, model), f32), slab] + slabs,
     )
-    second_own = after(second_own, outside_own)
 
     middle_back, branch_back, *mixed_back_t = on_core(
         branch_kernel,
@@ -886,10 +885,10 @@
 
     if paired():
         near_got = cube_swapped(near_sent, 1, 1)
-        wide_more = after(wide_more, near_sent)
+        near_next = (near_high + near_got[2:].astype(f32)).astype(bf16)
+        wide_more = after(wide_more, near_next)
         wide_last = wide_low_part[1] + wide_got[1].astype(f32) + wide_more[1].astype(f32)
         wide_end = cube_swapped(wide_last.astype(bf16), 2, 4)
-        near_next = (near_high + near_got[2:].astype(f32)).astype(bf16)
         near_more = cube_swapped(near_next, 4, 2)
         near_last = near_low[1] + near_got[1].astype(f32) + near_more[1].astype(f32)
         near_end = cube_swapped(near_last.astype(bf16), 2, 4)

time: 217 us -> 215 us (level)
  other arithmetic: 11.9 us -> 14.7 us
    ppermute x23, starting transfers between devices: 43.4 us -> 39.9 us  [passed_along(): lax.ppermute(array, 'uly', [(i, (i + by) % peers) for i in range(peers)])]
    ppermute x23, waiting for transfers between devices: 46.9 us -> 44.4 us  [passed_along(): lax.ppermute(array, 'uly', [(i, (i + by) % peers) for i in range(peers)])]
    unnamed x112 -> x108, local copies, waits for them, and re-layouts: 8.63 us -> 8.57 us
  transfers between devices with their start and end apart: 41 -> 41, of which waited for: 18 -> 20; matrix products, arithmetic and copies ran while one was open for 8% -> 10% of each run, Pallas kernels for 18% -> 16%
where the time goes in v4:
time: 215 us; the launch traced here: 214 us
  starting transfers between devices  64.3 us (30%)
  waiting for transfers between devices  63.1 us (29%)
  Pallas kernels  52.5 us (24%)
  local copies, waits for them, and re-layouts  18.1 us (8%)
  other arithmetic  14.7 us (7%)
    pallas_call x13, Pallas kernels, on_core(): pl.pallas_call(kernel, out_shape=[jax.ShapeDtypeStruct(shape, dtype) for...  52.5 us
    ppermute x23, waiting for transfers between devices, passed_along(): lax.ppermute(array, 'uly', [(i, (i + by) % peers) for i in range(peers)])  44.4 us
    ppermute x23, starting transfers between devices, passed_along(): lax.ppermute(array, 'uly', [(i, (i + by) % peers) for i in range(peers)])  39.9 us
    ppermute x12, waiting for transfers between devices, cube_swapped(): return lax.ppermute(array, CUBE, pairs)  15.8 us
    ppermute x6, starting transfers between devices, blk_swapped(): return lax.ppermute(array, 'blk', [(i, i ^ flip) for i in range(peers)])  13.3 us
    ppermute x12, starting transfers between devices, cube_swapped(): return lax.ppermute(array, CUBE, pairs)  11.2 us
    unnamed x108, local copies, waits for them, and re-layouts  8.57 us
  transfers between devices with their start and end apart: 41, of which 20 were waited for; matrix products, arithmetic and copies ran while one was open for 10% of the time, Pallas kernels for 16%

profile of v4, /device:TPU:0, one launch (start us, length us, event | category | flops | bytes accessed | tf_op | source)
XLA Modules:
  0.0 214.1 jit_solution(16909661207077689731)
XLA Ops:
  2.7 3.1 %collective-permute-start = (bf16[160,768]{1,0:T(8,128)(2,1)S(1)}, bf16[160,768]{1,0:T(8,128)(2,1)S(1)}, u32[]{:S(2)}, u32[]{:S(2)}) collective-permute-start(bf16[160,768]{1,0:T(8,128)(2,1)S(1)} %pad_maximum_fusion.4), channel_id=1, source_target_pairs={{0,1},{1,2},{2,3},{3,0},{4,5},{5,6},{6,7},{7,4},{8,9},{9,10},{10,1... | collective-permute-start | bytes 737288 | tf_op jit(solution)/shard_map/ppermute | solution.py:36
  8.0 5.7 %collective-permute-done.t1 = bf16[160,768]{1,0:T(8,128)(2,1)S(1)} collective-permute-done((bf16[160,768]{1,0:T(8,128)(2,1)S(1)}, bf16[160,768]{1,0:T(8,128)(2,1)S(1)}, u32[]{:S(2)}, u32[]{:S(2)}) %collective-permute-start) | collective-permute-done | bytes 245792 | tf_op jit(solution)/shard_map/ppermute | solution.py:36
  13.7 1.7 collective-permute-start.2
  17.2 1.6 collective-permute-start.1
  18.8 3.6 %collective-permute-done.1.first = bf16[112,576]{1,0:T(8,128)(2,1)S(1)} collective-permute-done((bf16[112,576]{1,0:T(8,128)(2,1)S(1)}, bf16[112,576]{1,0:T(8,128)(2,1)S(1)}, u32[]{:S(2)}, u32[]{:S(2)}) %collective-permute-start.1) | collective-permute-done | bytes 129056 | tf_op jit(solution)/shard_map/ppermute | solution.py:51
  22.4 1.6 collective-permute-start.3
  24.7 6.5 %collective-permute-done.4.t2 = bf16[160,768]{1,0:T(8,128)(2,1)S(1)} collective-permute-done((bf16[160,768]{1,0:T(8,128)(2,1)S(1)}, bf16[160,768]{1,0:T(8,128)(2,1)S(1)}, u32[]{:S(2)}, u32[]{:S(2)}) %collective-permute-start.4) | collective-permute-done | bytes 245792 | tf_op jit(solution)/shard_map/ppermute | solution.py:36
  31.7 1.6 collective-permute-start.12
  33.5 3.8 %shard_map.296 = (bf16[768,576]{1,0:T(8,128)(2,1)}, f32[16,768]{1,0:T(8,128)}, f32[1,768]{1,0:T(1,128)}, bf16[512,192]{1,0:T(8,128)(2,1)}, bf16[512,384]{1,0:T(8,128)(2,1)}, /*index=5*/bf16[512,768]{1,0:T(8,128)(2,1)}) custom-call(s32[2]{0:T(128)} %pad_add_fusion.1.index, bf16[112,576]{1,0:T(8,128)(2,1)} %copy-done.5, bf16[112,576]{1,0:T(8,128)(2,1)} %copy-done.9, ...), custom_call_target="tpu_custom_call" | custom-call | flops 30000001024 | tf_op jit(solution)/shard_map/pallas_call | solution.py:367
  38.0 3.5 %collective-permute-start.10 = (bf16[128,768]{1,0:T(8,128)(2,1)S(1)}, bf16[128,768]{1,0:T(8,128)(2,1)S(1)}, u32[]{:S(2)}, u32[]{:S(2)}) collective-permute-start(bf16[128,768]{1,0:T(8,128)(2,1)S(1)} %copy-done.36), channel_id=1, source_target_pairs={{0,3},{1,0},{2,1},{3,2},{4,7},{5,4},{6,5},{7,6},{8,11},{9,8},{10,9... | collective-permute-start | bytes 589832 | tf_op jit(solution)/shard_map/ppermute | solution.py:36
  42.2 1.6 collective-permute-start.6
  44.5 3.7 %shard_map.297 = (f32[8,512]{1,0:T(8,128)}, f32[8,512]{1,0:T(8,128)}, f32[192,512]{1,0:T(8,128)}) custom-call(s32[2]{0:T(128)} %pad_add_fusion.place, bf16[512,192]{1,0:T(8,128)(2,1)} %get-tuple-element.97.query, bf16[512,384]{1,0:T(8,128)(2,1)} %get-tuple-element.98.kv_own, bf16[512,384]{1,0:T(8,128)(2,1)} %copy-done.30), custom_call_target="tpu_custom_call" | custom-call | flops 30000001024 | tf_op jit(solution)/shard_map/pallas_call | solution.py:367
  48.2 3.3 %collective-permute-done.8.c1.refs_4_ = bf16[128,768]{1,0:T(8,128)(2,1)S(1)} collective-permute-done((bf16[128,768]{1,0:T(8,128)(2,1)S(1)}, bf16[128,768]{1,0:T(8,128)(2,1)S(1)}, u32[]{:S(2)}, u32[]{:S(2)}) %collective-permute-start.8) | collective-permute-done | bytes 196640 | tf_op jit(solution)/shard_map/ppermute | solution.py:36
  51.5 6.4 %collective-permute-done.9.c2.refs_5_ = bf16[128,768]{1,0:T(8,128)(2,1)S(1)} collective-permute-done((bf16[128,768]{1,0:T(8,128)(2,1)S(1)}, bf16[128,768]{1,0:T(8,128)(2,1)S(1)}, u32[]{:S(2)}, u32[]{:S(2)}) %collective-permute-start.9) | collective-permute-done | bytes 196640 | tf_op jit(solution)/shard_map/ppermute | solution.py:36
  60.9 1.7 collective-permute-done.13.refs_3_
  63.6 2.2 %shard_map.298 = (bf16[192,512]{1,0:T(8,128)(2,1)}, f32[192,512]{1,0:T(8,128)}, f32[8,512]{1,0:T(8,128)}) custom-call(s32[2]{0:T(128)} %pad_add_fusion.place, bf16[512,192]{1,0:T(8,128)(2,1)} %get-tuple-element.97.query, bf16[512,384]{1,0:T(8,128)(2,1)} %copy-done.31, bf16[512,384]{1,0:T(8,128)(2,1)} %copy-done.32, f32[8,512]{1,0:T(8,128)} %get-tuple-element.99.top_in, ...), custom_call_target="tpu_custom_call" | custom-call | flops 30000001024 | tf_op jit(solution)/shard_map/pallas_call | solution.py:367
  65.8 3.5 %collective-permute-start.14 = (bf16[192,512]{1,0:T(8,128)(2,1)}, bf16[192,512]{1,0:T(8,128)(2,1)S(1)}, u32[]{:S(2)}, u32[]{:S(2)}) collective-permute-start(bf16[192,512]{1,0:T(8,128)(2,1)} %get-tuple-element.108.m0), channel_id=1, source_target_pairs={{0,1},{1,2},{2,3},{3,0},{4,5},{5,6},{6,7},{7,4},{8,9},{9,10},{10,1... | collective-permute-start | bytes 589832 | tf_op jit(solution)/shard_map/ppermute | solution.py:36
  69.6 2.1 collective-permute-start.16
  72.9 4.1 %shard_map.299 = (bf16[8,96,768]{2,1,0:T(8,128)(2,1)}, bf16[8,96,768]{2,1,0:T(8,128)(2,1)}, bf16[8,96,768]{2,1,0:T(8,128)(2,1)}) custom-call(s32[1]{0:T(128)} %bitcast.2.refs_0_.index, bf16[96,2304]{1,0:T(8,128)(2,1)} %copy-done, bf16[96,2304]{1,0:T(8,128)(2,1)} %copy-done.2, bf16[2,96,2304]{2,1,0:T(8,128)(2,1)} %copy-done.6, bf16[4,96,2304]{2,1,0:T(8,128)(2,1)} %copy-done.28), custom_call_target="tpu_custom_call" | custom-call | flops 30000001024 | tf_op jit(solution)/shard_map/pallas_call | solution.py:367
  77.0 6.6 %collective-permute-done.15.m2 = bf16[192,512]{1,0:T(8,128)(2,1)S(1)} collective-permute-done((bf16[192,512]{1,0:T(8,128)(2,1)}, bf16[192,512]{1,0:T(8,128)(2,1)S(1)}, u32[]{:S(2)}, u32[]{:S(2)}) %collective-permute-start.15) | collective-permute-done | bytes 196640 | tf_op jit(solution)/shard_map/ppermute | solution.py:36
  84.4 7.5 %shard_map.300 = (f32[128,768]{1,0:T(8,128)}, bf16[512,768]{1,0:T(8,128)(2,1)}, bf16[768,128]{1,0:T(8,128)(2,1)}, bf16[512,768]{1,0:T(8,128)(2,1)}, bf16[512,768...) custom-call(s32[2]{0:T(128)} %pad_add_fusion.place, ...), custom_call_target="tpu_custom_call" | custom-call | flops 30000001024 | tf_op jit(solution)/shard_map/pallas_call | solution.py:367
  91.9 6.5 %collective-permute-start.18 = (bf16[128,768]{1,0:T(8,128)(2,1)}, bf16[128,768]{1,0:T(8,128)(2,1)S(1)}, u32[]{:S(2)}, u32[]{:S(2)}) collective-permute-start(bf16[128,768]{1,0:T(8,128)(2,1)} %get-tuple-element.116), channel_id=1, source_target_pairs={{0,3},{1,0},{2,1},{3,2},{4,7},{5,4},{6,5},{7,6},{8,11},{9,8},{10,9... | collective-permute-start | bytes 589832 | tf_op jit(solution)/shard_map/ppermute | solution.py:36
  99.0 3.7 %shard_map.303 = (f32[1,768]{1,0:T(1,128)}, f32[1,768]{1,0:T(1,128)}, f32[128,768]{1,0:T(8,128)}, bf16[128,768]{1,0:T(8,128)(2,1)}, bf16[128,768]{1,0:T(8,128)(2,1)}, /*index=5*/bf16[128,768]{1,0:T(8,128)(2,1)}) custom-call(s32[2]{0:T(128)} %pad_add_fusion.place, bf16[512,768]{1,0:T(8,128)(2,1)} %get-tuple-element.124.refs_7_.active, ...), custom_call_target="tpu_custom_call" | custom-call | flops 30000001024 | tf_op jit(solution)/shard_map/pallas_call | solution.py:367
  104.0 11.7 %collective-permute-done.19.r2 = bf16[128,768]{1,0:T(8,128)(2,1)S(1)} collective-permute-done((bf16[128,768]{1,0:T(8,128)(2,1)}, bf16[128,768]{1,0:T(8,128)(2,1)S(1)}, u32[]{:S(2)}, u32[]{:S(2)}) %collective-permute-start.19) | collective-permute-done | bytes 196640 | tf_op jit(solution)/shard_map/ppermute | solution.py:36
  116.4 3.3 %shard_map.301 = (f32[128,768]{1,0:T(8,128)}, bf16[128,768]{1,0:T(8,128)(2,1)}, bf16[192,128]{1,0:T(8,128)(2,1)}, bf16[192,128]{1,0:T(8,128)(2,1)}, bf16[192,128]{1,0:T(8,128)(2,1)}, /*index=5*/bf16[192,128]{1,0:T(8,128)(2,1)}) custom-call(s32[2]{0:T(128)} %pad_add_fusion.place, f32[128,768]{1,0:T(8,128)} %get-tuple-element.115.part_own, ...), custom_call_target="tpu_custom_call" | custom-call | flops 30000001024 | tf_op jit(solution)/shard_map/pallas_call | solution.py:367
  120.2 1.9 collective-permute-start.24
  122.1 2.9 %collective-permute-start.25 = (bf16[192,128]{1,0:T(8,128)(2,1)}, bf16[192,128]{1,0:T(8,128)(2,1)S(1)}, u32[]{:S(2)}, u32[]{:S(2)}) collective-permute-start(bf16[192,128]{1,0:T(8,128)(2,1)} %get-tuple-element.130), channel_id=1, source_target_pairs={{0,3},{1,0},{2,1},{3,2},{4,7},{5,4},{6,5},{7,6},{8,11},{9,8},{10,9... | collective-permute-start | bytes 147464 | tf_op jit(solution)/shard_map/ppermute | solution.py:36
  125.0 3.8 %collective-permute-start.22 = (bf16[128,768]{1,0:T(8,128)(2,1)S(1)}, bf16[128,768]{1,0:T(8,128)(2,1)S(1)}, u32[]{:S(2)}, u32[]{:S(2)}) collective-permute-start(bf16[128,768]{1,0:T(8,128)(2,1)S(1)} %copy-done.42), channel_id=1, source_target_pairs={{0,3},{1,0},{2,1},{3,2},{4,7},{5,4},{6,5},{7,6},{8,11},{9,8},{10,9... | collective-permute-start | bytes 589832 | tf_op jit(solution)/shard_map/ppermute | solution.py:36
  128.8 6.2 %shard_map.302 = (bf16[4,96,2304]{2,1,0:T(8,128)(2,1)}, f32[2,96,2304]{2,1,0:T(8,128)}, f32[2,96,2304]{2,1,0:T(8,128)}) custom-call(s32[1]{0:T(128)} %bitcast.2.refs_0_.index, bf16[512,768]{1,0:T(8,128)(2,1)} %get-tuple-element.122.refs_1_, bf16[512,768]{1,0:T(8,128)(2,1)} %get-tuple-element.123.refs_2_.hidden_back, bf16[128,768]{1,0:T(8,128)(2,1)} %c0.3, ...), custom_call_target="tpu_custom_call" | custom-call | flops 30000001024 | tf_op jit(solution)/shard_map/pallas_call | solution.py:367
  136.1 2.4 %shard_map.304 = (bf16[512,384]{1,0:T(8,128)(2,1)}, f32[192,512]{1,0:T(8,128)}) custom-call(s32[2]{0:T(128)} %pad_add_fusion.place, bf16[512,192]{1,0:T(8,128)(2,1)} %get-tuple-element.97.query, bf16[192,128]{1,0:T(8,128)(2,1)} %get-tuple-element.120.g0, bf16[192,128]{1,0:T(8,128)(2,1)} %copy-done.50, bf16[192,128]{1,0:T(8,128)(2,1)} %copy-done.51, ...), custom_call_target="tpu_custom_call" | custom-call | flops 30000001024 | tf_op jit(solution)/shard_map/pallas_call | solution.py:367
  141.2 2.9 %shard_map.305 = (bf16[512,384]{1,0:T(8,128)(2,1)}, f32[192,512]{1,0:T(8,128)}) custom-call(s32[2]{0:T(128)} %pad_add_fusion.place, bf16[512,192]{1,0:T(8,128)(2,1)} %get-tuple-element.97.query, bf16[192,128]{1,0:T(8,128)(2,1)} %get-tuple-element.120.g0, bf16[192,128]{1,0:T(8,128)(2,1)} %copy-done.50, bf16[192,128]{1,0:T(8,128)(2,1)} %copy-done.51, ...), custom_call_target="tpu_custom_call" | custom-call | flops 30000001024 | tf_op jit(solution)/shard_map/pallas_call | solution.py:367
  144.2 9.2 %collective-permute-start.29 = (bf16[512,384]{1,0:T(8,128)(2,1)}, bf16[512,384]{1,0:T(8,128)(2,1)S(1)}, u32[]{:S(2)}, u32[]{:S(2)}) collective-permute-start(bf16[512,384]{1,0:T(8,128)(2,1)} %get-tuple-element.146), channel_id=1, source_target_pairs={{0,8},{4,12},{8,0},{12,4},{1,9},{5,13},{9,1},{13,5},{2,10},{6,14},... | collective-permute-start | bytes 1179656 | tf_op jit(solution)/shard_map/ppermute | solution.py:45
  154.5 4.8 %shard_map.306 = (bf16[512,384]{1,0:T(8,128)(2,1)}, bf16[512,384]{1,0:T(8,128)(2,1)}, bf16[512,192]{1,0:T(8,128)(2,1)}) custom-call(s32[2]{0:T(128)} %pad_add_fusion.place, bf16[512,192]{1,0:T(8,128)(2,1)} %get-tuple-element.97.query, bf16[192,128]{1,0:T(8,128)(2,1)} %get-tuple-element.120.g0, bf16[192,128]{1,0:T(8,128)(2,1)} %copy-done.50, ...), custom_call_target="tpu_custom_call" | custom-call | flops 30000001024 | tf_op jit(solution)/shard_map/pallas_call | solution.py:367
  159.4 2.2 %collective-permute-start.28 = (bf16[512,384]{1,0:T(8,128)(2,1)}, bf16[512,384]{1,0:T(8,128)(2,1)S(1)}, u32[]{:S(2)}, u32[]{:S(2)}) collective-permute-start(bf16[512,384]{1,0:T(8,128)(2,1)} %get-tuple-element.145), channel_id=1, source_target_pairs={{0,4},{4,0},{8,12},{12,8},{1,5},{5,1},{9,13},{13,9},{2,6},{6,2},{1... | collective-permute-start | bytes 1179656 | tf_op jit(solution)/shard_map/ppermute | solution.py:45
  163.9 4.7 %shard_map.307 = (f32[128,768]{1,0:T(8,128)}, bf16[128,768]{1,0:T(8,128)(2,1)}, bf16[256,768]{1,0:T(8,128)(2,1)}, bf16[128,768]{1,0:T(8,128)(2,1)}, bf16[4,112,6...) custom-call(s32[1]{0:T(128)} %bitcast.2.refs_0_.index, ...), custom_call_target="tpu_custom_call" | custom-call | flops 30000001024 | tf_op jit(solution)/shard_map/pallas_call | solution.py:367
  169.0 1.5 collective-permute-start.31
  171.6 1.8 add_convert_fusion.2
  176.6 1.5 collective-permute-start.36
  178.2 1.9 collective-permute-start.30
  180.0 2.3 %collective-permute-done.31 = bf16[2,96,2304]{2,1,0:T(8,128)(2,1)} collective-permute-done((bf16[2,96,2304]{2,1,0:T(8,128)(2,1)}, bf16[2,96,2304]{2,1,0:T(8,128)(2,1)}, u32[]{:S(2)}, u32[]{:S(2)}) %collective-permute-start.31) | collective-permute-done | bytes 884768 | tf_op jit(solution)/shard_map/ppermute | solution.py:51
  182.3 3.1 %collective-permute-done.34 = bf16[2,112,640]{2,1,0:T(8,128)(2,1)} collective-permute-done((bf16[2,112,640]{2,1,0:T(8,128)(2,1)}, bf16[2,112,640]{2,1,0:T(8,128)(2,1)}, u32[]{:S(2)}, u32[]{:S(2)}) %collective-permute-start.34) | collective-permute-done | bytes 286752 | tf_op jit(solution)/shard_map/ppermute | solution.py:51
  186.6 1.5 collective-permute-start.35
  188.1 1.9 fusion
  195.2 3.5 %collective-permute-done.33 = bf16[96,2304]{1,0:T(8,128)(2,1)} collective-permute-done((bf16[96,2304]{1,0:T(8,128)(2,1)}, bf16[96,2304]{1,0:T(8,128)(2,1)}, u32[]{:S(2)}, u32[]{:S(2)}) %collective-permute-start.33) | collective-permute-done | bytes 442400 | tf_op jit(solution)/shard_map/ppermute | solution.py:51
  201.4 2.0 collective-permute-start.39
  203.4 1.9 collective-permute-start.38
  205.4 3.1 %shard_map.308 = (bf16[128,768]{1,0:T(8,128)(2,1)}, bf16[128,768]{1,0:T(8,128)(2,1)}) custom-call(s32[2]{0:T(128)} %pad_add_fusion.place, f32[128,768]{1,0:T(8,128)} %get-tuple-element.153.normed_own, bf16[128,768]{1,0:T(8,128)(2,1)} %collective-permute-done.30.n1, bf16[256,768]{1,0:T(8,128)(2,1)} %collective-permute-done.36.n2, ...), custom_call_target="tpu_custom_call" | custom-call | flops 30000001024 | tf_op jit(solution)/shard_map/pallas_call | solution.py:367
  208.8 2.5 %collective-permute-done.40 = bf16[112,192]{1,0:T(8,128)(2,1)S(1)} collective-permute-done((bf16[112,192]{1,0:T(8,128)(2,1)S(1)}, bf16[112,192]{1,0:T(8,128)(2,1)S(1)}, u32[]{:S(2)}, u32[]{:S(2)}) %collective-permute-start.40) | collective-permute-done | bytes 43040 | tf_op jit(solution)/shard_map/ppermute | solution.py:36
  (225 shorter events, 42.9 us)
Async XLA Ops:
  0.7 30.9 %copy-start.19 = (bf16[768,96]{0,1:T(8,128)(2,1)S(1)}, bf16[768,96]{0,1:T(8,128)(2,1)}, u32[]{:S(2)}) copy-start(bf16[768,96]{0,1:T(8,128)(2,1)} %param.23) | copy-start | bytes 442372
  0.7 30.9 %copy-start.7 = (bf16[96,768]{1,0:T(8,128)(2,1)S(1)}, bf16[96,768]{1,0:T(8,128)(2,1)}, u32[]{:S(2)}) copy-start(bf16[96,768]{1,0:T(8,128)(2,1)} %param.22) | copy-start | bytes 442372
  2.7 11.1 %collective-permute-start = (bf16[160,768]{1,0:T(8,128)(2,1)S(1)}, bf16[160,768]{1,0:T(8,128)(2,1)S(1)}, u32[]{:S(2)}, u32[]{:S(2)}) collective-permute-start(bf16[160,768]{1,0:T(8,128)(2,1)S(1)} %pad_maximum_fusion.4), channel_id=1, source_target_pairs={{0,1},{1,2},{2,3},{3,0},{4,5},{5,6},{6,7},{7,4},{8,9},{9,10},{10,1... | collective-permute-start | bytes 737288 | tf_op jit(solution)/shard_map/ppermute | solution.py:36
  13.7 18.0 %copy-start.20 = (bf16[160,768]{1,0:T(8,128)(2,1)}, bf16[160,768]{1,0:T(8,128)(2,1)S(1)}, u32[]{:S(2)}) copy-start(bf16[160,768]{1,0:T(8,128)(2,1)S(1)} %collective-permute-done.t1) | copy-start | bytes 737284
  13.7 8.7 %collective-permute-start.2 = (bf16[160,768]{1,0:T(8,128)(2,1)S(1)}, bf16[160,768]{1,0:T(8,128)(2,1)S(1)}, u32[]{:S(2)}, u32[]{:S(2)}) collective-permute-start(bf16[160,768]{1,0:T(8,128)(2,1)S(1)} %pad_maximum_fusion.4), channel_id=1, source_target_pairs={{0,3},{1,0},{2,1},{3,2},{4,7},{5,4},{6,5},{7,6},{8,11},{9,8},{10,9... | collective-permute-start | bytes 737288 | tf_op jit(solution)/shard_map/ppermute | solution.py:36
  17.2 5.2 %collective-permute-start.1 = (bf16[112,576]{1,0:T(8,128)(2,1)S(1)}, bf16[112,576]{1,0:T(8,128)(2,1)S(1)}, u32[]{:S(2)}, u32[]{:S(2)}) collective-permute-start(bf16[112,576]{1,0:T(8,128)(2,1)S(1)} %fusion.6.own), channel_id=1, source_target_pairs={{0,16},{4,12},{8,24},{12,4},{16,0},{20,28},{24,8},{28,20},{1,17},{... | collective-permute-start | bytes 387080 | tf_op jit(solution)/shard_map/ppermute | solution.py:51
  18.8 12.4 %collective-permute-start.4 = (bf16[160,768]{1,0:T(8,128)(2,1)S(1)}, bf16[160,768]{1,0:T(8,128)(2,1)S(1)}, u32[]{:S(2)}, u32[]{:S(2)}) collective-permute-start(bf16[160,768]{1,0:T(8,128)(2,1)S(1)} %pad_maximum_fusion.4), channel_id=1, source_target_pairs={{0,2},{1,3},{2,0},{3,1},{4,6},{5,7},{6,4},{7,5},{8,10},{9,11},{10,... | collective-permute-start | bytes 737288 | tf_op jit(solution)/shard_map/ppermute | solution.py:36
  22.4 8.7 %collective-permute-start.3 = (bf16[2,112,576]{2,1,0:T(8,128)(2,1)S(1)}, bf16[2,112,576]{2,1,0:T(8,128)(2,1)S(1)}, u32[]{:S(2)}, u32[]{:S(2)}) collective-permute-start(bf16[2,112,576]{2,1,0:T(8,128)(2,1)S(1)} %pad_maximum_fusion.3), channel_id=1, source_target_pairs={{0,8},{4,20},{8,0},{12,28},{16,24},{20,4},{24,16},{28,12},{1,9},{5... | collective-permute-start | bytes 774152 | tf_op jit(solution)/shard_map/ppermute | solution.py:51
  31.3 2.2 %collective-permute-start.5 = (bf16[4,112,576]{2,1,0:T(8,128)(2,1)S(1)}, bf16[4,112,576]{2,1,0:T(8,128)(2,1)}, u32[]{:S(2)}, u32[]{:S(2)}) collective-permute-start(bf16[4,112,576]{2,1,0:T(8,128)(2,1)S(1)} %pad_maximum_fusion.2), channel_id=1, source_target_pairs={{0,4},{4,0},{8,12},{12,8},{16,20},{20,16},{24,28},{28,24},{1,5},{5... | collective-permute-start | bytes 1548296 | tf_op jit(solution)/shard_map/ppermute | solution.py:51
  31.7 30.8 %copy-start = (bf16[96,2304]{1,0:T(8,128)(2,1)}, bf16[96,2304]{1,0:T(8,128)(2,1)S(1)}, u32[]{:S(2)}) copy-start(bf16[96,2304]{1,0:T(8,128)(2,1)S(1)} %concatenate.60.refs_1_) | copy-start | bytes 1327108
  31.7 10.3 %collective-permute-start.12 = (bf16[96,2304]{1,0:T(8,128)(2,1)S(1)}, bf16[96,2304]{1,0:T(8,128)(2,1)S(1)}, u32[]{:S(2)}, u32[]{:S(2)}) collective-permute-start(bf16[96,2304]{1,0:T(8,128)(2,1)S(1)} %concatenate.60.refs_1_), channel_id=1, source_target_pairs={{0,16},{4,12},{8,24},{12,4},{16,0},{20,28},{24,8},{28,20},{1,17},{... | collective-permute-start | bytes 1327112 | tf_op jit(solution)/shard_map/ppermute | solution.py:51
  37.2 6.5 %collective-permute-start.7 = (bf16[512,384]{1,0:T(8,128)(2,1)}, bf16[512,384]{1,0:T(8,128)(2,1)S(1)}, u32[]{:S(2)}, u32[]{:S(2)}) collective-permute-start(bf16[512,384]{1,0:T(8,128)(2,1)} %get-tuple-element.98.kv_own), channel_id=1, source_target_pairs={{0,4},{4,0},{8,12},{12,8},{1,5},{5,1},{9,13},{13,9},{2,6},{6,2},{1... | collective-permute-start | bytes 1179656 | tf_op jit(solution)/shard_map/ppermute | solution.py:45
  38.0 10.2 %collective-permute-start.10 = (bf16[128,768]{1,0:T(8,128)(2,1)S(1)}, bf16[128,768]{1,0:T(8,128)(2,1)S(1)}, u32[]{:S(2)}, u32[]{:S(2)}) collective-permute-start(bf16[128,768]{1,0:T(8,128)(2,1)S(1)} %copy-done.36), channel_id=1, source_target_pairs={{0,3},{1,0},{2,1},{3,2},{4,7},{5,4},{6,5},{7,6},{8,11},{9,8},{10,9... | collective-permute-start | bytes 589832 | tf_op jit(solution)/shard_map/ppermute | solution.py:36
  41.5 10.0 %collective-permute-start.8 = (bf16[128,768]{1,0:T(8,128)(2,1)S(1)}, bf16[128,768]{1,0:T(8,128)(2,1)S(1)}, u32[]{:S(2)}, u32[]{:S(2)}) collective-permute-start(bf16[128,768]{1,0:T(8,128)(2,1)S(1)} %copy-done.36), channel_id=1, source_target_pairs={{0,1},{1,2},{2,3},{3,0},{4,5},{5,6},{6,7},{7,4},{8,9},{9,10},{10,1... | collective-permute-start | bytes 589832 | tf_op jit(solution)/shard_map/ppermute | solution.py:36
  41.5 16.4 %collective-permute-start.9 = (bf16[128,768]{1,0:T(8,128)(2,1)S(1)}, bf16[128,768]{1,0:T(8,128)(2,1)S(1)}, u32[]{:S(2)}, u32[]{:S(2)}) collective-permute-start(bf16[128,768]{1,0:T(8,128)(2,1)S(1)} %copy-done.36), channel_id=1, source_target_pairs={{0,2},{1,3},{2,0},{3,1},{4,6},{5,7},{6,4},{7,5},{8,10},{9,11},{10,... | collective-permute-start | bytes 589832 | tf_op jit(solution)/shard_map/ppermute | solution.py:36
  42.1 20.5 %copy-start.2 = (bf16[96,2304]{1,0:T(8,128)(2,1)}, bf16[96,2304]{1,0:T(8,128)(2,1)S(1)}, u32[]{:S(2)}) copy-start(bf16[96,2304]{1,0:T(8,128)(2,1)S(1)} %collective-permute-done.12.refs_2_) | copy-start | bytes 1327108
  42.2 15.8 %collective-permute-start.6 = (bf16[512,384]{1,0:T(8,128)(2,1)S(1)}, bf16[512,384]{1,0:T(8,128)(2,1)S(1)}, u32[]{:S(2)}, u32[]{:S(2)}) collective-permute-start(bf16[512,384]{1,0:T(8,128)(2,1)S(1)} %copy-done.29), channel_id=1, source_target_pairs={{0,8},{4,12},{8,0},{12,4},{1,9},{5,13},{9,1},{13,5},{2,10},{6,14},... | collective-permute-start | bytes 1179656 | tf_op jit(solution)/shard_map/ppermute | solution.py:45
  43.8 18.8 %collective-permute-start.13 = (bf16[2,96,2304]{2,1,0:T(8,128)(2,1)S(1)}, bf16[2,96,2304]{2,1,0:T(8,128)(2,1)S(1)}, u32[]{:S(2)}, u32[]{:S(2)}) collective-permute-start(bf16[2,96,2304]{2,1,0:T(8,128)(2,1)S(1)} %pad_maximum_fusion.1), channel_id=1, source_target_pairs={{0,8},{4,20},{8,0},{12,28},{16,24},{20,4},{24,16},{28,12},{1,9},{5... | collective-permute-start | bytes 2654216 | tf_op jit(solution)/shard_map/ppermute | solution.py:51
  57.9 2.9 %collective-permute-start.11 = (bf16[512,384]{1,0:T(8,128)(2,1)S(1)}, bf16[512,384]{1,0:T(8,128)(2,1)S(1)}, u32[]{:S(2)}, u32[]{:S(2)}) collective-permute-start(bf16[512,384]{1,0:T(8,128)(2,1)S(1)} %collective-permute-done.6.kv_y), channel_id=1, source_target_pairs={{0,4},{4,0},{8,12},{12,8},{1,5},{5,1},{9,13},{13,9},{2,6},{6,2},{1... | collective-permute-start | bytes 1179656 | tf_op jit(solution)/shard_map/ppermute | solution.py:45
  63.6 8.1 %collective-permute-start.17 = (bf16[4,96,2304]{2,1,0:T(8,128)(2,1)S(1)}, bf16[4,96,2304]{2,1,0:T(8,128)(2,1)S(1)}, u32[]{:S(2)}, u32[]{:S(2)}) collective-permute-start(bf16[4,96,2304]{2,1,0:T(8,128)(2,1)S(1)} %pad_maximum_fusion), channel_id=1, source_target_pairs={{0,4},{4,0},{8,12},{12,8},{16,20},{20,16},{24,28},{28,24},{1,5},{5... | collective-permute-start | bytes 5308424 | tf_op jit(solution)/shard_map/ppermute | solution.py:51
  65.8 11.2 %collective-permute-start.14 = (bf16[192,512]{1,0:T(8,128)(2,1)}, bf16[192,512]{1,0:T(8,128)(2,1)S(1)}, u32[]{:S(2)}, u32[]{:S(2)}) collective-permute-start(bf16[192,512]{1,0:T(8,128)(2,1)} %get-tuple-element.108.m0), channel_id=1, source_target_pairs={{0,1},{1,2},{2,3},{3,0},{4,5},{5,6},{6,7},{7,4},{8,9},{9,10},{10,1... | collective-permute-start | bytes 589832 | tf_op jit(solution)/shard_map/ppermute | solution.py:36
  69.3 14.3 %collective-permute-start.15 = (bf16[192,512]{1,0:T(8,128)(2,1)}, bf16[192,512]{1,0:T(8,128)(2,1)S(1)}, u32[]{:S(2)}, u32[]{:S(2)}) collective-permute-start(bf16[192,512]{1,0:T(8,128)(2,1)} %get-tuple-element.108.m0), channel_id=1, source_target_pairs={{0,2},{1,3},{2,0},{3,1},{4,6},{5,7},{6,4},{7,5},{8,10},{9,11},{10,... | collective-permute-start | bytes 589832 | tf_op jit(solution)/shard_map/ppermute | solution.py:36
  69.6 14.0 %collective-permute-start.16 = (bf16[192,512]{1,0:T(8,128)(2,1)}, bf16[192,512]{1,0:T(8,128)(2,1)S(1)}, u32[]{:S(2)}, u32[]{:S(2)}) collective-permute-start(bf16[192,512]{1,0:T(8,128)(2,1)} %get-tuple-element.108.m0), channel_id=1, source_target_pairs={{0,3},{1,0},{2,1},{3,2},{4,7},{5,4},{6,5},{7,6},{8,11},{9,8},{10,9... | collective-permute-start | bytes 589832 | tf_op jit(solution)/shard_map/ppermute | solution.py:36
  91.9 12.1 %collective-permute-start.18 = (bf16[128,768]{1,0:T(8,128)(2,1)}, bf16[128,768]{1,0:T(8,128)(2,1)S(1)}, u32[]{:S(2)}, u32[]{:S(2)}) collective-permute-start(bf16[128,768]{1,0:T(8,128)(2,1)} %get-tuple-element.116), channel_id=1, source_target_pairs={{0,3},{1,0},{2,1},{3,2},{4,7},{5,4},{6,5},{7,6},{8,11},{9,8},{10,9... | collective-permute-start | bytes 589832 | tf_op jit(solution)/shard_map/ppermute | solution.py:36
  98.4 17.3 %collective-permute-start.19 = (bf16[128,768]{1,0:T(8,128)(2,1)}, bf16[128,768]{1,0:T(8,128)(2,1)S(1)}, u32[]{:S(2)}, u32[]{:S(2)}) collective-permute-start(bf16[128,768]{1,0:T(8,128)(2,1)} %get-tuple-element.117), channel_id=1, source_target_pairs={{0,2},{1,3},{2,0},{3,1},{4,6},{5,7},{6,4},{7,5},{8,10},{9,11},{10,... | collective-permute-start | bytes 589832 | tf_op jit(solution)/shard_map/ppermute | solution.py:36
  98.4 17.3 %collective-permute-start.20 = (bf16[128,768]{1,0:T(8,128)(2,1)}, bf16[128,768]{1,0:T(8,128)(2,1)S(1)}, u32[]{:S(2)}, u32[]{:S(2)}) collective-permute-start(bf16[128,768]{1,0:T(8,128)(2,1)} %get-tuple-element.118), channel_id=1, source_target_pairs={{0,1},{1,2},{2,3},{3,0},{4,5},{5,6},{6,7},{7,4},{8,9},{9,10},{10,1... | collective-permute-start | bytes 589832 | tf_op jit(solution)/shard_map/ppermute | solution.py:36
  119.7 15.3 %collective-permute-start.21 = (bf16[192,128]{1,0:T(8,128)(2,1)}, bf16[192,128]{1,0:T(8,128)(2,1)S(1)}, u32[]{:S(2)}, u32[]{:S(2)}) collective-permute-start(bf16[192,128]{1,0:T(8,128)(2,1)} %get-tuple-element.121), channel_id=1, source_target_pairs={{0,1},{1,2},{2,3},{3,0},{4,5},{5,6},{6,7},{7,4},{8,9},{9,10},{10,1... | collective-permute-start | bytes 147464 | tf_op jit(solution)/shard_map/ppermute | solution.py:36
  120.2 15.1 %collective-permute-start.24 = (bf16[192,128]{1,0:T(8,128)(2,1)}, bf16[192,128]{1,0:T(8,128)(2,1)S(1)}, u32[]{:S(2)}, u32[]{:S(2)}) collective-permute-start(bf16[192,128]{1,0:T(8,128)(2,1)} %get-tuple-element.131), channel_id=1, source_target_pairs={{0,2},{1,3},{2,0},{3,1},{4,6},{5,7},{6,4},{7,5},{8,10},{9,11},{10,... | collective-permute-start | bytes 147464 | tf_op jit(solution)/shard_map/ppermute | solution.py:36
  122.1 13.3 %collective-permute-start.25 = (bf16[192,128]{1,0:T(8,128)(2,1)}, bf16[192,128]{1,0:T(8,128)(2,1)S(1)}, u32[]{:S(2)}, u32[]{:S(2)}) collective-permute-start(bf16[192,128]{1,0:T(8,128)(2,1)} %get-tuple-element.130), channel_id=1, source_target_pairs={{0,3},{1,0},{2,1},{3,2},{4,7},{5,4},{6,5},{7,6},{8,11},{9,8},{10,9... | collective-permute-start | bytes 147464 | tf_op jit(solution)/shard_map/ppermute | solution.py:36
  125.0 10.0 %collective-permute-start.23 = (bf16[128,768]{1,0:T(8,128)(2,1)S(1)}, bf16[128,768]{1,0:T(8,128)(2,1)S(1)}, u32[]{:S(2)}, u32[]{:S(2)}) collective-permute-start(bf16[128,768]{1,0:T(8,128)(2,1)S(1)} %copy-done.43), channel_id=1, source_target_pairs={{0,1},{1,2},{2,3},{3,0},{4,5},{5,6},{6,7},{7,4},{8,9},{9,10},{10,1... | collective-permute-start | bytes 589832 | tf_op jit(solution)/shard_map/ppermute | solution.py:36
  125.0 10.4 %collective-permute-start.22 = (bf16[128,768]{1,0:T(8,128)(2,1)S(1)}, bf16[128,768]{1,0:T(8,128)(2,1)S(1)}, u32[]{:S(2)}, u32[]{:S(2)}) collective-permute-start(bf16[128,768]{1,0:T(8,128)(2,1)S(1)} %copy-done.42), channel_id=1, source_target_pairs={{0,3},{1,0},{2,1},{3,2},{4,7},{5,4},{6,5},{7,6},{8,11},{9,8},{10,9... | collective-permute-start | bytes 589832 | tf_op jit(solution)/shard_map/ppermute | solution.py:36
  138.5 2.0 collective-permute-start.27
  138.6 14.8 %collective-permute-start.26 = (bf16[4,96,2304]{2,1,0:T(8,128)(2,1)S(1)}, bf16[4,96,2304]{2,1,0:T(8,128)(2,1)S(1)}, u32[]{:S(2)}, u32[]{:S(2)}) collective-permute-start(bf16[4,96,2304]{2,1,0:T(8,128)(2,1)S(1)} %copy-done.27), channel_id=1, source_target_pairs={{0,4},{4,0},{8,12},{12,8},{16,20},{20,16},{24,28},{28,24},{1,5},{5... | collective-permute-start | bytes 5308424 | tf_op jit(solution)/shard_map/ppermute | solution.py:51
  144.2 18.8 %collective-permute-start.29 = (bf16[512,384]{1,0:T(8,128)(2,1)}, bf16[512,384]{1,0:T(8,128)(2,1)S(1)}, u32[]{:S(2)}, u32[]{:S(2)}) collective-permute-start(bf16[512,384]{1,0:T(8,128)(2,1)} %get-tuple-element.146), channel_id=1, source_target_pairs={{0,8},{4,12},{8,0},{12,4},{1,9},{5,13},{9,1},{13,5},{2,10},{6,14},... | collective-permute-start | bytes 1179656 | tf_op jit(solution)/shard_map/ppermute | solution.py:45
  153.3 34.8 %copy-start.3 = (bf16[4,96,2304]{2,1,0:T(8,128)(2,1)}, bf16[4,96,2304]{2,1,0:T(8,128)(2,1)S(1)}, u32[]{:S(2)}) copy-start(bf16[4,96,2304]{2,1,0:T(8,128)(2,1)S(1)} %collective-permute-done.26) | copy-start | bytes 5308420
  159.4 3.7 %collective-permute-start.28 = (bf16[512,384]{1,0:T(8,128)(2,1)}, bf16[512,384]{1,0:T(8,128)(2,1)S(1)}, u32[]{:S(2)}, u32[]{:S(2)}) collective-permute-start(bf16[512,384]{1,0:T(8,128)(2,1)} %get-tuple-element.145), channel_id=1, source_target_pairs={{0,4},{4,0},{8,12},{12,8},{1,5},{5,1},{9,13},{13,9},{2,6},{6,2},{1... | collective-permute-start | bytes 1179656 | tf_op jit(solution)/shard_map/ppermute | solution.py:45
  168.6 19.5 %copy-start.1 = (f32[2,96,2304]{2,1,0:T(8,128)S(1)}, f32[2,96,2304]{2,1,0:T(8,128)}, u32[]{:S(2)}) copy-start(f32[2,96,2304]{2,1,0:T(8,128)} %get-tuple-element.155) | copy-start | bytes 5308420
  168.6 2.2 %collective-permute-start.32 = (bf16[4,112,640]{2,1,0:T(8,128)(2,1)}, bf16[4,112,640]{2,1,0:T(8,128)(2,1)S(1)}, u32[]{:S(2)}, u32[]{:S(2)}) collective-permute-start(bf16[4,112,640]{2,1,0:T(8,128)(2,1)} %get-tuple-element.157), channel_id=1, source_target_pairs={{0,4},{4,0},{8,12},{12,8},{16,20},{20,16},{24,28},{28,24},{1,5},{5... | collective-permute-start | bytes 1720328 | tf_op jit(solution)/shard_map/ppermute | solution.py:51
  169.0 13.4 %collective-permute-start.31 = (bf16[2,96,2304]{2,1,0:T(8,128)(2,1)}, bf16[2,96,2304]{2,1,0:T(8,128)(2,1)}, u32[]{:S(2)}, u32[]{:S(2)}) collective-permute-start(bf16[2,96,2304]{2,1,0:T(8,128)(2,1)} %add_convert_fusion), channel_id=1, source_target_pairs={{0,16},{4,12},{8,24},{12,4},{16,0},{20,28},{24,8},{28,20},{1,17},{... | collective-permute-start | bytes 2654216 | tf_op jit(solution)/shard_map/ppermute | solution.py:51
  173.5 12.0 %collective-permute-start.34 = (bf16[2,112,640]{2,1,0:T(8,128)(2,1)}, bf16[2,112,640]{2,1,0:T(8,128)(2,1)}, u32[]{:S(2)}, u32[]{:S(2)}) collective-permute-start(bf16[2,112,640]{2,1,0:T(8,128)(2,1)} %add_convert_fusion.2), channel_id=1, source_target_pairs={{0,16},{4,12},{8,24},{12,4},{16,0},{20,28},{24,8},{28,20},{1,17},{... | collective-permute-start | bytes 860168 | tf_op jit(solution)/shard_map/ppermute | solution.py:51
  175.1 30.1 %collective-permute-start.37 = (bf16[128,768]{1,0:T(8,128)(2,1)}, bf16[128,768]{1,0:T(8,128)(2,1)}, u32[]{:S(2)}, u32[]{:S(2)}) collective-permute-start(bf16[128,768]{1,0:T(8,128)(2,1)} %get-tuple-element.163), channel_id=1, source_target_pairs={{0,1},{1,2},{2,3},{3,0},{4,5},{5,6},{6,7},{7,4},{8,9},{9,10},{10,1... | collective-permute-start | bytes 589832 | tf_op jit(solution)/shard_map/ppermute | solution.py:36
  176.6 28.8 %collective-permute-start.36 = (bf16[256,768]{1,0:T(8,128)(2,1)}, bf16[256,768]{1,0:T(8,128)(2,1)}, u32[]{:S(2)}, u32[]{:S(2)}) collective-permute-start(bf16[256,768]{1,0:T(8,128)(2,1)} %get-tuple-element.161), channel_id=1, source_target_pairs={{0,2},{1,3},{2,0},{3,1},{4,6},{5,7},{6,4},{7,5},{8,10},{9,11},{10,... | collective-permute-start | bytes 1179656 | tf_op jit(solution)/shard_map/ppermute | solution.py:36
  178.2 27.3 %collective-permute-start.30 = (bf16[128,768]{1,0:T(8,128)(2,1)}, bf16[128,768]{1,0:T(8,128)(2,1)}, u32[]{:S(2)}, u32[]{:S(2)}) collective-permute-start(bf16[128,768]{1,0:T(8,128)(2,1)} %get-tuple-element.154), channel_id=1, source_target_pairs={{0,3},{1,0},{2,1},{3,2},{4,7},{5,4},{6,5},{7,6},{8,11},{9,8},{10,9... | collective-permute-start | bytes 589832 | tf_op jit(solution)/shard_map/ppermute | solution.py:36
  186.6 5.2 %collective-permute-start.35 = (bf16[112,640]{1,0:T(8,128)(2,1)S(1)}, bf16[112,640]{1,0:T(8,128)(2,1)S(1)}, u32[]{:S(2)}, u32[]{:S(2)}) collective-permute-start(bf16[112,640]{1,0:T(8,128)(2,1)S(1)} %fusion.7), channel_id=1, source_target_pairs={{0,8},{4,20},{8,0},{12,28},{16,24},{20,4},{24,16},{28,12},{1,9},{5... | collective-permute-start | bytes 430088 | tf_op jit(solution)/shard_map/ppermute | solution.py:51
  190.0 8.6 %collective-permute-start.33 = (bf16[96,2304]{1,0:T(8,128)(2,1)}, bf16[96,2304]{1,0:T(8,128)(2,1)}, u32[]{:S(2)}, u32[]{:S(2)}) collective-permute-start(bf16[96,2304]{1,0:T(8,128)(2,1)} %fusion), channel_id=1, source_target_pairs={{0,8},{4,20},{8,0},{12,28},{16,24},{20,4},{24,16},{28,12},{1,9},{5... | collective-permute-start | bytes 1327112 | tf_op jit(solution)/shard_map/ppermute | solution.py:51
  201.4 7.2 %collective-permute-start.39 = (bf16[112,192]{1,0:T(8,128)(2,1)S(1)}, bf16[112,192]{1,0:T(8,128)(2,1)S(1)}, u32[]{:S(2)}, u32[]{:S(2)}) collective-permute-start(bf16[112,192]{1,0:T(8,128)(2,1)S(1)} %get-tuple-element.225), channel_id=1, source_target_pairs={{0,2},{1,3},{2,0},{3,1},{4,6},{5,7},{6,4},{7,5},{8,10},{9,11},{10,... | collective-permute-start | bytes 129032 | tf_op jit(solution)/shard_map/ppermute | solution.py:36
  203.4 5.3 %collective-permute-start.38 = (bf16[112,192]{1,0:T(8,128)(2,1)S(1)}, bf16[112,192]{1,0:T(8,128)(2,1)S(1)}, u32[]{:S(2)}, u32[]{:S(2)}) collective-permute-start(bf16[112,192]{1,0:T(8,128)(2,1)S(1)} %get-tuple-element.226), channel_id=1, source_target_pairs={{0,3},{1,0},{2,1},{3,2},{4,7},{5,4},{6,5},{7,6},{8,11},{9,8},{10,9... | collective-permute-start | bytes 129032 | tf_op jit(solution)/shard_map/ppermute | solution.py:36
  205.3 6.0 %collective-permute-start.40 = (bf16[112,192]{1,0:T(8,128)(2,1)S(1)}, bf16[112,192]{1,0:T(8,128)(2,1)S(1)}, u32[]{:S(2)}, u32[]{:S(2)}) collective-permute-start(bf16[112,192]{1,0:T(8,128)(2,1)S(1)} %get-tuple-element.224), channel_id=1, source_target_pairs={{0,1},{1,2},{2,3},{3,0},{4,5},{5,6},{6,7},{7,4},{8,9},{9,10},{10,1... | collective-permute-start | bytes 129032 | tf_op jit(solution)/shard_map/ppermute | solution.py:36
  (46 other events, 269.2 us)

commit v5 on v4

--- a/solution.py
+++ b/solution.py
@@ -9,7 +9,7 @@
 CUBE = ("fsdp", "blk")
 VEC_ROWS = 16
 VMEM_LIMIT = 56 * 1024 * 1024
-KERNEL_COST = 30_000_000_000
+KERNEL_COST = 60_000_000_000
 
 KEY_GROUP, KEY_HALF = (0, 0, 1), (0, 1, 0)
 VALUE_GROUP, VALUE_HALF = (2, 2, 1), (0, 1, 1)

time: 215 us -> 216 us (level)
    unnamed x108 -> x110, local copies, waits for them, and re-layouts: 8.57 us -> 9.32 us
  transfers between devices with their start and end apart: 41 -> 41, of which waited for: 20 -> 19; matrix products, arithmetic and copies ran while one was open for 10% -> 10% of each run, Pallas kernels for 16% -> 16%
where the time goes in v5:
time: 216 us; the launch traced here: 215 us
  starting transfers between devices  64.3 us (30%)
  waiting for transfers between devices  63.1 us (29%)
  Pallas kernels  52.4 us (24%)
  local copies, waits for them, and re-layouts  18.9 us (9%)
  other arithmetic  14.7 us (7%)
    pallas_call x13, Pallas kernels, on_core(): pl.pallas_call(kernel, out_shape=[jax.ShapeDtypeStruct(shape, dtype) for...  52.4 us
    ppermute x23, waiting for transfers between devices, passed_along(): lax.ppermute(array, 'uly', [(i, (i + by) % peers) for i in range(peers)])  44.4 us
    ppermute x23, starting transfers between devices, passed_along(): lax.ppermute(array, 'uly', [(i, (i + by) % peers) for i in range(peers)])  39.9 us
    ppermute x12, waiting for transfers between devices, cube_swapped(): return lax.ppermute(array, CUBE, pairs)  15.7 us
    ppermute x6, starting transfers between devices, blk_swapped(): return lax.ppermute(array, 'blk', [(i, i ^ flip) for i in range(peers)])  13.2 us
    ppermute x12, starting transfers between devices, cube_swapped(): return lax.ppermute(array, CUBE, pairs)  11.2 us
    unnamed x110, local copies, waits for them, and re-layouts  9.32 us
  transfers between devices with their start and end apart: 41, of which 19 were waited for; matrix products, arithmetic and copies ran while one was open for 10% of the time, Pallas kernels for 16%

profile of v5, /device:TPU:0, one launch (start us, length us, event | category | flops | bytes accessed | tf_op | source)
XLA Modules:
  0.0 214.8 jit_solution(2198261126367769213)
XLA Ops:
  2.7 3.1 %collective-permute-start = (bf16[160,768]{1,0:T(8,128)(2,1)S(1)}, bf16[160,768]{1,0:T(8,128)(2,1)S(1)}, u32[]{:S(2)}, u32[]{:S(2)}) collective-permute-start(bf16[160,768]{1,0:T(8,128)(2,1)S(1)} %pad_maximum_fusion.4), channel_id=1, source_target_pairs={{0,1},{1,2},{2,3},{3,0},{4,5},{5,6},{6,7},{7,4},{8,9},{9,10},{10,1... | collective-permute-start | bytes 737288 | tf_op jit(solution)/shard_map/ppermute | solution.py:36
  8.0 5.7 %collective-permute-done.t1 = bf16[160,768]{1,0:T(8,128)(2,1)S(1)} collective-permute-done((bf16[160,768]{1,0:T(8,128)(2,1)S(1)}, bf16[160,768]{1,0:T(8,128)(2,1)S(1)}, u32[]{:S(2)}, u32[]{:S(2)}) %collective-permute-start) | collective-permute-done | bytes 245792 | tf_op jit(solution)/shard_map/ppermute | solution.py:36
  13.7 1.7 collective-permute-start.2
  17.2 1.6 collective-permute-start.1
  18.8 3.6 %collective-permute-done.1.first = bf16[112,576]{1,0:T(8,128)(2,1)S(1)} collective-permute-done((bf16[112,576]{1,0:T(8,128)(2,1)S(1)}, bf16[112,576]{1,0:T(8,128)(2,1)S(1)}, u32[]{:S(2)}, u32[]{:S(2)}) %collective-permute-start.1) | collective-permute-done | bytes 129056 | tf_op jit(solution)/shard_map/ppermute | solution.py:51
  22.4 1.6 collective-permute-start.3
  24.7 6.5 %collective-permute-done.4.t2 = bf16[160,768]{1,0:T(8,128)(2,1)S(1)} collective-permute-done((bf16[160,768]{1,0:T(8,128)(2,1)S(1)}, bf16[160,768]{1,0:T(8,128)(2,1)S(1)}, u32[]{:S(2)}, u32[]{:S(2)}) %collective-permute-start.4) | collective-permute-done | bytes 245792 | tf_op jit(solution)/shard_map/ppermute | solution.py:36
  31.7 1.6 collective-permute-start.12
  34.2 3.7 %shard_map.296 = (bf16[768,576]{1,0:T(8,128)(2,1)}, f32[16,768]{1,0:T(8,128)}, f32[1,768]{1,0:T(1,128)}, bf16[512,192]{1,0:T(8,128)(2,1)}, bf16[512,384]{1,0:T(8,128)(2,1)}, /*index=5*/bf16[512,768]{1,0:T(8,128)(2,1)}) custom-call(s32[2]{0:T(128)} %pad_add_fusion.1.index, bf16[112,576]{1,0:T(8,128)(2,1)} %copy-done.5, bf16[112,576]{1,0:T(8,128)(2,1)} %copy-done.9, ...), custom_call_target="tpu_custom_call" | custom-call | flops 60000002048 | tf_op jit(solution)/shard_map/pallas_call | solution.py:367
  38.7 3.5 %collective-permute-start.10 = (bf16[128,768]{1,0:T(8,128)(2,1)S(1)}, bf16[128,768]{1,0:T(8,128)(2,1)S(1)}, u32[]{:S(2)}, u32[]{:S(2)}) collective-permute-start(bf16[128,768]{1,0:T(8,128)(2,1)S(1)} %copy-done.37), channel_id=1, source_target_pairs={{0,3},{1,0},{2,1},{3,2},{4,7},{5,4},{6,5},{7,6},{8,11},{9,8},{10,9... | collective-permute-start | bytes 589832 | tf_op jit(solution)/shard_map/ppermute | solution.py:36
  42.9 1.5 collective-permute-start.6
  45.2 3.7 %shard_map.297 = (f32[8,512]{1,0:T(8,128)}, f32[8,512]{1,0:T(8,128)}, f32[192,512]{1,0:T(8,128)}) custom-call(s32[2]{0:T(128)} %pad_add_fusion.place, bf16[512,192]{1,0:T(8,128)(2,1)} %get-tuple-element.97.query, bf16[512,384]{1,0:T(8,128)(2,1)} %get-tuple-element.98.kv_own, bf16[512,384]{1,0:T(8,128)(2,1)} %copy-done.31), custom_call_target="tpu_custom_call" | custom-call | flops 60000002048 | tf_op jit(solution)/shard_map/pallas_call | solution.py:367
  48.9 3.3 %collective-permute-done.8.c1.refs_4_ = bf16[128,768]{1,0:T(8,128)(2,1)S(1)} collective-permute-done((bf16[128,768]{1,0:T(8,128)(2,1)S(1)}, bf16[128,768]{1,0:T(8,128)(2,1)S(1)}, u32[]{:S(2)}, u32[]{:S(2)}) %collective-permute-start.8) | collective-permute-done | bytes 196640 | tf_op jit(solution)/shard_map/ppermute | solution.py:36
  52.2 6.4 %collective-permute-done.9.c2.refs_5_ = bf16[128,768]{1,0:T(8,128)(2,1)S(1)} collective-permute-done((bf16[128,768]{1,0:T(8,128)(2,1)S(1)}, bf16[128,768]{1,0:T(8,128)(2,1)S(1)}, u32[]{:S(2)}, u32[]{:S(2)}) %collective-permute-start.9) | collective-permute-done | bytes 196640 | tf_op jit(solution)/shard_map/ppermute | solution.py:36
  59.5 1.5 fusion.23
  61.6 1.7 collective-permute-done.13.refs_3_
  64.3 2.2 %shard_map.298 = (bf16[192,512]{1,0:T(8,128)(2,1)}, f32[192,512]{1,0:T(8,128)}, f32[8,512]{1,0:T(8,128)}) custom-call(s32[2]{0:T(128)} %pad_add_fusion.place, bf16[512,192]{1,0:T(8,128)(2,1)} %get-tuple-element.97.query, bf16[512,384]{1,0:T(8,128)(2,1)} %copy-done.32, bf16[512,384]{1,0:T(8,128)(2,1)} %copy-done.33, f32[8,512]{1,0:T(8,128)} %get-tuple-element.99.top_in, ...), custom_call_target="tpu_custom_call" | custom-call | flops 60000002048 | tf_op jit(solution)/shard_map/pallas_call | solution.py:367
  66.5 3.5 %collective-permute-start.14 = (bf16[192,512]{1,0:T(8,128)(2,1)}, bf16[192,512]{1,0:T(8,128)(2,1)S(1)}, u32[]{:S(2)}, u32[]{:S(2)}) collective-permute-start(bf16[192,512]{1,0:T(8,128)(2,1)} %get-tuple-element.108.m0), channel_id=1, source_target_pairs={{0,1},{1,2},{2,3},{3,0},{4,5},{5,6},{6,7},{7,4},{8,9},{9,10},{10,1... | collective-permute-start | bytes 589832 | tf_op jit(solution)/shard_map/ppermute | solution.py:36
  70.3 2.1 collective-permute-start.16
  73.6 4.1 %shard_map.299 = (bf16[8,96,768]{2,1,0:T(8,128)(2,1)}, bf16[8,96,768]{2,1,0:T(8,128)(2,1)}, bf16[8,96,768]{2,1,0:T(8,128)(2,1)}) custom-call(s32[1]{0:T(128)} %bitcast.2.refs_0_.index, bf16[96,2304]{1,0:T(8,128)(2,1)} %copy-done, bf16[96,2304]{1,0:T(8,128)(2,1)} %copy-done.2, bf16[2,96,2304]{2,1,0:T(8,128)(2,1)} %copy-done.6, bf16[4,96,2304]{2,1,0:T(8,128)(2,1)} %copy-done.28), custom_call_target="tpu_custom_call" | custom-call | flops 60000002048 | tf_op jit(solution)/shard_map/pallas_call | solution.py:367
  77.7 6.7 %collective-permute-done.15.m2 = bf16[192,512]{1,0:T(8,128)(2,1)S(1)} collective-permute-done((bf16[192,512]{1,0:T(8,128)(2,1)}, bf16[192,512]{1,0:T(8,128)(2,1)S(1)}, u32[]{:S(2)}, u32[]{:S(2)}) %collective-permute-start.15) | collective-permute-done | bytes 196640 | tf_op jit(solution)/shard_map/ppermute | solution.py:36
  85.1 7.5 %shard_map.300 = (f32[128,768]{1,0:T(8,128)}, bf16[512,768]{1,0:T(8,128)(2,1)}, bf16[768,128]{1,0:T(8,128)(2,1)}, bf16[512,768]{1,0:T(8,128)(2,1)}, bf16[512,768...) custom-call(s32[2]{0:T(128)} %pad_add_fusion.place, ...), custom_call_target="tpu_custom_call" | custom-call | flops 60000002048 | tf_op jit(solution)/shard_map/pallas_call | solution.py:367
  92.6 6.5 %collective-permute-start.18 = (bf16[128,768]{1,0:T(8,128)(2,1)}, bf16[128,768]{1,0:T(8,128)(2,1)S(1)}, u32[]{:S(2)}, u32[]{:S(2)}) collective-permute-start(bf16[128,768]{1,0:T(8,128)(2,1)} %get-tuple-element.116), channel_id=1, source_target_pairs={{0,3},{1,0},{2,1},{3,2},{4,7},{5,4},{6,5},{7,6},{8,11},{9,8},{10,9... | collective-permute-start | bytes 589832 | tf_op jit(solution)/shard_map/ppermute | solution.py:36
  99.7 3.7 %shard_map.303 = (f32[1,768]{1,0:T(1,128)}, f32[1,768]{1,0:T(1,128)}, f32[128,768]{1,0:T(8,128)}, bf16[128,768]{1,0:T(8,128)(2,1)}, bf16[128,768]{1,0:T(8,128)(2,1)}, /*index=5*/bf16[128,768]{1,0:T(8,128)(2,1)}) custom-call(s32[2]{0:T(128)} %pad_add_fusion.place, bf16[512,768]{1,0:T(8,128)(2,1)} %get-tuple-element.124.refs_7_.active, ...), custom_call_target="tpu_custom_call" | custom-call | flops 60000002048 | tf_op jit(solution)/shard_map/pallas_call | solution.py:367
  104.7 11.7 %collective-permute-done.19.r2 = bf16[128,768]{1,0:T(8,128)(2,1)S(1)} collective-permute-done((bf16[128,768]{1,0:T(8,128)(2,1)}, bf16[128,768]{1,0:T(8,128)(2,1)S(1)}, u32[]{:S(2)}, u32[]{:S(2)}) %collective-permute-start.19) | collective-permute-done | bytes 196640 | tf_op jit(solution)/shard_map/ppermute | solution.py:36
  117.1 3.3 %shard_map.301 = (f32[128,768]{1,0:T(8,128)}, bf16[128,768]{1,0:T(8,128)(2,1)}, bf16[192,128]{1,0:T(8,128)(2,1)}, bf16[192,128]{1,0:T(8,128)(2,1)}, bf16[192,128]{1,0:T(8,128)(2,1)}, /*index=5*/bf16[192,128]{1,0:T(8,128)(2,1)}) custom-call(s32[2]{0:T(128)} %pad_add_fusion.place, f32[128,768]{1,0:T(8,128)} %get-tuple-element.115.part_own, ...), custom_call_target="tpu_custom_call" | custom-call | flops 60000002048 | tf_op jit(solution)/shard_map/pallas_call | solution.py:367
  120.9 1.9 collective-permute-start.24
  122.8 2.9 %collective-permute-start.25 = (bf16[192,128]{1,0:T(8,128)(2,1)}, bf16[192,128]{1,0:T(8,128)(2,1)S(1)}, u32[]{:S(2)}, u32[]{:S(2)}) collective-permute-start(bf16[192,128]{1,0:T(8,128)(2,1)} %get-tuple-element.130), channel_id=1, source_target_pairs={{0,3},{1,0},{2,1},{3,2},{4,7},{5,4},{6,5},{7,6},{8,11},{9,8},{10,9... | collective-permute-start | bytes 147464 | tf_op jit(solution)/shard_map/ppermute | solution.py:36
  125.7 3.8 %collective-permute-start.22 = (bf16[128,768]{1,0:T(8,128)(2,1)S(1)}, bf16[128,768]{1,0:T(8,128)(2,1)S(1)}, u32[]{:S(2)}, u32[]{:S(2)}) collective-permute-start(bf16[128,768]{1,0:T(8,128)(2,1)S(1)} %copy-done.43), channel_id=1, source_target_pairs={{0,3},{1,0},{2,1},{3,2},{4,7},{5,4},{6,5},{7,6},{8,11},{9,8},{10,9... | collective-permute-start | bytes 589832 | tf_op jit(solution)/shard_map/ppermute | solution.py:36
  129.5 6.2 %shard_map.302 = (bf16[4,96,2304]{2,1,0:T(8,128)(2,1)}, f32[2,96,2304]{2,1,0:T(8,128)}, f32[2,96,2304]{2,1,0:T(8,128)}) custom-call(s32[1]{0:T(128)} %bitcast.2.refs_0_.index, bf16[512,768]{1,0:T(8,128)(2,1)} %get-tuple-element.122.refs_1_, bf16[512,768]{1,0:T(8,128)(2,1)} %get-tuple-element.123.refs_2_.hidden_back, bf16[128,768]{1,0:T(8,128)(2,1)} %c0.3, ...), custom_call_target="tpu_custom_call" | custom-call | flops 60000002048 | tf_op jit(solution)/shard_map/pallas_call | solution.py:367
  136.8 2.4 %shard_map.304 = (bf16[512,384]{1,0:T(8,128)(2,1)}, f32[192,512]{1,0:T(8,128)}) custom-call(s32[2]{0:T(128)} %pad_add_fusion.place, bf16[512,192]{1,0:T(8,128)(2,1)} %get-tuple-element.97.query, bf16[192,128]{1,0:T(8,128)(2,1)} %get-tuple-element.120.g0, bf16[192,128]{1,0:T(8,128)(2,1)} %copy-done.51, bf16[192,128]{1,0:T(8,128)(2,1)} %copy-done.52, ...), custom_call_target="tpu_custom_call" | custom-call | flops 60000002048 | tf_op jit(solution)/shard_map/pallas_call | solution.py:367
  141.9 2.9 %shard_map.305 = (bf16[512,384]{1,0:T(8,128)(2,1)}, f32[192,512]{1,0:T(8,128)}) custom-call(s32[2]{0:T(128)} %pad_add_fusion.place, bf16[512,192]{1,0:T(8,128)(2,1)} %get-tuple-element.97.query, bf16[192,128]{1,0:T(8,128)(2,1)} %get-tuple-element.120.g0, bf16[192,128]{1,0:T(8,128)(2,1)} %copy-done.51, bf16[192,128]{1,0:T(8,128)(2,1)} %copy-done.52, ...), custom_call_target="tpu_custom_call" | custom-call | flops 60000002048 | tf_op jit(solution)/shard_map/pallas_call | solution.py:367
  144.8 9.2 %collective-permute-start.29 = (bf16[512,384]{1,0:T(8,128)(2,1)}, bf16[512,384]{1,0:T(8,128)(2,1)S(1)}, u32[]{:S(2)}, u32[]{:S(2)}) collective-permute-start(bf16[512,384]{1,0:T(8,128)(2,1)} %get-tuple-element.146), channel_id=1, source_target_pairs={{0,8},{4,12},{8,0},{12,4},{1,9},{5,13},{9,1},{13,5},{2,10},{6,14},... | collective-permute-start | bytes 1179656 | tf_op jit(solution)/shard_map/ppermute | solution.py:45
  155.2 4.8 %shard_map.306 = (bf16[512,384]{1,0:T(8,128)(2,1)}, bf16[512,384]{1,0:T(8,128)(2,1)}, bf16[512,192]{1,0:T(8,128)(2,1)}) custom-call(s32[2]{0:T(128)} %pad_add_fusion.place, bf16[512,192]{1,0:T(8,128)(2,1)} %get-tuple-element.97.query, bf16[192,128]{1,0:T(8,128)(2,1)} %get-tuple-element.120.g0, bf16[192,128]{1,0:T(8,128)(2,1)} %copy-done.51, ...), custom_call_target="tpu_custom_call" | custom-call | flops 60000002048 | tf_op jit(solution)/shard_map/pallas_call | solution.py:367
  160.0 2.2 %collective-permute-start.28 = (bf16[512,384]{1,0:T(8,128)(2,1)}, bf16[512,384]{1,0:T(8,128)(2,1)S(1)}, u32[]{:S(2)}, u32[]{:S(2)}) collective-permute-start(bf16[512,384]{1,0:T(8,128)(2,1)} %get-tuple-element.145), channel_id=1, source_target_pairs={{0,4},{4,0},{8,12},{12,8},{1,5},{5,1},{9,13},{13,9},{2,6},{6,2},{1... | collective-permute-start | bytes 1179656 | tf_op jit(solution)/shard_map/ppermute | solution.py:45
  164.6 4.7 %shard_map.307 = (f32[128,768]{1,0:T(8,128)}, bf16[128,768]{1,0:T(8,128)(2,1)}, bf16[256,768]{1,0:T(8,128)(2,1)}, bf16[128,768]{1,0:T(8,128)(2,1)}, bf16[4,112,6...) custom-call(s32[1]{0:T(128)} %bitcast.2.refs_0_.index, ...), custom_call_target="tpu_custom_call" | custom-call | flops 60000002048 | tf_op jit(solution)/shard_map/pallas_call | solution.py:367
  172.3 1.8 add_convert_fusion.2
  177.3 1.5 collective-permute-start.36
  178.8 1.9 collective-permute-start.30
  180.7 2.3 %collective-permute-done.31 = bf16[2,96,2304]{2,1,0:T(8,128)(2,1)} collective-permute-done((bf16[2,96,2304]{2,1,0:T(8,128)(2,1)}, bf16[2,96,2304]{2,1,0:T(8,128)(2,1)}, u32[]{:S(2)}, u32[]{:S(2)}) %collective-permute-start.31) | collective-permute-done | bytes 884768 | tf_op jit(solution)/shard_map/ppermute | solution.py:51
  183.0 3.1 %collective-permute-done.34 = bf16[2,112,640]{2,1,0:T(8,128)(2,1)} collective-permute-done((bf16[2,112,640]{2,1,0:T(8,128)(2,1)}, bf16[2,112,640]{2,1,0:T(8,128)(2,1)}, u32[]{:S(2)}, u32[]{:S(2)}) %collective-permute-start.34) | collective-permute-done | bytes 286752 | tf_op jit(solution)/shard_map/ppermute | solution.py:51
  187.2 1.5 collective-permute-start.35
  188.8 1.9 fusion
  195.8 3.5 %collective-permute-done.33 = bf16[96,2304]{1,0:T(8,128)(2,1)} collective-permute-done((bf16[96,2304]{1,0:T(8,128)(2,1)}, bf16[96,2304]{1,0:T(8,128)(2,1)}, u32[]{:S(2)}, u32[]{:S(2)}) %collective-permute-start.33) | collective-permute-done | bytes 442400 | tf_op jit(solution)/shard_map/ppermute | solution.py:51
  202.1 2.0 collective-permute-start.39
  204.1 1.9 collective-permute-start.38
  206.1 3.1 %shard_map.308 = (bf16[128,768]{1,0:T(8,128)(2,1)}, bf16[128,768]{1,0:T(8,128)(2,1)}) custom-call(s32[2]{0:T(128)} %pad_add_fusion.place, f32[128,768]{1,0:T(8,128)} %get-tuple-element.153.normed_own, bf16[128,768]{1,0:T(8,128)(2,1)} %collective-permute-done.30.n1, bf16[256,768]{1,0:T(8,128)(2,1)} %collective-permute-done.36.n2, ...), custom_call_target="tpu_custom_call" | custom-call | flops 60000002048 | tf_op jit(solution)/shard_map/pallas_call | solution.py:367
  209.4 2.5 %collective-permute-done.40 = bf16[112,192]{1,0:T(8,128)(2,1)S(1)} collective-permute-done((bf16[112,192]{1,0:T(8,128)(2,1)S(1)}, bf16[112,192]{1,0:T(8,128)(2,1)S(1)}, u32[]{:S(2)}, u32[]{:S(2)}) %collective-permute-start.40) | collective-permute-done | bytes 43040 | tf_op jit(solution)/shard_map/ppermute | solution.py:36
  (227 shorter events, 43.6 us)
Async XLA Ops:
  0.7 30.9 %copy-start.19 = (bf16[768,96]{0,1:T(8,128)(2,1)S(1)}, bf16[768,96]{0,1:T(8,128)(2,1)}, u32[]{:S(2)}) copy-start(bf16[768,96]{0,1:T(8,128)(2,1)} %param.23) | copy-start | bytes 442372
  0.7 30.9 %copy-start.7 = (bf16[96,768]{1,0:T(8,128)(2,1)S(1)}, bf16[96,768]{1,0:T(8,128)(2,1)}, u32[]{:S(2)}) copy-start(bf16[96,768]{1,0:T(8,128)(2,1)} %param.22) | copy-start | bytes 442372
  2.7 11.1 %collective-permute-start = (bf16[160,768]{1,0:T(8,128)(2,1)S(1)}, bf16[160,768]{1,0:T(8,128)(2,1)S(1)}, u32[]{:S(2)}, u32[]{:S(2)}) collective-permute-start(bf16[160,768]{1,0:T(8,128)(2,1)S(1)} %pad_maximum_fusion.4), channel_id=1, source_target_pairs={{0,1},{1,2},{2,3},{3,0},{4,5},{5,6},{6,7},{7,4},{8,9},{9,10},{10,1... | collective-permute-start | bytes 737288 | tf_op jit(solution)/shard_map/ppermute | solution.py:36
  13.7 18.0 %copy-start.20 = (bf16[160,768]{1,0:T(8,128)(2,1)}, bf16[160,768]{1,0:T(8,128)(2,1)S(1)}, u32[]{:S(2)}) copy-start(bf16[160,768]{1,0:T(8,128)(2,1)S(1)} %collective-permute-done.t1) | copy-start | bytes 737284
  13.7 8.7 %collective-permute-start.2 = (bf16[160,768]{1,0:T(8,128)(2,1)S(1)}, bf16[160,768]{1,0:T(8,128)(2,1)S(1)}, u32[]{:S(2)}, u32[]{:S(2)}) collective-permute-start(bf16[160,768]{1,0:T(8,128)(2,1)S(1)} %pad_maximum_fusion.4), channel_id=1, source_target_pairs={{0,3},{1,0},{2,1},{3,2},{4,7},{5,4},{6,5},{7,6},{8,11},{9,8},{10,9... | collective-permute-start | bytes 737288 | tf_op jit(solution)/shard_map/ppermute | solution.py:36
  17.2 5.2 %collective-permute-start.1 = (bf16[112,576]{1,0:T(8,128)(2,1)S(1)}, bf16[112,576]{1,0:T(8,128)(2,1)S(1)}, u32[]{:S(2)}, u32[]{:S(2)}) collective-permute-start(bf16[112,576]{1,0:T(8,128)(2,1)S(1)} %fusion.6.own), channel_id=1, source_target_pairs={{0,16},{4,12},{8,24},{12,4},{16,0},{20,28},{24,8},{28,20},{1,17},{... | collective-permute-start | bytes 387080 | tf_op jit(solution)/shard_map/ppermute | solution.py:51
  18.8 12.4 %collective-permute-start.4 = (bf16[160,768]{1,0:T(8,128)(2,1)S(1)}, bf16[160,768]{1,0:T(8,128)(2,1)S(1)}, u32[]{:S(2)}, u32[]{:S(2)}) collective-permute-start(bf16[160,768]{1,0:T(8,128)(2,1)S(1)} %pad_maximum_fusion.4), channel_id=1, source_target_pairs={{0,2},{1,3},{2,0},{3,1},{4,6},{5,7},{6,4},{7,5},{8,10},{9,11},{10,... | collective-permute-start | bytes 737288 | tf_op jit(solution)/shard_map/ppermute | solution.py:36
  22.4 8.7 %collective-permute-start.3 = (bf16[2,112,576]{2,1,0:T(8,128)(2,1)S(1)}, bf16[2,112,576]{2,1,0:T(8,128)(2,1)S(1)}, u32[]{:S(2)}, u32[]{:S(2)}) collective-permute-start(bf16[2,112,576]{2,1,0:T(8,128)(2,1)S(1)} %pad_maximum_fusion.3), channel_id=1, source_target_pairs={{0,8},{4,20},{8,0},{12,28},{16,24},{20,4},{24,16},{28,12},{1,9},{5... | collective-permute-start | bytes 774152 | tf_op jit(solution)/shard_map/ppermute | solution.py:51
  31.3 2.0 collective-permute-start.5
  31.7 31.5 %copy-start = (bf16[96,2304]{1,0:T(8,128)(2,1)}, bf16[96,2304]{1,0:T(8,128)(2,1)S(1)}, u32[]{:S(2)}) copy-start(bf16[96,2304]{1,0:T(8,128)(2,1)S(1)} %concatenate.60.refs_1_) | copy-start | bytes 1327108
  31.7 11.1 %collective-permute-start.12 = (bf16[96,2304]{1,0:T(8,128)(2,1)S(1)}, bf16[96,2304]{1,0:T(8,128)(2,1)S(1)}, u32[]{:S(2)}, u32[]{:S(2)}) collective-permute-start(bf16[96,2304]{1,0:T(8,128)(2,1)S(1)} %concatenate.60.refs_1_), channel_id=1, source_target_pairs={{0,16},{4,12},{8,24},{12,4},{16,0},{20,28},{24,8},{28,20},{1,17},{... | collective-permute-start | bytes 1327112 | tf_op jit(solution)/shard_map/ppermute | solution.py:51
  37.9 6.5 %collective-permute-start.7 = (bf16[512,384]{1,0:T(8,128)(2,1)}, bf16[512,384]{1,0:T(8,128)(2,1)S(1)}, u32[]{:S(2)}, u32[]{:S(2)}) collective-permute-start(bf16[512,384]{1,0:T(8,128)(2,1)} %get-tuple-element.98.kv_own), channel_id=1, source_target_pairs={{0,4},{4,0},{8,12},{12,8},{1,5},{5,1},{9,13},{13,9},{2,6},{6,2},{1... | collective-permute-start | bytes 1179656 | tf_op jit(solution)/shard_map/ppermute | solution.py:45
  38.7 10.2 %collective-permute-start.10 = (bf16[128,768]{1,0:T(8,128)(2,1)S(1)}, bf16[128,768]{1,0:T(8,128)(2,1)S(1)}, u32[]{:S(2)}, u32[]{:S(2)}) collective-permute-start(bf16[128,768]{1,0:T(8,128)(2,1)S(1)} %copy-done.37), channel_id=1, source_target_pairs={{0,3},{1,0},{2,1},{3,2},{4,7},{5,4},{6,5},{7,6},{8,11},{9,8},{10,9... | collective-permute-start | bytes 589832 | tf_op jit(solution)/shard_map/ppermute | solution.py:36
  42.3 10.0 %collective-permute-start.8 = (bf16[128,768]{1,0:T(8,128)(2,1)S(1)}, bf16[128,768]{1,0:T(8,128)(2,1)S(1)}, u32[]{:S(2)}, u32[]{:S(2)}) collective-permute-start(bf16[128,768]{1,0:T(8,128)(2,1)S(1)} %copy-done.37), channel_id=1, source_target_pairs={{0,1},{1,2},{2,3},{3,0},{4,5},{5,6},{6,7},{7,4},{8,9},{9,10},{10,1... | collective-permute-start | bytes 589832 | tf_op jit(solution)/shard_map/ppermute | solution.py:36
  42.3 16.4 %collective-permute-start.9 = (bf16[128,768]{1,0:T(8,128)(2,1)S(1)}, bf16[128,768]{1,0:T(8,128)(2,1)S(1)}, u32[]{:S(2)}, u32[]{:S(2)}) collective-permute-start(bf16[128,768]{1,0:T(8,128)(2,1)S(1)} %copy-done.37), channel_id=1, source_target_pairs={{0,2},{1,3},{2,0},{3,1},{4,6},{5,7},{6,4},{7,5},{8,10},{9,11},{10,... | collective-permute-start | bytes 589832 | tf_op jit(solution)/shard_map/ppermute | solution.py:36
  42.8 20.4 %copy-start.2 = (bf16[96,2304]{1,0:T(8,128)(2,1)}, bf16[96,2304]{1,0:T(8,128)(2,1)S(1)}, u32[]{:S(2)}) copy-start(bf16[96,2304]{1,0:T(8,128)(2,1)S(1)} %collective-permute-done.12.refs_2_) | copy-start | bytes 1327108
  42.9 15.7 %collective-permute-start.6 = (bf16[512,384]{1,0:T(8,128)(2,1)S(1)}, bf16[512,384]{1,0:T(8,128)(2,1)S(1)}, u32[]{:S(2)}, u32[]{:S(2)}) collective-permute-start(bf16[512,384]{1,0:T(8,128)(2,1)S(1)} %copy-done.30), channel_id=1, source_target_pairs={{0,8},{4,12},{8,0},{12,4},{1,9},{5,13},{9,1},{13,5},{2,10},{6,14},... | collective-permute-start | bytes 1179656 | tf_op jit(solution)/shard_map/ppermute | solution.py:45
  44.5 18.8 %collective-permute-start.13 = (bf16[2,96,2304]{2,1,0:T(8,128)(2,1)S(1)}, bf16[2,96,2304]{2,1,0:T(8,128)(2,1)S(1)}, u32[]{:S(2)}, u32[]{:S(2)}) collective-permute-start(bf16[2,96,2304]{2,1,0:T(8,128)(2,1)S(1)} %pad_maximum_fusion.1), channel_id=1, source_target_pairs={{0,8},{4,20},{8,0},{12,28},{16,24},{20,4},{24,16},{28,12},{1,9},{5... | collective-permute-start | bytes 2654216 | tf_op jit(solution)/shard_map/ppermute | solution.py:51
  58.6 2.9 %collective-permute-start.11 = (bf16[512,384]{1,0:T(8,128)(2,1)S(1)}, bf16[512,384]{1,0:T(8,128)(2,1)S(1)}, u32[]{:S(2)}, u32[]{:S(2)}) collective-permute-start(bf16[512,384]{1,0:T(8,128)(2,1)S(1)} %collective-permute-done.6.kv_y), channel_id=1, source_target_pairs={{0,4},{4,0},{8,12},{12,8},{1,5},{5,1},{9,13},{13,9},{2,6},{6,2},{1... | collective-permute-start | bytes 1179656 | tf_op jit(solution)/shard_map/ppermute | solution.py:45
  64.3 8.1 %collective-permute-start.17 = (bf16[4,96,2304]{2,1,0:T(8,128)(2,1)S(1)}, bf16[4,96,2304]{2,1,0:T(8,128)(2,1)S(1)}, u32[]{:S(2)}, u32[]{:S(2)}) collective-permute-start(bf16[4,96,2304]{2,1,0:T(8,128)(2,1)S(1)} %pad_maximum_fusion), channel_id=1, source_target_pairs={{0,4},{4,0},{8,12},{12,8},{16,20},{20,16},{24,28},{28,24},{1,5},{5... | collective-permute-start | bytes 5308424 | tf_op jit(solution)/shard_map/ppermute | solution.py:51
  66.5 11.2 %collective-permute-start.14 = (bf16[192,512]{1,0:T(8,128)(2,1)}, bf16[192,512]{1,0:T(8,128)(2,1)S(1)}, u32[]{:S(2)}, u32[]{:S(2)}) collective-permute-start(bf16[192,512]{1,0:T(8,128)(2,1)} %get-tuple-element.108.m0), channel_id=1, source_target_pairs={{0,1},{1,2},{2,3},{3,0},{4,5},{5,6},{6,7},{7,4},{8,9},{9,10},{10,1... | collective-permute-start | bytes 589832 | tf_op jit(solution)/shard_map/ppermute | solution.py:36
  70.0 14.3 %collective-permute-start.15 = (bf16[192,512]{1,0:T(8,128)(2,1)}, bf16[192,512]{1,0:T(8,128)(2,1)S(1)}, u32[]{:S(2)}, u32[]{:S(2)}) collective-permute-start(bf16[192,512]{1,0:T(8,128)(2,1)} %get-tuple-element.108.m0), channel_id=1, source_target_pairs={{0,2},{1,3},{2,0},{3,1},{4,6},{5,7},{6,4},{7,5},{8,10},{9,11},{10,... | collective-permute-start | bytes 589832 | tf_op jit(solution)/shard_map/ppermute | solution.py:36
  70.3 14.0 %collective-permute-start.16 = (bf16[192,512]{1,0:T(8,128)(2,1)}, bf16[192,512]{1,0:T(8,128)(2,1)S(1)}, u32[]{:S(2)}, u32[]{:S(2)}) collective-permute-start(bf16[192,512]{1,0:T(8,128)(2,1)} %get-tuple-element.108.m0), channel_id=1, source_target_pairs={{0,3},{1,0},{2,1},{3,2},{4,7},{5,4},{6,5},{7,6},{8,11},{9,8},{10,9... | collective-permute-start | bytes 589832 | tf_op jit(solution)/shard_map/ppermute | solution.py:36
  92.6 12.1 %collective-permute-start.18 = (bf16[128,768]{1,0:T(8,128)(2,1)}, bf16[128,768]{1,0:T(8,128)(2,1)S(1)}, u32[]{:S(2)}, u32[]{:S(2)}) collective-permute-start(bf16[128,768]{1,0:T(8,128)(2,1)} %get-tuple-element.116), channel_id=1, source_target_pairs={{0,3},{1,0},{2,1},{3,2},{4,7},{5,4},{6,5},{7,6},{8,11},{9,8},{10,9... | collective-permute-start | bytes 589832 | tf_op jit(solution)/shard_map/ppermute | solution.py:36
  99.1 17.3 %collective-permute-start.19 = (bf16[128,768]{1,0:T(8,128)(2,1)}, bf16[128,768]{1,0:T(8,128)(2,1)S(1)}, u32[]{:S(2)}, u32[]{:S(2)}) collective-permute-start(bf16[128,768]{1,0:T(8,128)(2,1)} %get-tuple-element.117), channel_id=1, source_target_pairs={{0,2},{1,3},{2,0},{3,1},{4,6},{5,7},{6,4},{7,5},{8,10},{9,11},{10,... | collective-permute-start | bytes 589832 | tf_op jit(solution)/shard_map/ppermute | solution.py:36
  99.1 17.3 %collective-permute-start.20 = (bf16[128,768]{1,0:T(8,128)(2,1)}, bf16[128,768]{1,0:T(8,128)(2,1)S(1)}, u32[]{:S(2)}, u32[]{:S(2)}) collective-permute-start(bf16[128,768]{1,0:T(8,128)(2,1)} %get-tuple-element.118), channel_id=1, source_target_pairs={{0,1},{1,2},{2,3},{3,0},{4,5},{5,6},{6,7},{7,4},{8,9},{9,10},{10,1... | collective-permute-start | bytes 589832 | tf_op jit(solution)/shard_map/ppermute | solution.py:36
  120.4 15.2 %collective-permute-start.21 = (bf16[192,128]{1,0:T(8,128)(2,1)}, bf16[192,128]{1,0:T(8,128)(2,1)S(1)}, u32[]{:S(2)}, u32[]{:S(2)}) collective-permute-start(bf16[192,128]{1,0:T(8,128)(2,1)} %get-tuple-element.121), channel_id=1, source_target_pairs={{0,1},{1,2},{2,3},{3,0},{4,5},{5,6},{6,7},{7,4},{8,9},{9,10},{10,1... | collective-permute-start | bytes 147464 | tf_op jit(solution)/shard_map/ppermute | solution.py:36
  120.9 15.2 %collective-permute-start.24 = (bf16[192,128]{1,0:T(8,128)(2,1)}, bf16[192,128]{1,0:T(8,128)(2,1)S(1)}, u32[]{:S(2)}, u32[]{:S(2)}) collective-permute-start(bf16[192,128]{1,0:T(8,128)(2,1)} %get-tuple-element.131), channel_id=1, source_target_pairs={{0,2},{1,3},{2,0},{3,1},{4,6},{5,7},{6,4},{7,5},{8,10},{9,11},{10,... | collective-permute-start | bytes 147464 | tf_op jit(solution)/shard_map/ppermute | solution.py:36
  122.8 13.3 %collective-permute-start.25 = (bf16[192,128]{1,0:T(8,128)(2,1)}, bf16[192,128]{1,0:T(8,128)(2,1)S(1)}, u32[]{:S(2)}, u32[]{:S(2)}) collective-permute-start(bf16[192,128]{1,0:T(8,128)(2,1)} %get-tuple-element.130), channel_id=1, source_target_pairs={{0,3},{1,0},{2,1},{3,2},{4,7},{5,4},{6,5},{7,6},{8,11},{9,8},{10,9... | collective-permute-start | bytes 147464 | tf_op jit(solution)/shard_map/ppermute | solution.py:36
  125.7 10.0 %collective-permute-start.23 = (bf16[128,768]{1,0:T(8,128)(2,1)S(1)}, bf16[128,768]{1,0:T(8,128)(2,1)S(1)}, u32[]{:S(2)}, u32[]{:S(2)}) collective-permute-start(bf16[128,768]{1,0:T(8,128)(2,1)S(1)} %copy-done.44), channel_id=1, source_target_pairs={{0,1},{1,2},{2,3},{3,0},{4,5},{5,6},{6,7},{7,4},{8,9},{9,10},{10,1... | collective-permute-start | bytes 589832 | tf_op jit(solution)/shard_map/ppermute | solution.py:36
  125.7 10.4 %collective-permute-start.22 = (bf16[128,768]{1,0:T(8,128)(2,1)S(1)}, bf16[128,768]{1,0:T(8,128)(2,1)S(1)}, u32[]{:S(2)}, u32[]{:S(2)}) collective-permute-start(bf16[128,768]{1,0:T(8,128)(2,1)S(1)} %copy-done.43), channel_id=1, source_target_pairs={{0,3},{1,0},{2,1},{3,2},{4,7},{5,4},{6,5},{7,6},{8,11},{9,8},{10,9... | collective-permute-start | bytes 589832 | tf_op jit(solution)/shard_map/ppermute | solution.py:36
  139.2 2.0 collective-permute-start.27
  139.3 14.8 %collective-permute-start.26 = (bf16[4,96,2304]{2,1,0:T(8,128)(2,1)S(1)}, bf16[4,96,2304]{2,1,0:T(8,128)(2,1)S(1)}, u32[]{:S(2)}, u32[]{:S(2)}) collective-permute-start(bf16[4,96,2304]{2,1,0:T(8,128)(2,1)S(1)} %copy-done.27), channel_id=1, source_target_pairs={{0,4},{4,0},{8,12},{12,8},{16,20},{20,16},{24,28},{28,24},{1,5},{5... | collective-permute-start | bytes 5308424 | tf_op jit(solution)/shard_map/ppermute | solution.py:51
  144.8 18.8 %collective-permute-start.29 = (bf16[512,384]{1,0:T(8,128)(2,1)}, bf16[512,384]{1,0:T(8,128)(2,1)S(1)}, u32[]{:S(2)}, u32[]{:S(2)}) collective-permute-start(bf16[512,384]{1,0:T(8,128)(2,1)} %get-tuple-element.146), channel_id=1, source_target_pairs={{0,8},{4,12},{8,0},{12,4},{1,9},{5,13},{9,1},{13,5},{2,10},{6,14},... | collective-permute-start | bytes 1179656 | tf_op jit(solution)/shard_map/ppermute | solution.py:45
  154.0 34.7 %copy-start.3 = (bf16[4,96,2304]{2,1,0:T(8,128)(2,1)}, bf16[4,96,2304]{2,1,0:T(8,128)(2,1)S(1)}, u32[]{:S(2)}) copy-start(bf16[4,96,2304]{2,1,0:T(8,128)(2,1)S(1)} %collective-permute-done.26) | copy-start | bytes 5308420
  160.0 3.7 %collective-permute-start.28 = (bf16[512,384]{1,0:T(8,128)(2,1)}, bf16[512,384]{1,0:T(8,128)(2,1)S(1)}, u32[]{:S(2)}, u32[]{:S(2)}) collective-permute-start(bf16[512,384]{1,0:T(8,128)(2,1)} %get-tuple-element.145), channel_id=1, source_target_pairs={{0,4},{4,0},{8,12},{12,8},{1,5},{5,1},{9,13},{13,9},{2,6},{6,2},{1... | collective-permute-start | bytes 1179656 | tf_op jit(solution)/shard_map/ppermute | solution.py:45
  169.3 19.5 %copy-start.1 = (f32[2,96,2304]{2,1,0:T(8,128)S(1)}, f32[2,96,2304]{2,1,0:T(8,128)}, u32[]{:S(2)}) copy-start(f32[2,96,2304]{2,1,0:T(8,128)} %get-tuple-element.155) | copy-start | bytes 5308420
  169.3 2.2 %collective-permute-start.32 = (bf16[4,112,640]{2,1,0:T(8,128)(2,1)}, bf16[4,112,640]{2,1,0:T(8,128)(2,1)S(1)}, u32[]{:S(2)}, u32[]{:S(2)}) collective-permute-start(bf16[4,112,640]{2,1,0:T(8,128)(2,1)} %get-tuple-element.157), channel_id=1, source_target_pairs={{0,4},{4,0},{8,12},{12,8},{16,20},{20,16},{24,28},{28,24},{1,5},{5... | collective-permute-start | bytes 1720328 | tf_op jit(solution)/shard_map/ppermute | solution.py:51
  169.6 13.4 %collective-permute-start.31 = (bf16[2,96,2304]{2,1,0:T(8,128)(2,1)}, bf16[2,96,2304]{2,1,0:T(8,128)(2,1)}, u32[]{:S(2)}, u32[]{:S(2)}) collective-permute-start(bf16[2,96,2304]{2,1,0:T(8,128)(2,1)} %add_convert_fusion), channel_id=1, source_target_pairs={{0,16},{4,12},{8,24},{12,4},{16,0},{20,28},{24,8},{28,20},{1,17},{... | collective-permute-start | bytes 2654216 | tf_op jit(solution)/shard_map/ppermute | solution.py:51
  174.1 11.9 %collective-permute-start.34 = (bf16[2,112,640]{2,1,0:T(8,128)(2,1)}, bf16[2,112,640]{2,1,0:T(8,128)(2,1)}, u32[]{:S(2)}, u32[]{:S(2)}) collective-permute-start(bf16[2,112,640]{2,1,0:T(8,128)(2,1)} %add_convert_fusion.2), channel_id=1, source_target_pairs={{0,16},{4,12},{8,24},{12,4},{16,0},{20,28},{24,8},{28,20},{1,17},{... | collective-permute-start | bytes 860168 | tf_op jit(solution)/shard_map/ppermute | solution.py:51
  175.8 30.1 %collective-permute-start.37 = (bf16[128,768]{1,0:T(8,128)(2,1)}, bf16[128,768]{1,0:T(8,128)(2,1)}, u32[]{:S(2)}, u32[]{:S(2)}) collective-permute-start(bf16[128,768]{1,0:T(8,128)(2,1)} %get-tuple-element.163), channel_id=1, source_target_pairs={{0,1},{1,2},{2,3},{3,0},{4,5},{5,6},{6,7},{7,4},{8,9},{9,10},{10,1... | collective-permute-start | bytes 589832 | tf_op jit(solution)/shard_map/ppermute | solution.py:36
  177.3 28.8 %collective-permute-start.36 = (bf16[256,768]{1,0:T(8,128)(2,1)}, bf16[256,768]{1,0:T(8,128)(2,1)}, u32[]{:S(2)}, u32[]{:S(2)}) collective-permute-start(bf16[256,768]{1,0:T(8,128)(2,1)} %get-tuple-element.161), channel_id=1, source_target_pairs={{0,2},{1,3},{2,0},{3,1},{4,6},{5,7},{6,4},{7,5},{8,10},{9,11},{10,... | collective-permute-start | bytes 1179656 | tf_op jit(solution)/shard_map/ppermute | solution.py:36
  178.8 27.3 %collective-permute-start.30 = (bf16[128,768]{1,0:T(8,128)(2,1)}, bf16[128,768]{1,0:T(8,128)(2,1)}, u32[]{:S(2)}, u32[]{:S(2)}) collective-permute-start(bf16[128,768]{1,0:T(8,128)(2,1)} %get-tuple-element.154), channel_id=1, source_target_pairs={{0,3},{1,0},{2,1},{3,2},{4,7},{5,4},{6,5},{7,6},{8,11},{9,8},{10,9... | collective-permute-start | bytes 589832 | tf_op jit(solution)/shard_map/ppermute | solution.py:36
  187.2 5.2 %collective-permute-start.35 = (bf16[112,640]{1,0:T(8,128)(2,1)S(1)}, bf16[112,640]{1,0:T(8,128)(2,1)S(1)}, u32[]{:S(2)}, u32[]{:S(2)}) collective-permute-start(bf16[112,640]{1,0:T(8,128)(2,1)S(1)} %fusion.7), channel_id=1, source_target_pairs={{0,8},{4,20},{8,0},{12,28},{16,24},{20,4},{24,16},{28,12},{1,9},{5... | collective-permute-start | bytes 430088 | tf_op jit(solution)/shard_map/ppermute | solution.py:51
  190.7 8.6 %collective-permute-start.33 = (bf16[96,2304]{1,0:T(8,128)(2,1)}, bf16[96,2304]{1,0:T(8,128)(2,1)}, u32[]{:S(2)}, u32[]{:S(2)}) collective-permute-start(bf16[96,2304]{1,0:T(8,128)(2,1)} %fusion), channel_id=1, source_target_pairs={{0,8},{4,20},{8,0},{12,28},{16,24},{20,4},{24,16},{28,12},{1,9},{5... | collective-permute-start | bytes 1327112 | tf_op jit(solution)/shard_map/ppermute | solution.py:51
  202.1 7.2 %collective-permute-start.39 = (bf16[112,192]{1,0:T(8,128)(2,1)S(1)}, bf16[112,192]{1,0:T(8,128)(2,1)S(1)}, u32[]{:S(2)}, u32[]{:S(2)}) collective-permute-start(bf16[112,192]{1,0:T(8,128)(2,1)S(1)} %get-tuple-element.225), channel_id=1, source_target_pairs={{0,2},{1,3},{2,0},{3,1},{4,6},{5,7},{6,4},{7,5},{8,10},{9,11},{10,... | collective-permute-start | bytes 129032 | tf_op jit(solution)/shard_map/ppermute | solution.py:36
  204.1 5.3 %collective-permute-start.38 = (bf16[112,192]{1,0:T(8,128)(2,1)S(1)}, bf16[112,192]{1,0:T(8,128)(2,1)S(1)}, u32[]{:S(2)}, u32[]{:S(2)}) collective-permute-start(bf16[112,192]{1,0:T(8,128)(2,1)S(1)} %get-tuple-element.226), channel_id=1, source_target_pairs={{0,3},{1,0},{2,1},{3,2},{4,7},{5,4},{6,5},{7,6},{8,11},{9,8},{10,9... | collective-permute-start | bytes 129032 | tf_op jit(solution)/shard_map/ppermute | solution.py:36
  205.9 6.0 %collective-permute-start.40 = (bf16[112,192]{1,0:T(8,128)(2,1)S(1)}, bf16[112,192]{1,0:T(8,128)(2,1)S(1)}, u32[]{:S(2)}, u32[]{:S(2)}) collective-permute-start(bf16[112,192]{1,0:T(8,128)(2,1)S(1)} %get-tuple-element.224), channel_id=1, source_target_pairs={{0,1},{1,2},{2,3},{3,0},{4,5},{5,6},{6,7},{7,4},{8,9},{9,10},{10,1... | collective-permute-start | bytes 129032 | tf_op jit(solution)/shard_map/ppermute | solution.py:36
  (47 other events, 270.0 us)
